TPU v7x, 256 devices: a whole 4x4x8 slice. The times are simulated.
256 devices in a mesh: pipe: 8 (over z_lo, x), tensor: 8 (over z_hi, core), dp: 4 (over y).
Axes of the slice: x: 4, y: 4, z: 8 (z_hi: 4, z_lo: 2; z = z_hi * 2 + z_lo), core: 2. Of those that a mesh axis runs over, the one named last changes fastest.
Arguments:
- act: bfloat16 [8, 4, 512, 4096], P('pipe', 'dp', 'tensor'), may hold values from -6 to 6
- direction: int32 [8, 4], P(None, 'dp'), may hold values from 0 to 1
- positions: int32 [8, 4, 512], P('pipe', 'dp'), may hold values from 0 to 511, as said below
- w_query: bfloat16 [8, 4096, 32, 128], P('pipe', 'dp', 'tensor'), may hold values from -0.09375 to 0.09375
- w_keyval: bfloat16 [8, 4096, 8, 2, 128], P('pipe', 'dp', 'tensor'), may hold values from -0.09375 to 0.09375
- out_grad: bfloat16 [8, 4, 512, 32, 128], P('pipe', 'dp', None, 'tensor'), may hold values from -6 to 6
Outputs:
- attn_out: bfloat16 [8, 4, 512, 32, 128], P('pipe', 'dp', None, 'tensor')
- grad_input: bfloat16 [8, 4, 512, 4096], P('pipe', 'dp', 'tensor')
- grad_query: float32 [8, 4096, 32, 128], P('pipe', 'dp', 'tensor')
- grad_keyval: float32 [8, 4096, 8, 2, 128], P('pipe', 'dp', 'tensor')
Inputs may be any that keep to these rules, and one draw needn't show every extreme that they name: Each micro-batch's positions are a permutation of 0 to 511.
All inputs are finite; a program needn't handle non-finite values.
Results may differ from a plain program's by a relative error of at most 0.035.
Values may be sent and summed in bfloat16 or wider, within the bound.
No kernel may reach another device: no remote copies, remote signals or barrier semaphores. Data moves between devices by JAX's collectives and lax.ppermute only.
A program may use at most 128 MiB of HBM per device.

v0:
```python
import functools
import math

import jax
import jax.numpy as jnp
from jax import lax
from jax.experimental import pallas as pl
from jax.experimental.pallas import tpu as pltpu
from jax.sharding import PartitionSpec as P

BF = jnp.bfloat16
F32 = jnp.float32
GROUP = 128
LIGHT = pl.CostEstimate(flops=1, bytes_accessed=1, transcendentals=0)
VM = pl.BlockSpec(memory_space=pltpu.VMEM)


def sin_turns(r):
    a = jnp.abs(r)
    m = jnp.minimum(a, 0.5 - a)
    x = (2.0 * math.pi) * m
    y = x * x
    p = -1.0 / 39916800.0
    p = p * y + 1.0 / 362880.0
    p = p * y - 1.0 / 5040.0
    p = p * y + 1.0 / 120.0
    p = p * y - 1.0 / 6.0
    s = x + x * (y * p)
    return jnp.where(r < 0, -s, s)


def quantize_block(w):
    top = jnp.max(jnp.abs(w), axis=0, keepdims=True)
    scale = (top + 1e-06) / 7.0
    t = w * (1.0 / scale)
    wave = sin_turns(t - jnp.round(t))
    return scale * (t - wave * (1.0 / (2.0 * math.pi)))


def quantize_kernel(wq_ref, wkv_ref, out_ref):
    columns = wq_ref.shape[1]
    out_ref[:, :columns] = quantize_block(wq_ref[...].astype(F32)).astype(BF)
    out_ref[:, columns:] = quantize_block(wkv_ref[...].astype(F32)).astype(BF)


def quantize(w_query, w_keyval):
    rows, q_cols = w_query.shape
    kv_cols = w_keyval.shape[1]
    cols = q_cols + kv_cols
    return pl.pallas_call(
        quantize_kernel,
        grid=(rows // GROUP,),
        in_specs=[
            pl.BlockSpec((GROUP, q_cols), lambda i: (i, 0)),
            pl.BlockSpec((GROUP, kv_cols), lambda i: (i, 0)),
        ],
        out_specs=pl.BlockSpec((GROUP, cols), lambda i: (i, 0)),
        out_shape=jax.ShapeDtypeStruct((rows, cols), BF),
        compiler_params=pltpu.CompilerParams(vmem_limit_bytes=16 * 2**20),
        cost_estimate=LIGHT,
    )(w_query, w_keyval)


def dot(a, b, dims):
    return lax.dot_general(a, b, (dims, ((), ())), preferred_element_type=F32)


def whole(shape):
    return pl.BlockSpec(shape, lambda *_: (0,) * len(shape))


def tie_kernel(*refs):
    pass


def tie(*values):
    place = [pl.BlockSpec(memory_space=pl.ANY)] * len(values)
    return pl.pallas_call(
        tie_kernel,
        in_specs=place,
        out_specs=place,
        out_shape=[jax.ShapeDtypeStruct(v.shape, v.dtype) for v in values],
        input_output_aliases={i: i for i in range(len(values))},
        cost_estimate=LIGHT,
    )(*values)


def join_kernel(*refs):
    out_ref, row = refs[-1], 0
    for ref in refs[:-1]:
        out_ref[row : row + ref.shape[0], :] = ref[...]
        row += ref.shape[0]


def join(*parts):
    rows = sum(p.shape[0] for p in parts)
    return pl.pallas_call(
        join_kernel,
        in_specs=[VM] * len(parts),
        out_specs=VM,
        out_shape=jax.ShapeDtypeStruct((rows, parts[0].shape[1]), BF),
        compiler_params=pltpu.CompilerParams(vmem_limit_bytes=16 * 2**20),
        cost_estimate=LIGHT,
    )(*parts)


def halves_kernel(w0_ref, w1_ref, x0_ref, x1_ref, pos_ref, chip_ref, w0_out, w1_out, x0_out, x1_out, pos_out, chip_out):
    w0_out[...] = w0_ref[...]
    w1_out[...] = w1_ref[...]
    x0_out[...] = x0_ref[...]
    x1_out[...] = x1_ref[...]
    pos_out[...] = pos_ref[...]
    chip_out[...] = chip_ref[...]


def first_half(value):
    return pl.BlockSpec((value.shape[0] // 2, value.shape[1]), lambda i: (0, 0))


def second_half(value):
    return pl.BlockSpec((value.shape[0] // 2, value.shape[1]), lambda i: (1, 0))


def half_of(value):
    return jax.ShapeDtypeStruct((value.shape[0] // 2, value.shape[1]), value.dtype)


def halves(w0, w1, x0, x1, pos, chip):
    outs = [half_of(w0), half_of(w1), half_of(x0), half_of(x1)]
    outs += [jax.ShapeDtypeStruct(v.shape, v.dtype) for v in (pos, chip)]
    return pl.pallas_call(
        halves_kernel,
        grid=(1,),
        in_specs=[first_half(w0), second_half(w1), first_half(x0), second_half(x1)]
        + [whole(pos.shape), whole(chip.shape)],
        out_specs=[whole(o.shape) for o in outs],
        out_shape=outs,
        compiler_params=pltpu.CompilerParams(vmem_limit_bytes=16 * 2**20),
        cost_estimate=LIGHT,
    )(w0, w1, x0, x1, pos, chip)


def second_step_kernel(d0_ref, d1_ref, up_ref, down_ref, next_ref, prev_ref, d0_out, d1_out, up_out, down_out):
    d0_out[...] = d0_ref[...]
    d1_out[...] = d1_ref[...]
    up_out[...] = (up_ref[...].astype(F32) + next_ref[...].astype(F32)).astype(BF)
    down_out[...] = (down_ref[...].astype(F32) + prev_ref[...].astype(F32)).astype(BF)


def second_step(d0, d1, up, down, next_top, prev_bot):
    outs = [half_of(d0), half_of(d1), half_of(up), half_of(down)]
    return pl.pallas_call(
        second_step_kernel,
        grid=(1,),
        in_specs=[first_half(d0), second_half(d1), first_half(up), first_half(down)]
        + [whole(next_top.shape), whole(prev_bot.shape)],
        out_specs=[whole(o.shape) for o in outs],
        out_shape=outs,
        compiler_params=pltpu.CompilerParams(vmem_limit_bytes=16 * 2**20),
        cost_estimate=LIGHT,
    )(d0, d1, up, down, next_top, prev_bot)


def input_grad_kernel(shift_ref, kept_ref, up_ref, down_ref, up2_ref, down2_ref, out_ref):
    half = up2_ref.shape[0]
    total = kept_ref[...].astype(F32)
    bottom = total[half:] + up_ref[...].astype(F32) + down2_ref[...].astype(F32)
    top = total[:half] + up2_ref[...].astype(F32) + down_ref[...].astype(F32)
    out_ref[:half, :] = top.astype(BF)
    out_ref[half:, :] = bottom.astype(BF)


def input_grad(replica, replicas, kept, up, down, up2, down2):
    rows, model = kept.shape
    tile = model // replicas
    part = lambda r, k: pl.BlockSpec((r, tile), lambda j, s: (k, j))
    return pl.pallas_call(
        input_grad_kernel,
        grid_spec=pltpu.PrefetchScalarGridSpec(
            num_scalar_prefetch=1,
            grid=(replicas,),
            in_specs=[
                part(rows, 0),
                part(rows // 2, 1),
                part(rows // 2, 1),
                part(rows // 2, 0),
                part(rows // 2, 0),
            ],
            out_specs=pl.BlockSpec((rows, tile), lambda j, s: (0, (j + s[0]) % replicas)),
        ),
        out_shape=jax.ShapeDtypeStruct((rows, model), BF),
        compiler_params=pltpu.CompilerParams(vmem_limit_bytes=16 * 2**20),
        cost_estimate=pl.CostEstimate(
            flops=40 * 10**9, bytes_accessed=160 * 2**20, transcendentals=0
        ),
    )(replica.reshape(1), kept, up, down, up2, down2)


def project_kernel(parts, *refs):
    tokens, weights = refs[:parts], refs[parts:-3]
    out_ref, first_ref, held = refs[-3:]

    @pl.when(pl.program_id(0) == 0)
    def _():
        row = 0
        for ref in tokens:
            held[row : row + ref.shape[0], :] = ref[...]
            row += ref.shape[0]
        first_ref[...] = held[:, : first_ref.shape[1]]

    total, at = None, 0
    for ref in weights:
        term = dot(held[:, at : at + ref.shape[0]], ref[...], ((1,), (0,)))
        total = term if total is None else total + term
        at += ref.shape[0]
    out_ref[...] = total.astype(BF)


def project(tokens, weights, first):
    rows = sum(t.shape[0] for t in tokens)
    model = tokens[0].shape[1]
    cols = weights[0].shape[1]
    tile = 256
    return pl.pallas_call(
        functools.partial(project_kernel, len(tokens)),
        grid=(cols // tile,),
        in_specs=[whole(t.shape) for t in tokens]
        + [pl.BlockSpec((w.shape[0], tile), lambda i: (0, i)) for w in weights],
        out_specs=[pl.BlockSpec((rows, tile), lambda i: (0, i)), whole((rows, first))],
        out_shape=[
            jax.ShapeDtypeStruct((rows, cols), BF),
            jax.ShapeDtypeStruct((rows, first), BF),
        ],
        scratch_shapes=[pltpu.VMEM((rows, model), BF)],
        compiler_params=pltpu.CompilerParams(vmem_limit_bytes=32 * 2**20),
        cost_estimate=LIGHT,
    )(*tokens, *weights)


def pack_kernel(parts, *refs):
    outs = refs[parts + 1 :]
    row = 0
    for ref in refs[:parts]:
        rows, cols = ref.shape[0], outs[0].shape[1]
        for i, out in enumerate(outs):
            out[row : row + rows, :] = ref[:, (i + 1) * cols : (i + 2) * cols]
        row += rows


def pack(tokens, cols, after):
    rows = sum(t.shape[0] for t in tokens)
    count = tokens[0].shape[1] // cols - 1
    return pl.pallas_call(
        functools.partial(pack_kernel, len(tokens)),
        in_specs=[pl.BlockSpec(memory_space=pltpu.VMEM)] * len(tokens)
        + [pl.BlockSpec(memory_space=pl.ANY)],
        out_shape=[jax.ShapeDtypeStruct((rows, cols), BF)] * count,
        compiler_params=pltpu.CompilerParams(vmem_limit_bytes=16 * 2**20),
        cost_estimate=LIGHT,
    )(*tokens, after)


def attention_kernel(
    q_ref, kv_ref, cos_ref, sin_ref, pos_row_ref, pos_col_ref, og_ref,
    out_ref, d_ref, k_rot, dk_sum, dv_sum,
):
    width = cos_ref.shape[1]
    half = width // 2
    head = pl.program_id(0)
    heads = pl.num_programs(0)
    cosine = cos_ref[...]
    signed = sin_ref[...]

    @pl.when(head == 0)
    def _():
        k = kv_ref[:, :width].astype(F32)
        k_rot[...] = (k * cosine + pltpu.roll(k, half, 1) * signed).astype(BF)
        dk_sum[...] = jnp.zeros_like(dk_sum)
        dv_sum[...] = jnp.zeros_like(dv_sum)

    values = kv_ref[:, width:]
    keys = k_rot[...]
    q = q_ref[...].astype(F32)
    q_rot = (q * cosine + pltpu.roll(q, half, 1) * signed).astype(BF)
    factor = 1.0 / math.sqrt(width)
    scores = dot(q_rot, keys, ((1,), (1,))) * factor
    visible = pos_row_ref[...] <= pos_col_ref[...]
    scores = jnp.where(visible, scores, -1e30)
    raised = jnp.exp(scores - jnp.max(scores, axis=1, keepdims=True))
    weights = raised / jnp.sum(raised, axis=1, keepdims=True)
    weights_low = weights.astype(BF)
    out_ref[...] = dot(weights_low, values, ((1,), (0,))).astype(BF)
    cotangent = og_ref[...]
    dv_sum[...] += dot(weights_low, cotangent, ((0,), (0,)))
    d_weights = dot(cotangent, values, ((1,), (1,)))
    delta = jnp.sum(d_weights * weights, axis=1, keepdims=True)
    d_scores = (weights * (d_weights - delta) * factor).astype(BF)
    dq = dot(d_scores, keys, ((1,), (0,)))
    dk_sum[...] += dot(d_scores, q_rot, ((0,), (0,)))
    place = pl.ds(pl.multiple_of(head * width, width), width)
    d_ref[:, place] = (dq * cosine + pltpu.roll(dq * signed, half, 1)).astype(BF)

    @pl.when(head == heads - 1)
    def _():
        dk = dk_sum[...]
        q_cols = d_ref.shape[1] - 2 * width
        dk = (dk * cosine + pltpu.roll(dk * signed, half, 1)).astype(BF)
        d_ref[:, q_cols : q_cols + width] = dk
        d_ref[:, q_cols + width :] = dv_sum[...].astype(BF)


def attention(projected, heads, width, cos_t, sin_t, positions, out_grad):
    length, cols = projected.shape
    q_cols = heads * width
    column = pl.BlockSpec((length, width), lambda h: (0, h))
    return pl.pallas_call(
        attention_kernel,
        grid=(heads,),
        in_specs=[
            column,
            pl.BlockSpec((length, 2 * width), lambda h: (0, heads // 2)),
            whole((length, width)),
            whole((length, width)),
            whole((1, length)),
            whole((length, 1)),
            column,
        ],
        out_specs=[column, whole((length, cols))],
        out_shape=[
            jax.ShapeDtypeStruct((length, q_cols), BF),
            jax.ShapeDtypeStruct((length, cols), BF),
        ],
        scratch_shapes=[
            pltpu.VMEM((length, width), BF),
            pltpu.VMEM((length, width), F32),
            pltpu.VMEM((length, width), F32),
        ],
        compiler_params=pltpu.CompilerParams(vmem_limit_bytes=24 * 2**20),
        cost_estimate=LIGHT,
    )(projected, projected, cos_t, sin_t, positions[None, :], positions[:, None], out_grad)


def partial_kernel(parts, rows, cuts, *refs):
    grads = refs[0][rows[0] : rows[1], :]
    weights, rest = refs[1 : 1 + parts], refs[1 + parts :]
    other = None
    if rows[0] == 0:
        other, rest = rest[0], rest[1:]
    at = 0
    for ref in weights:
        columns = slice(at, at + ref.shape[0])
        total = dot(grads, ref[...], ((1,), (1,)))
        if other is not None:
            total += other[:, columns].astype(F32)
        total = total.astype(BF)
        for out, ranges in zip(rest, cuts):
            row = 0
            for low, high in ranges:
                out[row : row + high - low, columns] = total[low:high]
                row += high - low
        at += ref.shape[0]


def partial(grads, weights, other, cuts):
    near, cols = grads.shape[0] // 2, grads.shape[1]
    model = sum(w.shape[0] for w in weights)
    rows = (near, 2 * near) if other is None else (0, near)
    sizes = [sum(high - low for low, high in ranges) for ranges in cuts]
    return pl.pallas_call(
        functools.partial(partial_kernel, len(weights), rows, cuts),
        out_shape=[jax.ShapeDtypeStruct((p, model), BF) for p in sizes],
        compiler_params=pltpu.CompilerParams(vmem_limit_bytes=24 * 2**20),
        cost_estimate=LIGHT,
    )(grads, *weights, *(() if other is None else (other,)))


def weight_grad_kernel(count, first, *refs):
    tokens, grads, rest = refs[:count], refs[count : 2 * count], refs[2 * count :]
    total = None if first else rest[0][...]
    for x, d in zip(tokens, grads):
        term = dot(x[...], d[...], ((0,), (0,)))
        total = term if total is None else total + term
    if first:
        rest[0][...] = total
    else:
        q_ref, kv_ref = rest[1:]
        q_cols = q_ref.shape[1]
        q_ref[...] = total[:, :q_cols].astype(BF)
        kv_ref[...] = total[:, q_cols:].astype(BF)


def weight_grad(tokens, grads, sums, q_cols):
    count = len(tokens)
    d_rows = tokens[0].shape[1]
    cols = grads[0][0].shape[1]
    tile = 256
    block = lambda width: pl.BlockSpec((tile, width), lambda i: (i, 0))
    in_specs = [pl.BlockSpec((t.shape[0], tile), lambda i: (0, i)) for t in tokens]
    for grad, part in grads:
        if part is None:
            in_specs.append(whole(grad.shape))
        else:
            shape = (grad.shape[0] // 2, cols)
            in_specs.append(pl.BlockSpec(shape, functools.partial(lambda p, i: (p, 0), part)))
    if sums is None:
        operands = ()
        out_specs = block(cols)
        out_shape = jax.ShapeDtypeStruct((d_rows, cols), F32)
    else:
        operands = (sums,)
        in_specs.append(block(cols))
        out_specs = [block(q_cols), block(cols - q_cols)]
        out_shape = [
            jax.ShapeDtypeStruct((d_rows, q_cols), BF),
            jax.ShapeDtypeStruct((d_rows, cols - q_cols), BF),
        ]
    return pl.pallas_call(
        functools.partial(weight_grad_kernel, count, sums is None),
        grid=(d_rows // tile,),
        in_specs=in_specs,
        out_specs=out_specs,
        out_shape=out_shape,
        compiler_params=pltpu.CompilerParams(vmem_limit_bytes=24 * 2**20),
        cost_estimate=LIGHT,
    )(*tokens, *[g for g, _ in grads], *operands)


def mirror_sum_kernel(q_ref, q_far_ref, kv_ref, kv_far_ref, out_q_ref, out_kv_ref):
    width = out_q_ref.shape[-1]
    q = q_ref[...].astype(F32) + q_far_ref[...].astype(F32)
    kv = kv_ref[...].astype(F32) + kv_far_ref[...].astype(F32)
    for i in range(out_q_ref.shape[1]):
        out_q_ref[:, i, :] = q[:, i * width : (i + 1) * width]
    for i in range(out_kv_ref.shape[1]):
        out_kv_ref[:, i, :] = kv[:, i * width : (i + 1) * width]


def mirror_sum(q, q_far, kv, kv_far, width):
    rows, q_cols = q.shape
    kv_cols = kv.shape[1]
    tile = 256
    flat = lambda cols: pl.BlockSpec((tile, cols), lambda i: (i, 0))
    deep = lambda cols: pl.BlockSpec((tile, cols // width, width), lambda i: (i, 0, 0))
    return pl.pallas_call(
        mirror_sum_kernel,
        grid=(rows // tile,),
        in_specs=[flat(q_cols), flat(q_cols), flat(kv_cols), flat(kv_cols)],
        out_specs=[deep(q_cols), deep(kv_cols)],
        out_shape=[
            jax.ShapeDtypeStruct((rows, q_cols // width, width), F32),
            jax.ShapeDtypeStruct((rows, kv_cols // width, width), F32),
        ],
        compiler_params=pltpu.CompilerParams(vmem_limit_bytes=16 * 2**20),
        cost_estimate=LIGHT,
    )(q, q_far, kv, kv_far)


def shifted(value, axis, step):
    count = lax.axis_size(axis)
    return lax.ppermute(value, axis, [(i, (i + step) % count) for i in range(count)])


def shifted_chips(value, step):
    count = lax.axis_size("tensor")
    chips = count // 2
    pairs = [(i, ((i // 2 + step) % chips) * 2 + i % 2) for i in range(count)]
    return lax.ppermute(value, "tensor", pairs)


def other_core(value):
    return lax.ppermute(value, "tensor", [(i, i ^ 1) for i in range(lax.axis_size("tensor"))])


def roll_blocks(value, axis, shift, count):
    block = value.shape[axis] // count
    doubled = jnp.concatenate([value, value], axis=axis)
    return lax.dynamic_slice_in_dim(doubled, shift * block, value.shape[axis], axis=axis)


def on_device(act, direction, positions, w_query, w_keyval, out_grad):
    section = lax.axis_index("pipe")
    sections = lax.axis_size("pipe")
    tensor = lax.axis_index("tensor")
    chip, core = tensor // 2, tensor % 2
    chips = lax.axis_size("tensor") // 2
    replica = lax.axis_index("dp")
    replicas = lax.axis_size("dp")
    d_rows, heads, width = w_query.shape[1:]
    seq_len = positions.shape[2]
    q_cols = heads * width
    piece = act.shape[2]
    near = seq_len // 2
    half = piece // 2

    fresh = act[0, 0]
    ends = sections - 1
    from_below = lax.ppermute(fresh, "pipe", [(i, i + 1) for i in range(ends)])
    from_above = lax.ppermute(fresh, "pipe", [(i + 1, i) for i in range(ends)])

    w_own = quantize(w_query[0].reshape(d_rows, -1), w_keyval[0].reshape(d_rows, -1))
    w_before = shifted(w_own, "dp", 1)
    w_after = shifted(w_own, "dp", -1)

    heading = lax.dynamic_index_in_dim(direction, section, 0, keepdims=False)[0]
    down_src = jnp.where(section == 0, fresh, from_below)
    up_src = jnp.where(section == ends, fresh, from_above)
    own = roll_blocks(jnp.where(heading == 0, down_src, up_src), 1, replica, replicas)
    prev = shifted_chips(own, 1)
    after = shifted_chips(own, -1)

    before_top, after_bot, prev_top, next_bot, late_pos, late_chip = halves(
        w_before, w_after, prev, after, positions[0], chip.reshape(1, 1)
    )
    late_chip = late_chip[0, 0]
    far_top = shifted(before_top, "dp", 1)
    far_bot = shifted(after_bot, "dp", -1)
    across_top = shifted_chips(prev_top, 1)
    across_bot = shifted_chips(next_bot, -1)

    close = join(own, after, prev)
    across = join(across_top, across_bot)
    token_parts = [close, across]
    other_parts = [other_core(part) for part in token_parts]

    def to_relative(value):
        rest = value.shape[1:]
        value = value.reshape((chips, 2, piece) + rest)
        value = roll_blocks(value, 0, late_chip, chips)
        value = jnp.concatenate([value[:2], value[3:], value[2:3]])
        pair = jnp.where(
            core == 0, jnp.stack([value[:, 0], value[:, 1]]), jnp.stack([value[:, 1], value[:, 0]])
        )
        return pair.reshape((seq_len,) + rest)

    def to_absolute(value):
        rest = value.shape[1:]
        value = value.reshape((2, chips, piece) + rest)
        pair = jnp.where(
            core == 0, jnp.stack([value[0], value[1]], 1), jnp.stack([value[1], value[0]], 1)
        )
        pair = jnp.concatenate([pair[:2], pair[3:], pair[2:3]])
        return roll_blocks(pair, 0, (chips - chip) % chips, chips).reshape((seq_len,) + rest)

    pos = to_relative(late_pos[0][:, None])[:, 0]
    cotangent = to_relative(out_grad[0, 0].reshape(seq_len, -1))
    angle_half = width // 2
    inv_freq = 1000000.0 ** (-jnp.arange(angle_half, dtype=F32) / angle_half)
    angles = pos.astype(F32)[:, None] * inv_freq[None, :]
    cosine, sine = jnp.cos(angles), jnp.sin(angles)
    cos_t = jnp.concatenate([cosine, cosine], axis=1)
    sin_t = jnp.concatenate([-sine, sine], axis=1)

    blocks = pack(token_parts, d_rows, far_top)
    sent = [shifted(blocks[k - 1], "dp", k) for k in range(1, replicas)]

    weights = [w_own, w_after, far_top, far_bot, w_before]
    projected, x_own = project(token_parts + other_parts, weights, d_rows)
    attended, d_own = attention(projected, heads, width, cos_t, sin_t, pos, cotangent)
    sent[0], sent[2], d_own = tie(sent[0], sent[2], d_own)
    attn_out = to_absolute(attended).reshape(1, 1, seq_len, heads, width)

    other_part = other_core(partial(d_own, weights, None, [[(0, near)]])[0])
    low = [i * piece for i in range(chips)]
    mid = [i * piece + half for i in range(chips)]
    high = [(i + 1) * piece for i in range(chips)]
    kept, up, next_top, down, prev_bot = partial(
        d_own,
        weights,
        other_part,
        [
            [(low[0], high[0])],
            [(low[3], mid[3]), (mid[1], high[1])],
            [(low[1], mid[1])],
            [(mid[3], high[3]), (low[2], mid[2])],
            [(mid[2], high[2])],
        ],
    )
    up = shifted_chips(up, 1)
    down = shifted_chips(down, -1)

    d_before = shifted(d_own, "dp", 1)
    d_after = shifted(d_own, "dp", -1)
    before_top, after_bot, up2, down2 = second_step(
        d_before, d_after, up, down, next_top, prev_bot
    )
    d_far_top = shifted(before_top, "dp", 1)
    d_far_bot = shifted(after_bot, "dp", -1)
    up2 = shifted_chips(up2, 1)
    down2 = shifted_chips(down2, -1)
    grad_input = input_grad(replica, replicas, kept, up, down, up2, down2)

    near_other = other_core(join(sent[0], sent[2]))
    sums = weight_grad(
        [x_own, sent[0], near_other[:near], sent[2], near_other[near:]],
        [(d_own, None), (d_before, 0), (d_before, 1), (d_after, 0), (d_after, 1)],
        None,
        q_cols,
    )
    own_q, own_kv = weight_grad(
        [sent[1], other_core(sent[1])], [(d_far_top, None), (d_far_bot, None)], sums, q_cols
    )
    pairs = [(i, ends - i) for i in range(sections)]
    far_q = lax.ppermute(own_q, "pipe", pairs)
    far_kv = lax.ppermute(own_kv, "pipe", pairs)
    grad_query, grad_keyval = mirror_sum(own_q, far_q, own_kv, far_kv, width)
    return attn_out, grad_input[None, None], grad_query[None], grad_keyval[None, :, None]


def solution(mesh):
    return jax.shard_map(
        on_device,
        mesh=mesh,
        in_specs=(
            P("pipe", "dp", "tensor", None),
            P(None, "dp"),
            P("pipe", "dp", None),
            P("pipe", "dp", "tensor", None),
            P("pipe", "dp", "tensor", None, None),
            P("pipe", "dp", None, "tensor", None),
        ),
        out_specs=(
            P("pipe", "dp", None, "tensor", None),
            P("pipe", "dp", "tensor", None),
            P("pipe", "dp", "tensor", None),
            P("pipe", "dp", "tensor", None, None),
        ),
        check_vma=False,
    )
```

profile of v0, /device:TPU:24, one launch (start us, length us, event | category | flops | bytes accessed | tf_op | source)
XLA Modules:
  0.0 220.0 jit_solution(4283765811346350713)
XLA Ops:
  2.1 5.4 %collective-permute-start = (bf16[64,4096]{1,0:T(8,128)(2,1)}, bf16[64,4096]{1,0:T(8,128)(2,1)}, u32[]{:S(2)}, u32[]{:S(2)}) collective-permute-start(bf16[64,4096]{1,0:T(8,128)(2,1)} %bitcast.54), channel_id=1, source_target_pairs={{0,32},{32,64},{64,96},{96,128},{128,160},{160,192},{192,224},{1,3... | collective-permute-start | bytes 1572872 | tf_op jit(solution)/shard_map/ppermute | solution.py:497
  9.0 3.5 %shard_map.94.refs_4_.refs_1_ = bf16[1024,768]{1,0:T(8,128)(2,1)S(1)} custom-call(bf16[1024,512]{1,0:T(8,128)(2,1)S(1)} %bitcast.45, bf16[1024,256]{1,0:T(8,128)(2,1)S(1)} %bitcast.47), custom_call_target="tpu_custom_call" | custom-call | flops 1 | bytes 1 | tf_op jit(solution)/shard_map/pallas_call | solution.py:50
  20.8 6.3 %collective-permute-start.2 = (bf16[64,4096]{1,0:T(8,128)(2,1)}, bf16[64,4096]{1,0:T(8,128)(2,1)}, u32[]{:S(2)}, u32[]{:S(2)}) collective-permute-start(bf16[64,4096]{1,0:T(8,128)(2,1)} %fusion.1.refs_0_), channel_id=1, source_target_pairs={{0,24},{4,28},{8,0},{12,4},{16,8},{20,12},{24,16},{28,20},{1,25},{... | collective-permute-start | bytes 1572872 | tf_op jit(solution)/shard_map/ppermute | solution.py:467
  29.2 19.5 %collective-permute-done.2.refs_1_.x1_ref = bf16[64,4096]{1,0:T(8,128)(2,1)} collective-permute-done((bf16[64,4096]{1,0:T(8,128)(2,1)}, bf16[64,4096]{1,0:T(8,128)(2,1)}, u32[]{:S(2)}, u32[]{:S(2)}) %collective-permute-start.2) | collective-permute-done | bytes 524320 | tf_op jit(solution)/shard_map/ppermute | solution.py:467
  48.7 4.3 %collective-permute-done.3.refs_2_.x0_ref = bf16[64,4096]{1,0:T(8,128)(2,1)} collective-permute-done((bf16[64,4096]{1,0:T(8,128)(2,1)}, bf16[64,4096]{1,0:T(8,128)(2,1)}, u32[]{:S(2)}, u32[]{:S(2)}) %collective-permute-start.3) | collective-permute-done | bytes 524320 | tf_op jit(solution)/shard_map/ppermute | solution.py:467
  53.0 2.6 %shard_map.93.refs_0_ = bf16[192,4096]{1,0:T(8,128)(2,1)} custom-call(bf16[64,4096]{1,0:T(8,128)(2,1)} %fusion.1.refs_0_, bf16[64,4096]{1,0:T(8,128)(2,1)} %collective-permute-done.2.refs_1_.x1_ref, bf16[64,4096]{1,0:T(8,128)(2,1)} %collective-permute-done.3.refs_2_.x0_ref), custom_call_target="tpu_custom_call" | custom-call | flops 1 | bytes 1 | tf_op jit(solution)/shard_map/pallas_call | solution.py:97
  62.2 4.1 %collective-permute-start.7 = (bf16[32,4096]{1,0:T(8,128)(2,1)}, bf16[32,4096]{1,0:T(8,128)(2,1)}, u32[]{:S(2)}, u32[]{:S(2)}) collective-permute-start(bf16[32,4096]{1,0:T(8,128)(2,1)} %copy-done.23), channel_id=1, source_target_pairs={{0,24},{4,28},{8,0},{12,4},{16,8},{20,12},{24,16},{28,20},{1,25},{... | collective-permute-start | bytes 786440 | tf_op jit(solution)/shard_map/ppermute | solution.py:467
  72.5 6.2 %collective-permute-done.6.refs_0_ = bf16[32,4096]{1,0:T(8,128)(2,1)S(1)} collective-permute-done((bf16[32,4096]{1,0:T(8,128)(2,1)}, bf16[32,4096]{1,0:T(8,128)(2,1)S(1)}, u32[]{:S(2)}, u32[]{:S(2)}) %collective-permute-start.6) | collective-permute-done | bytes 262176 | tf_op jit(solution)/shard_map/ppermute | solution.py:467
  80.6 5.5 %collective-permute-done.10.refs_6_.refs_2_.refs_3_ = bf16[512,768]{1,0:T(8,128)(2,1)} collective-permute-done((bf16[512,768]{1,0:T(8,128)(2,1)}, bf16[512,768]{1,0:T(8,128)(2,1)}, u32[]{:S(2)}, u32[]{:S(2)}) %collective-permute-start.10) | collective-permute-done | bytes 786464 | tf_op jit(solution)/shard_map/ppermute | solution.py:460
  94.3 6.8 %shard_map.97 = (bf16[512,768]{1,0:T(8,128)(2,1)S(1)}, bf16[512,1024]{1,0:T(8,128)(2,1)S(1)}) custom-call(bf16[192,4096]{1,0:T(8,128)(2,1)} %shard_map.93.refs_0_, bf16[64,4096]{1,0:T(8,128)(2,1)} %shard_map.96.refs_1_, bf16[192,4096]{1,0:T(8,128)(2,1)} %collective-permute-done.8.refs_2_, bf16[64,4096]{1,0:T(8,128)(2,1)} %collective-permute-done.9.refs_3_, ...), custom_call_target="tpu_custom_call" | custom-call | flops 1 | bytes 1 | tf_op jit(solution)/shard_map/pallas_call | solution.py:224
  101.2 7.6 %shard_map.98 = (bf16[512,512]{1,0:T(8,128)(2,1)S(1)}, bf16[512,768]{1,0:T(8,128)(2,1)S(1)}) custom-call(bf16[512,768]{1,0:T(8,128)(2,1)S(1)} %get-tuple-element.37.q_ref.kv_ref, bf16[512,768]{1,0:T(8,128)(2,1)S(1)} %get-tuple-element.37.q_ref.kv_ref, f32[512,128]{1,0:T(8,128)S(1)} %get-tuple-element.87.cos_ref, f32[512,128]{1,0:T(8,128)S(1)} %get-tuple-element.88.sin_ref, ...), custom_call_target="tpu_custom_call" | custom-call | flops 1 | bytes 1 | tf_op jit(solution)/shard_map/pallas_call | solution.py:316
  111.7 5.0 %shard_map.101 = bf16[256,4096]{1,0:T(8,128)(2,1)} custom-call(bf16[512,768]{1,0:T(8,128)(2,1)S(1)} %copy-done.1, bf16[1024,768]{1,0:T(8,128)(2,1)S(1)} %shard_map.94.refs_4_.refs_1_, bf16[1024,768]{1,0:T(8,128)(2,1)} %collective-permute-done.5.w1_ref.refs_5_.refs_2_, bf16[512,768]{1,0:T(8,128)(2,1)} %collective-permute-done.10.refs_6_.refs_2_.refs_3_, ...), custom_call_target="tpu_custom_call" | custom-call | flops 1 | bytes 1 | tf_op jit(solution)/shard_map/pallas_call | solution.py:369
  123.9 4.4 %shard_map.102 = (bf16[64,4096]{1,0:T(8,128)(2,1)S(1)}, bf16[64,4096]{1,0:T(8,128)(2,1)S(1)}, bf16[32,4096]{1,0:T(8,128)(2,1)S(1)}, bf16[64,4096]{1,0:T(8,128)(2,1)S(1)}, bf16[32,4096]{1,0:T(8,128)(2,1)S(1)}) custom-call(bf16[512,768]{1,0:T(8,128)(2,1)S(1)} %copy-done.2, bf16[1024,768]{1,0:T(8,128)(2,1)S(1)} %shard_map.94.refs_4_.refs_1_, ...), custom_call_target="tpu_custom_call" | custom-call | flops 1 | bytes 1 | tf_op jit(solution)/shard_map/pallas_call | solution.py:369
  128.4 4.9 %collective-permute-done.21.refs_0_ = bf16[256,1024]{1,0:T(8,128)(2,1)} collective-permute-done((bf16[256,1024]{1,0:T(8,128)(2,1)}, bf16[256,1024]{1,0:T(8,128)(2,1)}, u32[]{:S(2)}, u32[]{:S(2)}) %collective-permute-start.21) | collective-permute-done | bytes 524320 | tf_op jit(solution)/shard_map/ppermute | solution.py:460
  133.6 16.1 %collective-permute-done.17.d0_ref.refs_6_.refs_7_ = bf16[512,768]{1,0:T(8,128)(2,1)S(1)} collective-permute-done((bf16[512,768]{1,0:T(8,128)(2,1)S(1)}, bf16[512,768]{1,0:T(8,128)(2,1)S(1)}, u32[]{:S(2)}, u32[]{:S(2)}) %collective-permute-start.17) | collective-permute-done | bytes 786464 | tf_op jit(solution)/shard_map/ppermute | solution.py:460
  149.7 6.2 %collective-permute-done.15.up_ref = bf16[64,4096]{1,0:T(8,128)(2,1)S(1)} collective-permute-done((bf16[64,4096]{1,0:T(8,128)(2,1)S(1)}, bf16[64,4096]{1,0:T(8,128)(2,1)S(1)}, u32[]{:S(2)}, u32[]{:S(2)}) %collective-permute-start.15) | collective-permute-done | bytes 524320 | tf_op jit(solution)/shard_map/ppermute | solution.py:467
  155.9 2.8 %collective-permute-done.16.down_ref = bf16[64,4096]{1,0:T(8,128)(2,1)S(1)} collective-permute-done((bf16[64,4096]{1,0:T(8,128)(2,1)S(1)}, bf16[64,4096]{1,0:T(8,128)(2,1)S(1)}, u32[]{:S(2)}, u32[]{:S(2)}) %collective-permute-start.16) | collective-permute-done | bytes 524320 | tf_op jit(solution)/shard_map/ppermute | solution.py:467
  159.9 2.8 %collective-permute-start.23 = (bf16[256,768]{1,0:T(8,128)(2,1)}, bf16[256,768]{1,0:T(8,128)(2,1)}, u32[]{:S(2)}, u32[]{:S(2)}) collective-permute-start(bf16[256,768]{1,0:T(8,128)(2,1)} %get-tuple-element.53), channel_id=1, source_target_pairs={{0,1},{1,2},{2,3},{3,0},{4,5},{5,6},{6,7},{7,4},{8,9},{9,10},{10,1... | collective-permute-start | bytes 1179656 | tf_op jit(solution)/shard_map/ppermute | solution.py:460
  166.0 3.9 %collective-permute-start.20 = (bf16[32,4096]{1,0:T(8,128)(2,1)}, bf16[32,4096]{1,0:T(8,128)(2,1)S(1)}, u32[]{:S(2)}, u32[]{:S(2)}) collective-permute-start(bf16[32,4096]{1,0:T(8,128)(2,1)} %copy-done.21), channel_id=1, source_target_pairs={{0,24},{4,28},{8,0},{12,4},{16,8},{20,12},{24,16},{28,20},{1,25},{... | collective-permute-start | bytes 786440 | tf_op jit(solution)/shard_map/ppermute | solution.py:467
  171.1 4.6 %shard_map.106.refs_4_ = f32[1024,768]{1,0:T(8,128)S(1)} custom-call(bf16[512,1024]{1,0:T(8,128)(2,1)S(1)} %copy-done.9, bf16[256,1024]{1,0:T(8,128)(2,1)} %get-tuple-element.56.refs_0_.refs_1_, bf16[256,1024]{1,0:T(8,128)(2,1)S(1)} %get-tuple-element.73.refs_2_, bf16[256,1024]{1,0:T(8,128)(2,1)} %get-tuple-element.57.refs_1_.refs_3_, ...), custom_call_target="tpu_custom_call" | custom-call | flops 1 | bytes 1 | tf_op jit(solution)/shard_map/pallas_call | solution.py:417
  175.8 3.6 %shard_map.107 = (bf16[1024,512]{1,0:T(8,128)(2,1)S(1)}, bf16[1024,256]{1,0:T(8,128)(2,1)S(1)}) custom-call(bf16[256,1024]{1,0:T(8,128)(2,1)} %collective-permute-done.21.refs_0_, bf16[256,1024]{1,0:T(8,128)(2,1)} %collective-permute-done.22.refs_1_, bf16[256,768]{1,0:T(8,128)(2,1)} %collective-permute-done.23.refs_2_, ...), custom_call_target="tpu_custom_call" | custom-call | flops 1 | bytes 1 | tf_op jit(solution)/shard_map/pallas_call | solution.py:417
  179.4 4.3 %collective-permute-start.26 = (bf16[1024,512]{1,0:T(8,128)(2,1)S(1)}, bf16[1024,512]{1,0:T(8,128)(2,1)S(1)}, u32[]{:S(2)}, u32[]{:S(2)}) collective-permute-start(bf16[1024,512]{1,0:T(8,128)(2,1)S(1)} %get-tuple-element.58.q_ref), channel_id=1, source_target_pairs={{0,224},{32,192},{64,160},{96,128},{128,96},{160,64},{192,32},{224... | collective-permute-start | bytes 3145736 | tf_op jit(solution)/shard_map/ppermute | solution.py:603
  185.5 31.5 %collective-permute-done.27.kv_far_ref = bf16[1024,256]{1,0:T(8,128)(2,1)S(1)} collective-permute-done((bf16[1024,256]{1,0:T(8,128)(2,1)S(1)}, bf16[1024,256]{1,0:T(8,128)(2,1)S(1)}, u32[]{:S(2)}, u32[]{:S(2)}) %collective-permute-start.27) | collective-permute-done | bytes 524320 | tf_op jit(solution)/shard_map/ppermute | solution.py:604
  217.0 3.0 %shard_map.108 = (f32[1024,4,128]{2,1,0:T(4,128)}, f32[1024,2,128]{2,1,0:T(2,128)}) custom-call(bf16[1024,512]{1,0:T(8,128)(2,1)S(1)} %get-tuple-element.58.q_ref, bf16[1024,512]{1,0:T(8,128)(2,1)S(1)} %collective-permute-done.26.q_far_ref, bf16[1024,256]{1,0:T(8,128)(2,1)S(1)} %get-tuple-element.59.kv_ref, ...), custom_call_target="tpu_custom_call" | custom-call | flops 1 | bytes 1 | tf_op jit(solution)/shard_map/pallas_call | solution.py:444
  (141 shorter events, 51.9 us)
Async XLA Ops:
  0.6 16.0 %collective-permute-start.1 = (bf16[64,4096]{1,0:T(8,128)(2,1)}, bf16[64,4096]{1,0:T(8,128)(2,1)}, u32[]{:S(2)}, u32[]{:S(2)}) collective-permute-start(bf16[64,4096]{1,0:T(8,128)(2,1)} %bitcast.53), channel_id=1, source_target_pairs={{32,0},{64,32},{96,64},{128,96},{160,128},{192,160},{224,192},{33,... | collective-permute-start | bytes 1572872 | tf_op jit(solution)/shard_map/ppermute | solution.py:498
  12.5 43.2 %collective-permute-start.4 = (bf16[1024,768]{1,0:T(8,128)(2,1)S(1)}, bf16[1024,768]{1,0:T(8,128)(2,1)S(1)}, u32[]{:S(2)}, u32[]{:S(2)}) collective-permute-start(bf16[1024,768]{1,0:T(8,128)(2,1)S(1)} %shard_map.94.refs_4_.refs_1_), channel_id=1, source_target_pairs={{0,1},{1,2},{2,3},{3,0},{4,5},{5,6},{6,7},{7,4},{8,9},{9,10},{10,1... | collective-permute-start | bytes 4718600 | tf_op jit(solution)/shard_map/ppermute | solution.py:460
  14.5 41.1 %collective-permute-start.5 = (bf16[1024,768]{1,0:T(8,128)(2,1)S(1)}, bf16[1024,768]{1,0:T(8,128)(2,1)}, u32[]{:S(2)}, u32[]{:S(2)}) collective-permute-start(bf16[1024,768]{1,0:T(8,128)(2,1)S(1)} %shard_map.94.refs_4_.refs_1_), channel_id=1, source_target_pairs={{0,3},{1,0},{2,1},{3,2},{4,7},{5,4},{6,5},{7,6},{8,11},{9,8},{10,9... | collective-permute-start | bytes 4718600 | tf_op jit(solution)/shard_map/ppermute | solution.py:460
  20.8 27.8 %collective-permute-start.2 = (bf16[64,4096]{1,0:T(8,128)(2,1)}, bf16[64,4096]{1,0:T(8,128)(2,1)}, u32[]{:S(2)}, u32[]{:S(2)}) collective-permute-start(bf16[64,4096]{1,0:T(8,128)(2,1)} %fusion.1.refs_0_), channel_id=1, source_target_pairs={{0,24},{4,28},{8,0},{12,4},{16,8},{20,12},{24,16},{28,20},{1,25},{... | collective-permute-start | bytes 1572872 | tf_op jit(solution)/shard_map/ppermute | solution.py:467
  27.1 25.9 %collective-permute-start.3 = (bf16[64,4096]{1,0:T(8,128)(2,1)}, bf16[64,4096]{1,0:T(8,128)(2,1)}, u32[]{:S(2)}, u32[]{:S(2)}) collective-permute-start(bf16[64,4096]{1,0:T(8,128)(2,1)} %fusion.1.refs_0_), channel_id=1, source_target_pairs={{0,8},{4,12},{8,16},{12,20},{16,24},{20,28},{24,0},{28,4},{1,9},{5... | collective-permute-start | bytes 1572872 | tf_op jit(solution)/shard_map/ppermute | solution.py:467
  55.6 38.7 %collective-permute-start.8 = (bf16[192,4096]{1,0:T(8,128)(2,1)}, bf16[192,4096]{1,0:T(8,128)(2,1)}, u32[]{:S(2)}, u32[]{:S(2)}) collective-permute-start(bf16[192,4096]{1,0:T(8,128)(2,1)} %shard_map.93.refs_0_), channel_id=1, source_target_pairs={{0,4},{4,0},{8,12},{12,8},{16,20},{20,16},{24,28},{28,24},{1,5},{5... | collective-permute-start | bytes 4718600 | tf_op jit(solution)/shard_map/ppermute | solution.py:471
  62.1 16.7 %collective-permute-start.6 = (bf16[32,4096]{1,0:T(8,128)(2,1)}, bf16[32,4096]{1,0:T(8,128)(2,1)S(1)}, u32[]{:S(2)}, u32[]{:S(2)}) collective-permute-start(bf16[32,4096]{1,0:T(8,128)(2,1)} %copy-done.24), channel_id=1, source_target_pairs={{0,8},{4,12},{8,16},{12,20},{16,24},{20,28},{24,0},{28,4},{1,9},{5... | collective-permute-start | bytes 786440 | tf_op jit(solution)/shard_map/ppermute | solution.py:467
  62.2 16.6 %collective-permute-start.7 = (bf16[32,4096]{1,0:T(8,128)(2,1)}, bf16[32,4096]{1,0:T(8,128)(2,1)}, u32[]{:S(2)}, u32[]{:S(2)}) collective-permute-start(bf16[32,4096]{1,0:T(8,128)(2,1)} %copy-done.23), channel_id=1, source_target_pairs={{0,24},{4,28},{8,0},{12,4},{16,8},{20,12},{24,16},{28,20},{1,25},{... | collective-permute-start | bytes 786440 | tf_op jit(solution)/shard_map/ppermute | solution.py:467
  66.3 19.7 %collective-permute-start.10 = (bf16[512,768]{1,0:T(8,128)(2,1)}, bf16[512,768]{1,0:T(8,128)(2,1)}, u32[]{:S(2)}, u32[]{:S(2)}) collective-permute-start(bf16[512,768]{1,0:T(8,128)(2,1)} %copy-done.17), channel_id=1, source_target_pairs={{0,1},{1,2},{2,3},{3,0},{4,5},{5,6},{6,7},{7,4},{8,9},{9,10},{10,1... | collective-permute-start | bytes 2359304 | tf_op jit(solution)/shard_map/ppermute | solution.py:460
  66.5 27.8 %collective-permute-start.11 = (bf16[512,768]{1,0:T(8,128)(2,1)}, bf16[512,768]{1,0:T(8,128)(2,1)}, u32[]{:S(2)}, u32[]{:S(2)}) collective-permute-start(bf16[512,768]{1,0:T(8,128)(2,1)} %copy-done.16), channel_id=1, source_target_pairs={{0,3},{1,0},{2,1},{3,2},{4,7},{5,4},{6,5},{7,6},{8,11},{9,8},{10,9... | collective-permute-start | bytes 2359304 | tf_op jit(solution)/shard_map/ppermute | solution.py:460
  89.4 21.2 %collective-permute-start.12 = (bf16[256,1024]{1,0:T(8,128)(2,1)}, bf16[256,1024]{1,0:T(8,128)(2,1)}, u32[]{:S(2)}, u32[]{:S(2)}) collective-permute-start(bf16[256,1024]{1,0:T(8,128)(2,1)} %get-tuple-element.41), channel_id=1, source_target_pairs={{0,1},{1,2},{2,3},{3,0},{4,5},{5,6},{6,7},{7,4},{8,9},{9,10},{10,1... | collective-permute-start | bytes 1572872 | tf_op jit(solution)/shard_map/ppermute | solution.py:460
  90.9 19.7 %collective-permute-start.13 = (bf16[256,1024]{1,0:T(8,128)(2,1)}, bf16[256,1024]{1,0:T(8,128)(2,1)}, u32[]{:S(2)}, u32[]{:S(2)}) collective-permute-start(bf16[256,1024]{1,0:T(8,128)(2,1)} %get-tuple-element.42), channel_id=1, source_target_pairs={{0,3},{1,0},{2,1},{3,2},{4,7},{5,4},{6,5},{7,6},{8,11},{9,8},{10,9... | collective-permute-start | bytes 1572872 | tf_op jit(solution)/shard_map/ppermute | solution.py:460
  116.7 16.6 %collective-permute-start.21 = (bf16[256,1024]{1,0:T(8,128)(2,1)}, bf16[256,1024]{1,0:T(8,128)(2,1)}, u32[]{:S(2)}, u32[]{:S(2)}) collective-permute-start(bf16[256,1024]{1,0:T(8,128)(2,1)} %copy-done.18), channel_id=1, source_target_pairs={{0,2},{1,3},{2,0},{3,1},{4,6},{5,7},{6,4},{7,5},{8,10},{9,11},{10,... | collective-permute-start | bytes 1572872 | tf_op jit(solution)/shard_map/ppermute | solution.py:460
  119.1 30.6 %collective-permute-start.17 = (bf16[512,768]{1,0:T(8,128)(2,1)S(1)}, bf16[512,768]{1,0:T(8,128)(2,1)S(1)}, u32[]{:S(2)}, u32[]{:S(2)}) collective-permute-start(bf16[512,768]{1,0:T(8,128)(2,1)S(1)} %copy-done.2), channel_id=1, source_target_pairs={{0,1},{1,2},{2,3},{3,0},{4,5},{5,6},{6,7},{7,4},{8,9},{9,10},{10,1... | collective-permute-start | bytes 2359304 | tf_op jit(solution)/shard_map/ppermute | solution.py:460
  121.4 28.3 %collective-permute-start.18 = (bf16[512,768]{1,0:T(8,128)(2,1)S(1)}, bf16[512,768]{1,0:T(8,128)(2,1)S(1)}, u32[]{:S(2)}, u32[]{:S(2)}) collective-permute-start(bf16[512,768]{1,0:T(8,128)(2,1)S(1)} %copy-done.2), channel_id=1, source_target_pairs={{0,3},{1,0},{2,1},{3,2},{4,7},{5,4},{6,5},{7,6},{8,11},{9,8},{10,9... | collective-permute-start | bytes 2359304 | tf_op jit(solution)/shard_map/ppermute | solution.py:460
  123.9 42.1 %collective-permute-start.25 = (bf16[512,1024]{1,0:T(8,128)(2,1)}, bf16[512,1024]{1,0:T(8,128)(2,1)}, u32[]{:S(2)}, u32[]{:S(2)}) collective-permute-start(bf16[512,1024]{1,0:T(8,128)(2,1)} %shard_map.105), channel_id=1, source_target_pairs={{0,4},{4,0},{8,12},{12,8},{16,20},{20,16},{24,28},{28,24},{1,5},{5... | collective-permute-start | bytes 3145736 | tf_op jit(solution)/shard_map/ppermute | solution.py:471
  128.3 27.6 %collective-permute-start.15 = (bf16[64,4096]{1,0:T(8,128)(2,1)S(1)}, bf16[64,4096]{1,0:T(8,128)(2,1)S(1)}, u32[]{:S(2)}, u32[]{:S(2)}) collective-permute-start(bf16[64,4096]{1,0:T(8,128)(2,1)S(1)} %get-tuple-element.46), channel_id=1, source_target_pairs={{0,8},{4,12},{8,16},{12,20},{16,24},{20,28},{24,0},{28,4},{1,9},{5... | collective-permute-start | bytes 1572872 | tf_op jit(solution)/shard_map/ppermute | solution.py:467
  133.3 25.4 %collective-permute-start.16 = (bf16[64,4096]{1,0:T(8,128)(2,1)S(1)}, bf16[64,4096]{1,0:T(8,128)(2,1)S(1)}, u32[]{:S(2)}, u32[]{:S(2)}) collective-permute-start(bf16[64,4096]{1,0:T(8,128)(2,1)S(1)} %get-tuple-element.47), channel_id=1, source_target_pairs={{0,24},{4,28},{8,0},{12,4},{16,8},{20,12},{24,16},{28,20},{1,25},{... | collective-permute-start | bytes 1572872 | tf_op jit(solution)/shard_map/ppermute | solution.py:467
  149.7 26.1 %collective-permute-start.22 = (bf16[256,1024]{1,0:T(8,128)(2,1)}, bf16[256,1024]{1,0:T(8,128)(2,1)}, u32[]{:S(2)}, u32[]{:S(2)}) collective-permute-start(bf16[256,1024]{1,0:T(8,128)(2,1)} %collective-permute-done.21.refs_0_), channel_id=1, source_target_pairs={{0,4},{4,0},{8,12},{12,8},{16,20},{20,16},{24,28},{28,24},{1,5},{5... | collective-permute-start | bytes 1572872 | tf_op jit(solution)/shard_map/ppermute | solution.py:471
  159.9 15.9 %collective-permute-start.23 = (bf16[256,768]{1,0:T(8,128)(2,1)}, bf16[256,768]{1,0:T(8,128)(2,1)}, u32[]{:S(2)}, u32[]{:S(2)}) collective-permute-start(bf16[256,768]{1,0:T(8,128)(2,1)} %get-tuple-element.53), channel_id=1, source_target_pairs={{0,1},{1,2},{2,3},{3,0},{4,5},{5,6},{6,7},{7,4},{8,9},{9,10},{10,1... | collective-permute-start | bytes 1179656 | tf_op jit(solution)/shard_map/ppermute | solution.py:460
  165.7 18.1 %collective-permute-start.19 = (bf16[32,4096]{1,0:T(8,128)(2,1)}, bf16[32,4096]{1,0:T(8,128)(2,1)S(1)}, u32[]{:S(2)}, u32[]{:S(2)}) collective-permute-start(bf16[32,4096]{1,0:T(8,128)(2,1)} %copy-done.22), channel_id=1, source_target_pairs={{0,8},{4,12},{8,16},{12,20},{16,24},{20,28},{24,0},{28,4},{1,9},{5... | collective-permute-start | bytes 786440 | tf_op jit(solution)/shard_map/ppermute | solution.py:467
  166.0 17.9 %collective-permute-start.20 = (bf16[32,4096]{1,0:T(8,128)(2,1)}, bf16[32,4096]{1,0:T(8,128)(2,1)S(1)}, u32[]{:S(2)}, u32[]{:S(2)}) collective-permute-start(bf16[32,4096]{1,0:T(8,128)(2,1)} %copy-done.21), channel_id=1, source_target_pairs={{0,24},{4,28},{8,0},{12,4},{16,8},{20,12},{24,16},{28,20},{1,25},{... | collective-permute-start | bytes 786440 | tf_op jit(solution)/shard_map/ppermute | solution.py:467
  179.4 37.6 %collective-permute-start.26 = (bf16[1024,512]{1,0:T(8,128)(2,1)S(1)}, bf16[1024,512]{1,0:T(8,128)(2,1)S(1)}, u32[]{:S(2)}, u32[]{:S(2)}) collective-permute-start(bf16[1024,512]{1,0:T(8,128)(2,1)S(1)} %get-tuple-element.58.q_ref), channel_id=1, source_target_pairs={{0,224},{32,192},{64,160},{96,128},{128,96},{160,64},{192,32},{224... | collective-permute-start | bytes 3145736 | tf_op jit(solution)/shard_map/ppermute | solution.py:603
  183.7 33.3 %collective-permute-start.27 = (bf16[1024,256]{1,0:T(8,128)(2,1)S(1)}, bf16[1024,256]{1,0:T(8,128)(2,1)S(1)}, u32[]{:S(2)}, u32[]{:S(2)}) collective-permute-start(bf16[1024,256]{1,0:T(8,128)(2,1)S(1)} %get-tuple-element.59.kv_ref), channel_id=1, source_target_pairs={{0,224},{32,192},{64,160},{96,128},{128,96},{160,64},{192,32},{224... | collective-permute-start | bytes 1572872 | tf_op jit(solution)/shard_map/ppermute | solution.py:604
  (31 other events, 225.1 us)
where the time goes:
time: 223 us; the launch traced here: 220 us
  waiting for transfers between devices  99.7 us (45%)
  Pallas kernels  52.4 us (23%)
  starting transfers between devices  38.9 us (17%)
  local copies, waits for them, and re-layouts  17.7 us (8%)
  other arithmetic  8.12 us (4%)
  between operations  3.24 us (1%)
    ppermute x8, waiting for transfers between devices, shifted_chips(): return lax.ppermute(value, 'tensor', pairs)  39.1 us
    ppermute x1, waiting for transfers between devices, on_device(): far_kv = lax.ppermute(own_kv, 'pipe', pairs)  31.5 us
    ppermute x11, waiting for transfers between devices, shifted(): lax.ppermute(value, axis, [(i, (i + step) % count) for i in range(count)])  26.4 us
    ppermute x8, starting transfers between devices, shifted_chips(): return lax.ppermute(value, 'tensor', pairs)  15 us
    ppermute x11, starting transfers between devices, shifted(): lax.ppermute(value, axis, [(i, (i + step) % count) for i in range(count)])  12.7 us
    pallas_call x2, Pallas kernels, partial(): pl.pallas_call(functools.partial(partial_kernel, len(weights), rows, cuts...  9.37 us
    unnamed x62, local copies, waits for them, and re-layouts  8.51 us
    pallas_call x2, Pallas kernels, weight_grad(): pl.pallas_call(functools.partial(weight_grad_kernel, count, sums is None)...  8.21 us
  transfers between devices with their start and end apart: 28, of which 11 were waited for; matrix products, arithmetic and copies ran while one was open for 9% of the time, Pallas kernels for 20%

commit v1 on v0

v1 whole, which is shorter than its diff:
```python
import functools
import math

import jax
import jax.numpy as jnp
from jax import lax
from jax.experimental import pallas as pl
from jax.experimental.pallas import tpu as pltpu
from jax.sharding import PartitionSpec as P

BF = jnp.bfloat16
F32 = jnp.float32
GROUP = 128
LIGHT = pl.CostEstimate(flops=1, bytes_accessed=1, transcendentals=0)
VM = pl.BlockSpec(memory_space=pltpu.VMEM)


def sin_turns(r):
    a = jnp.abs(r)
    m = jnp.minimum(a, 0.5 - a)
    x = (2.0 * math.pi) * m
    y = x * x
    p = -1.0 / 39916800.0
    p = p * y + 1.0 / 362880.0
    p = p * y - 1.0 / 5040.0
    p = p * y + 1.0 / 120.0
    p = p * y - 1.0 / 6.0
    s = x + x * (y * p)
    return jnp.where(r < 0, -s, s)


def quantize_block(w):
    top = jnp.max(jnp.abs(w), axis=0, keepdims=True)
    scale = (top + 1e-06) / 7.0
    t = w * (1.0 / scale)
    wave = sin_turns(t - jnp.round(t))
    return scale * (t - wave * (1.0 / (2.0 * math.pi)))


def quantize_kernel(wq_ref, wkv_ref, out_ref):
    columns = wq_ref.shape[1]
    out_ref[:, :columns] = quantize_block(wq_ref[...].astype(F32)).astype(BF)
    out_ref[:, columns:] = quantize_block(wkv_ref[...].astype(F32)).astype(BF)


def quantize(w_query, w_keyval):
    rows, q_cols = w_query.shape
    kv_cols = w_keyval.shape[1]
    cols = q_cols + kv_cols
    return pl.pallas_call(
        quantize_kernel,
        grid=(rows // GROUP,),
        in_specs=[
            pl.BlockSpec((GROUP, q_cols), lambda i: (i, 0)),
            pl.BlockSpec((GROUP, kv_cols), lambda i: (i, 0)),
        ],
        out_specs=pl.BlockSpec((GROUP, cols), lambda i: (i, 0)),
        out_shape=jax.ShapeDtypeStruct((rows, cols), BF),
        compiler_params=pltpu.CompilerParams(vmem_limit_bytes=4 * 2**20),
        cost_estimate=LIGHT,
    )(w_query, w_keyval)


def dot(a, b, dims):
    return lax.dot_general(a, b, (dims, ((), ())), preferred_element_type=F32)


def whole(shape):
    return pl.BlockSpec(shape, lambda *_: (0,) * len(shape))


def copy_kernel(moves, count, *refs):
    sems = refs[-1]
    copies = []
    for n, (source, take, target, put) in enumerate(moves):
        copies.append(
            pltpu.make_async_copy(
                refs[source].at[take], refs[count + target].at[put], sems.at[n]
            )
        )
    for copy in copies:
        copy.start()
    for copy in copies:
        copy.wait()


def copied(inputs, specs, after, moves, shapes):
    count = len(inputs) + len(after)
    return pl.pallas_call(
        functools.partial(copy_kernel, moves, count),
        grid=(1,),
        in_specs=specs + [pl.BlockSpec(memory_space=pl.ANY)] * len(after),
        out_specs=[pl.BlockSpec(memory_space=pltpu.HBM)] * len(shapes),
        out_shape=[jax.ShapeDtypeStruct(shape, BF) for shape in shapes],
        scratch_shapes=[pltpu.SemaphoreType.DMA((len(moves),))],
        compiler_params=pltpu.CompilerParams(vmem_limit_bytes=8 * 2**20),
        cost_estimate=LIGHT,
    )(*inputs, *after)


def halves(first, second, after, both):
    rows, cols = first.shape
    half = rows // 2
    top = (slice(0, half), slice(0, cols))
    if both:
        every = (slice(0, rows), slice(0, cols))
        bottom = (slice(half, rows), slice(0, cols))
        specs = [whole(first.shape), whole(second.shape)]
        rest = (slice(rows, 2 * rows), slice(0, cols))
        moves = [(0, top, 0, top), (1, bottom, 1, top), (0, every, 2, every), (1, every, 2, rest)]
        shapes = [(half, cols)] * 2 + [(2 * rows, cols)]
    else:
        specs = [
            pl.BlockSpec((half, cols), lambda i: (0, 0)),
            pl.BlockSpec((half, cols), lambda i: (1, 0)),
        ]
        moves = [(0, top, 0, top), (1, top, 1, top)]
        shapes = [(half, cols)] * 2
    return copied([first, second], specs, after, moves, shapes)


def pack(tokens, cols, joined, after):
    count = tokens[0].shape[1] // cols - 1
    rows = sum(t.shape[0] for t in tokens)
    moves = []
    for block in range(count):
        row = 0
        for n, part in enumerate(tokens):
            size = part.shape[0]
            take = (slice(0, size), slice((block + 1) * cols, (block + 2) * cols))
            moves.append((n, take, block, (slice(row, row + size), slice(0, cols))))
            row += size
    row, model = 0, tokens[0].shape[1]
    for n in range(len(tokens) - joined, len(tokens)):
        size = tokens[n].shape[0]
        every = (slice(0, size), slice(0, model))
        moves.append((n, every, count, (slice(row, row + size), slice(0, model))))
        row += size
    specs = [whole(t.shape) for t in tokens]
    return copied(tokens, specs, after, moves, [(rows, cols)] * count + [(row, model)])


def relay_kernel(place_ref, fresh_ref, below_ref, above_ref, *rest):
    out_ref = rest[-1]
    source = place_ref[1]

    @pl.when(source == 0)
    def _():
        out_ref[...] = fresh_ref[...]

    @pl.when(source == 1)
    def _():
        out_ref[...] = below_ref[...]

    @pl.when(source == 2)
    def _():
        out_ref[...] = above_ref[...]


def relay(place, blocks, fresh, below, above, after):
    rows, model = fresh.shape
    tile = model // blocks
    source = pl.BlockSpec((rows, tile), lambda j, s: (0, (j + s[0]) % blocks))
    return pl.pallas_call(
        relay_kernel,
        grid_spec=pltpu.PrefetchScalarGridSpec(
            num_scalar_prefetch=1,
            grid=(blocks,),
            in_specs=[source] * 3 + [pl.BlockSpec(memory_space=pl.ANY)] * len(after),
            out_specs=pl.BlockSpec((rows, tile), lambda j, s: (0, j)),
        ),
        out_shape=jax.ShapeDtypeStruct((rows, model), BF),
        compiler_params=pltpu.CompilerParams(vmem_limit_bytes=4 * 2**20),
        cost_estimate=LIGHT,
    )(place, fresh, below, above, *after)


def gather_kernel(place_ref, in_ref, out_ref):
    width = in_ref.shape[2]
    for i in range(in_ref.shape[1]):
        out_ref[:, i * width : (i + 1) * width] = in_ref[:, i, :]


def gather_rows(place, value):
    rows, heads, width = value.shape
    count = place.shape[0]
    tile = rows // count
    return pl.pallas_call(
        gather_kernel,
        grid_spec=pltpu.PrefetchScalarGridSpec(
            num_scalar_prefetch=1,
            grid=(count,),
            in_specs=[pl.BlockSpec((tile, heads, width), lambda i, s: (s[i], 0, 0))],
            out_specs=pl.BlockSpec((tile, heads * width), lambda i, s: (i, 0)),
        ),
        out_shape=jax.ShapeDtypeStruct((rows, heads * width), value.dtype),
        compiler_params=pltpu.CompilerParams(vmem_limit_bytes=4 * 2**20),
        cost_estimate=LIGHT,
    )(place, value)


def scatter_kernel(place_ref, in_ref, after_ref, out_ref):
    width = out_ref.shape[2]
    for i in range(out_ref.shape[1]):
        out_ref[:, i, :] = in_ref[:, i * width : (i + 1) * width]


def scatter_rows(place, value, width, after):
    rows, cols = value.shape
    heads = cols // width
    count = place.shape[0]
    tile = rows // count
    return pl.pallas_call(
        scatter_kernel,
        grid_spec=pltpu.PrefetchScalarGridSpec(
            num_scalar_prefetch=1,
            grid=(count,),
            in_specs=[
                pl.BlockSpec((tile, cols), lambda i, s: (i, 0)),
                pl.BlockSpec(memory_space=pl.ANY),
            ],
            out_specs=pl.BlockSpec((tile, heads, width), lambda i, s: (s[i], 0, 0)),
        ),
        out_shape=jax.ShapeDtypeStruct((rows, heads, width), value.dtype),
        compiler_params=pltpu.CompilerParams(vmem_limit_bytes=4 * 2**20),
        cost_estimate=LIGHT,
    )(place, value, after)


def first_half(value):
    return pl.BlockSpec((value.shape[0] // 2, value.shape[1]), lambda i: (0, 0))


def half_of(value):
    return jax.ShapeDtypeStruct((value.shape[0] // 2, value.shape[1]), value.dtype)


def second_step_kernel(up_ref, down_ref, next_ref, prev_ref, up_out, down_out):
    up_out[...] = (up_ref[...].astype(F32) + next_ref[...].astype(F32)).astype(BF)
    down_out[...] = (down_ref[...].astype(F32) + prev_ref[...].astype(F32)).astype(BF)


def second_step(up, down, next_top, prev_bot):
    outs = [half_of(up), half_of(down)]
    return pl.pallas_call(
        second_step_kernel,
        grid=(1,),
        in_specs=[first_half(up), first_half(down)]
        + [whole(next_top.shape), whole(prev_bot.shape)],
        out_specs=[whole(o.shape) for o in outs],
        out_shape=outs,
        compiler_params=pltpu.CompilerParams(vmem_limit_bytes=4 * 2**20),
        cost_estimate=LIGHT,
    )(up, down, next_top, prev_bot)


def input_grad_kernel(shift_ref, kept_ref, up_ref, down_ref, up2_ref, down2_ref, out_ref):
    half = up2_ref.shape[0]
    total = kept_ref[...].astype(F32)
    bottom = total[half:] + up_ref[...].astype(F32) + down2_ref[...].astype(F32)
    top = total[:half] + up2_ref[...].astype(F32) + down_ref[...].astype(F32)
    out_ref[:half, :] = top.astype(BF)
    out_ref[half:, :] = bottom.astype(BF)


def input_grad(replica, replicas, kept, up, down, up2, down2):
    rows, model = kept.shape
    tile = model // replicas
    part = lambda r, k: pl.BlockSpec((r, tile), lambda j, s: (k, j))
    return pl.pallas_call(
        input_grad_kernel,
        grid_spec=pltpu.PrefetchScalarGridSpec(
            num_scalar_prefetch=1,
            grid=(replicas,),
            in_specs=[
                part(rows, 0),
                part(rows // 2, 1),
                part(rows // 2, 1),
                part(rows // 2, 0),
                part(rows // 2, 0),
            ],
            out_specs=pl.BlockSpec((rows, tile), lambda j, s: (0, (j + s[0]) % replicas)),
        ),
        out_shape=jax.ShapeDtypeStruct((rows, model), BF),
        compiler_params=pltpu.CompilerParams(vmem_limit_bytes=4 * 2**20),
        cost_estimate=pl.CostEstimate(
            flops=40 * 10**9, bytes_accessed=160 * 2**20, transcendentals=0
        ),
    )(replica.reshape(1), kept, up, down, up2, down2)


def project_kernel(parts, *refs):
    tokens, weights = refs[:parts], refs[parts:-3]
    out_ref, first_ref, held = refs[-3:]

    @pl.when(pl.program_id(0) == 0)
    def _():
        row = 0
        for ref in tokens:
            held[row : row + ref.shape[0], :] = ref[...]
            row += ref.shape[0]
        first_ref[...] = held[:, : first_ref.shape[1]]

    total, at = None, 0
    for ref in weights:
        term = dot(held[:, at : at + ref.shape[0]], ref[...], ((1,), (0,)))
        total = term if total is None else total + term
        at += ref.shape[0]
    out_ref[...] = total.astype(BF)


def project(tokens, weights, first):
    rows = sum(t.shape[0] for t in tokens)
    model = tokens[0].shape[1]
    cols = weights[0].shape[1]
    tile = 256
    return pl.pallas_call(
        functools.partial(project_kernel, len(tokens)),
        grid=(cols // tile,),
        in_specs=[whole(t.shape) for t in tokens]
        + [pl.BlockSpec((w.shape[0], tile), lambda i: (0, i)) for w in weights],
        out_specs=[pl.BlockSpec((rows, tile), lambda i: (0, i)), whole((rows, first))],
        out_shape=[
            jax.ShapeDtypeStruct((rows, cols), BF),
            jax.ShapeDtypeStruct((rows, first), BF),
        ],
        scratch_shapes=[pltpu.VMEM((rows, model), BF)],
        compiler_params=pltpu.CompilerParams(vmem_limit_bytes=28 * 2**20),
        cost_estimate=LIGHT,
    )(*tokens, *weights)


def attention_kernel(
    q_ref, kv_ref, cos_ref, sin_ref, pos_row_ref, pos_col_ref, og_ref,
    out_ref, d_ref, k_rot, dk_sum, dv_sum,
):
    width = cos_ref.shape[1]
    half = width // 2
    head = pl.program_id(0)
    heads = pl.num_programs(0)
    cosine = cos_ref[...]
    signed = sin_ref[...]

    @pl.when(head == 0)
    def _():
        k = kv_ref[:, :width].astype(F32)
        k_rot[...] = (k * cosine + pltpu.roll(k, half, 1) * signed).astype(BF)
        dk_sum[...] = jnp.zeros_like(dk_sum)
        dv_sum[...] = jnp.zeros_like(dv_sum)

    values = kv_ref[:, width:]
    keys = k_rot[...]
    q = q_ref[...].astype(F32)
    q_rot = (q * cosine + pltpu.roll(q, half, 1) * signed).astype(BF)
    factor = 1.0 / math.sqrt(width)
    scores = dot(q_rot, keys, ((1,), (1,)))
    visible = pos_row_ref[...] <= pos_col_ref[...]
    scores = jnp.where(visible, scores, -1e30)
    raised = jnp.exp2(
        (scores - jnp.max(scores, axis=1, keepdims=True)) * (factor * math.log2(math.e))
    )
    weights = raised * (1.0 / jnp.sum(raised, axis=1, keepdims=True))
    weights_low = weights.astype(BF)
    out_ref[...] = dot(weights_low, values, ((1,), (0,))).astype(BF)
    cotangent = og_ref[...]
    dv_sum[...] += dot(weights_low, cotangent, ((0,), (0,)))
    d_weights = dot(cotangent, values, ((1,), (1,)))
    delta = jnp.sum(d_weights * weights, axis=1, keepdims=True)
    d_scores = (weights * (d_weights - delta)).astype(BF)
    dq = dot(d_scores, keys, ((1,), (0,))) * factor
    dk_sum[...] += dot(d_scores, q_rot, ((0,), (0,)))
    place = pl.ds(pl.multiple_of(head * width, width), width)
    d_ref[:, place] = (dq * cosine + pltpu.roll(dq * signed, half, 1)).astype(BF)

    @pl.when(head == heads - 1)
    def _():
        dk = dk_sum[...] * factor
        q_cols = d_ref.shape[1] - 2 * width
        dk = (dk * cosine + pltpu.roll(dk * signed, half, 1)).astype(BF)
        d_ref[:, q_cols : q_cols + width] = dk
        d_ref[:, q_cols + width :] = dv_sum[...].astype(BF)


def attention(projected, heads, width, cos_t, sin_t, positions, out_grad):
    length, cols = projected.shape
    q_cols = heads * width
    column = pl.BlockSpec((length, width), lambda h: (0, h))
    return pl.pallas_call(
        attention_kernel,
        grid=(heads,),
        in_specs=[
            column,
            pl.BlockSpec((length, 2 * width), lambda h: (0, heads // 2)),
            whole((length, width)),
            whole((length, width)),
            whole((1, length)),
            whole((length, 1)),
            column,
        ],
        out_specs=[column, whole((length, cols))],
        out_shape=[
            jax.ShapeDtypeStruct((length, q_cols), BF),
            jax.ShapeDtypeStruct((length, cols), BF),
        ],
        scratch_shapes=[
            pltpu.VMEM((length, width), BF),
            pltpu.VMEM((length, width), F32),
            pltpu.VMEM((length, width), F32),
        ],
        compiler_params=pltpu.CompilerParams(vmem_limit_bytes=16 * 2**20),
        cost_estimate=LIGHT,
    )(projected, projected, cos_t, sin_t, positions[None, :], positions[:, None], out_grad)


def partial_kernel(parts, rows, *refs):
    weights, (out_ref, held, sems) = refs[1 : 1 + parts], refs[-3:]
    copies, at = [], 0
    for n, ref in enumerate(weights):
        size = ref.shape[0]
        copies.append(pltpu.make_async_copy(ref, held.at[at : at + size, :], sems.at[n]))
        at += size
    for copy in copies:
        copy.start()
    grads = refs[0][rows[0] : rows[1], :]
    at = 0
    for copy, ref in zip(copies, weights):
        columns = slice(at, at + ref.shape[0])
        copy.wait()
        out_ref[:, columns] = dot(grads, held[columns, :], ((1,), (1,))).astype(BF)
        at += ref.shape[0]


def partial(grads, weights, rows, after):
    cols = grads.shape[1]
    model = sum(w.shape[0] for w in weights)
    anywhere = pl.BlockSpec(memory_space=pl.ANY)
    return pl.pallas_call(
        functools.partial(partial_kernel, len(weights), rows),
        in_specs=[VM] + [anywhere] * (len(weights) + len(after)),
        out_specs=VM,
        out_shape=jax.ShapeDtypeStruct((rows[1] - rows[0], model), BF),
        scratch_shapes=[
            pltpu.VMEM((model, cols), BF),
            pltpu.SemaphoreType.DMA((len(weights),)),
        ],
        compiler_params=pltpu.CompilerParams(vmem_limit_bytes=12 * 2**20),
        cost_estimate=LIGHT,
    )(grads, *weights, *after)


def chip_sum_kernel(cuts, a_ref, b_ref, *outs):
    for out, ranges in zip(outs, cuts):
        row = 0
        for low, high in ranges:
            total = a_ref[low:high, :].astype(F32) + b_ref[low:high, :].astype(F32)
            out[row : row + high - low, :] = total.astype(BF)
            row += high - low


def chip_sum(a, b, cuts):
    rows, model = a.shape
    tile = model // 4
    sizes = [sum(high - low for low, high in ranges) for ranges in cuts]
    block = lambda r: pl.BlockSpec((r, tile), lambda j: (0, j))
    return pl.pallas_call(
        functools.partial(chip_sum_kernel, cuts),
        grid=(model // tile,),
        in_specs=[block(rows)] * 2,
        out_specs=[block(size) for size in sizes],
        out_shape=[jax.ShapeDtypeStruct((size, model), BF) for size in sizes],
        compiler_params=pltpu.CompilerParams(vmem_limit_bytes=6 * 2**20),
        cost_estimate=LIGHT,
    )(a, b)


def weight_grad_kernel(count, first, *refs):
    tokens, grads, rest = refs[:count], refs[count : 2 * count], refs[2 * count :]
    rest = rest[-1:] if first else rest[:1] + rest[-2:]
    total = None if first else rest[0][...]
    for x, d in zip(tokens, grads):
        term = dot(x[...], d[...], ((0,), (0,)))
        total = term if total is None else total + term
    if first:
        rest[0][...] = total
    else:
        q_ref, kv_ref = rest[1:]
        q_cols = q_ref.shape[1]
        q_ref[...] = total[:, :q_cols].astype(BF)
        kv_ref[...] = total[:, q_cols:].astype(BF)


def weight_grad(tokens, grads, sums, q_cols, after=()):
    count = len(tokens)
    d_rows = tokens[0].shape[1]
    cols = grads[0][0].shape[1]
    tile = 256
    block = lambda width: pl.BlockSpec((tile, width), lambda i: (i, 0))
    in_specs = [pl.BlockSpec((t.shape[0], tile), lambda i: (0, i)) for t in tokens]
    for grad, part in grads:
        if part is None:
            in_specs.append(whole(grad.shape))
        else:
            shape = (grad.shape[0] // 2, cols)
            in_specs.append(pl.BlockSpec(shape, functools.partial(lambda p, i: (p, 0), part)))
    if sums is None:
        operands = tuple(after)
        in_specs += [pl.BlockSpec(memory_space=pl.ANY)] * len(after)
        out_specs = block(cols)
        out_shape = jax.ShapeDtypeStruct((d_rows, cols), F32)
    else:
        operands = (sums,) + tuple(after)
        in_specs.append(block(cols))
        in_specs += [pl.BlockSpec(memory_space=pl.ANY)] * len(after)
        out_specs = [block(q_cols), block(cols - q_cols)]
        out_shape = [
            jax.ShapeDtypeStruct((d_rows, q_cols), BF),
            jax.ShapeDtypeStruct((d_rows, cols - q_cols), BF),
        ]
    return pl.pallas_call(
        functools.partial(weight_grad_kernel, count, sums is None),
        grid=(d_rows // tile,),
        in_specs=in_specs,
        out_specs=out_specs,
        out_shape=out_shape,
        compiler_params=pltpu.CompilerParams(vmem_limit_bytes=13 * 2**20),
        cost_estimate=LIGHT,
    )(*tokens, *[g for g, _ in grads], *operands)


def mirror_sum_kernel(q_ref, q_far_ref, kv_ref, kv_far_ref, *rest):
    out_q_ref, out_kv_ref = rest[-2:]
    width = out_q_ref.shape[-1]
    q = q_ref[...].astype(F32) + q_far_ref[...].astype(F32)
    kv = kv_ref[...].astype(F32) + kv_far_ref[...].astype(F32)
    for i in range(out_q_ref.shape[1]):
        out_q_ref[:, i, :] = q[:, i * width : (i + 1) * width]
    for i in range(out_kv_ref.shape[1]):
        out_kv_ref[:, i, :] = kv[:, i * width : (i + 1) * width]


def mirror_sum(q, q_far, kv, kv_far, after, width):
    rows, q_cols = q.shape
    kv_cols = kv.shape[1]
    tile = 256
    flat = lambda cols: pl.BlockSpec((tile, cols), lambda i: (i, 0))
    deep = lambda cols: pl.BlockSpec((tile, cols // width, width), lambda i: (i, 0, 0))
    return pl.pallas_call(
        mirror_sum_kernel,
        grid=(rows // tile,),
        in_specs=[flat(q_cols), flat(q_cols), flat(kv_cols), flat(kv_cols)]
        + [pl.BlockSpec(memory_space=pl.ANY)] * len(after),
        out_specs=[deep(q_cols), deep(kv_cols)],
        out_shape=[
            jax.ShapeDtypeStruct((rows, q_cols // width, width), F32),
            jax.ShapeDtypeStruct((rows, kv_cols // width, width), F32),
        ],
        compiler_params=pltpu.CompilerParams(vmem_limit_bytes=6 * 2**20),
        cost_estimate=LIGHT,
    )(q, q_far, kv, kv_far, *after)


def shifted(value, axis, step):
    count = lax.axis_size(axis)
    return lax.ppermute(value, axis, [(i, (i + step) % count) for i in range(count)])


def shifted_chips(value, step):
    count = lax.axis_size("tensor")
    chips = count // 2
    pairs = [(i, ((i // 2 + step) % chips) * 2 + i % 2) for i in range(count)]
    return lax.ppermute(value, "tensor", pairs)


def other_core(value):
    return lax.ppermute(value, "tensor", [(i, i ^ 1) for i in range(lax.axis_size("tensor"))])


def roll_blocks(value, axis, shift, count):
    block = value.shape[axis] // count
    doubled = jnp.concatenate([value, value], axis=axis)
    return lax.dynamic_slice_in_dim(doubled, shift * block, value.shape[axis], axis=axis)


def on_device(act, direction, positions, w_query, w_keyval, out_grad):
    section = lax.axis_index("pipe")
    sections = lax.axis_size("pipe")
    tensor = lax.axis_index("tensor")
    chip, core = tensor // 2, tensor % 2
    chips = lax.axis_size("tensor") // 2
    replica = lax.axis_index("dp")
    replicas = lax.axis_size("dp")
    d_rows, heads, width = w_query.shape[1:]
    seq_len = positions.shape[2]
    q_cols = heads * width
    piece = act.shape[2]
    near = seq_len // 2
    half = piece // 2

    fresh = act[0, 0]
    ends = sections - 1
    from_below = lax.ppermute(fresh, "pipe", [(i, i + 1) for i in range(ends)])
    from_above = lax.ppermute(fresh, "pipe", [(i + 1, i) for i in range(ends)])

    w_own = quantize(w_query[0].reshape(d_rows, -1), w_keyval[0].reshape(d_rows, -1))
    w_before = shifted(w_own, "dp", 1)
    w_after = shifted(w_own, "dp", -1)

    heading = lax.dynamic_index_in_dim(direction, section, 0, keepdims=False)[0]
    source = jnp.where(
        heading == 0, jnp.where(section == 0, 0, 1), jnp.where(section == ends, 0, 2)
    )
    order = jnp.array([0, 1, chips - 1, 2], jnp.int32)
    order = (chip + order) % chips
    place = jnp.concatenate([order * 2 + core, order * 2 + 1 - core])
    pos = jnp.take(positions[0, 0].reshape(-1, piece), place, axis=0).reshape(-1)
    cotangent = gather_rows(place, out_grad[0, 0])
    angle_half = width // 2
    inv_freq = 1000000.0 ** (-jnp.arange(angle_half, dtype=F32) / angle_half)
    angles = pos.astype(F32)[:, None] * inv_freq[None, :]
    cosine, sine = jnp.cos(angles), jnp.sin(angles)
    cos_t = jnp.concatenate([cosine, cosine], axis=1)
    sin_t = jnp.concatenate([-sine, sine], axis=1)
    own = relay(
        jnp.stack([replica, source]),
        replicas,
        fresh,
        from_below,
        from_above,
        [w_own, cos_t, sin_t, cotangent],
    )
    prev = shifted_chips(own, 1)
    after = shifted_chips(own, -1)

    other_own = other_core(own)
    before_top, after_bot = halves(w_before, w_after, [other_own], False)
    next_top, prev_bot, beside = halves(after, prev, [before_top], True)
    far_top = shifted(before_top, "dp", 1)
    far_bot = shifted(after_bot, "dp", -1)
    across_top = shifted_chips(next_top, -1)
    across_bot = shifted_chips(prev_bot, 1)

    *blocks, across = pack(
        [own, beside, across_top, across_bot], d_rows, 2, [far_top, far_bot]
    )
    sent = [shifted(blocks[k - 1], "dp", k) for k in range(1, replicas)]
    token_parts = [own, beside, across]
    other_parts = [other_own, other_core(beside), other_core(across)]

    weights = [w_own, w_after, far_top, far_bot, w_before]
    projected, x_own = project(token_parts + other_parts, weights, d_rows)
    attended, d_own = attention(projected, heads, width, cos_t, sin_t, pos, cotangent)

    other_part = other_core(partial(d_own, weights, (near, seq_len), sent))
    sent_other = [other_core(x) for x in sent]
    own_part = partial(d_own, weights, (0, near), ())
    low = [i * piece for i in range(chips)]
    mid = [i * piece + half for i in range(chips)]
    high = [(i + 1) * piece for i in range(chips)]
    kept, up, next_top, down, prev_bot = chip_sum(
        own_part,
        other_part,
        [
            [(low[0], high[0])],
            [(low[3], mid[3]), (mid[1], high[1])],
            [(low[1], mid[1])],
            [(mid[3], high[3]), (low[2], mid[2])],
            [(mid[2], high[2])],
        ],
    )
    up = shifted_chips(up, 1)
    down = shifted_chips(down, -1)

    up2_part, down2_part = second_step(up, down, next_top, prev_bot)
    up2 = shifted_chips(up2_part, 1)
    down2 = shifted_chips(down2_part, -1)
    grad_input = input_grad(replica, replicas, kept, up, down, up2, down2)

    d_sent = [shifted(d_own, "dp", k) for k in range(1, replicas)]
    attn_out = scatter_rows(place, attended, width, kept)[None, None]
    sums = weight_grad(
        [x_own, sent[0], sent_other[0], sent[2], sent_other[2]],
        [(d_own, None), (d_sent[0], 0), (d_sent[0], 1), (d_sent[2], 0), (d_sent[2], 1)],
        None,
        q_cols,
        [kept, attn_out],
    )
    own_q, own_kv = weight_grad(
        [sent[1], sent_other[1]], [(d_sent[1], 0), (d_sent[1], 1)], sums, q_cols, [up2_part]
    )
    pairs = [(i, ends - i) for i in range(sections)]
    far_q = lax.ppermute(own_q, "pipe", pairs)
    far_kv = lax.ppermute(own_kv, "pipe", pairs)
    grad_query, grad_keyval = mirror_sum(
        own_q, far_q, own_kv, far_kv, [grad_input], width
    )
    return attn_out, grad_input[None, None], grad_query[None], grad_keyval[None, :, None]


def solution(mesh):
    return jax.shard_map(
        on_device,
        mesh=mesh,
        in_specs=(
            P("pipe", "dp", "tensor", None),
            P(None, "dp"),
            P("pipe", "dp", None),
            P("pipe", "dp", "tensor", None),
            P("pipe", "dp", "tensor", None, None),
            P("pipe", "dp", None, "tensor", None),
        ),
        out_specs=(
            P("pipe", "dp", None, "tensor", None),
            P("pipe", "dp", "tensor", None),
            P("pipe", "dp", "tensor", None),
            P("pipe", "dp", "tensor", None, None),
        ),
        check_vma=False,
    )
```

time: 223 us -> 207 us (0.928)
  other arithmetic: 8.12 us -> 2.8 us
  local copies, waits for them, and re-layouts: 17.7 us -> 12.9 us
  waiting for transfers between devices: 99.7 us -> 96.9 us
    another operation x6 -> x1, local copies, waits for them, and re-layouts: 5.07 us -> 0.08 us  [on_device(): positions[0, 0].reshape(-1, piece)]
    ppermute x1, waiting for transfers between devices: 31.5 us -> 28 us  [on_device(): far_kv = lax.ppermute(own_kv, 'pipe', pairs)]
    select_n x3 -> x1, other arithmetic: 3.29 us -> 0.08 us  [on_device(): jnp.take(positions[0, 0].reshape(-1, piece), place, axis=0).reshape(-1)]
    ppermute x8, starting transfers between devices: 15 us -> 17.7 us  [shifted_chips(): return lax.ppermute(value, 'tensor', pairs)]
    unnamed x62 -> x47, local copies, waits for them, and re-layouts: 8.51 us -> 11.2 us
    concatenate x5 -> x1, other arithmetic: 2.39 us -> 0.01 us  [on_device(): place = jnp.concatenate([order * 2 + core, order * 2 + 1 - core])]
    slice x4 -> x0, local copies, waits for them, and re-layouts: 2.34 us -> none  [the longest x1 1.27 us: on_device(): near_other[near:]]
    ppermute x11 -> x10, starting transfers between devices: 12.7 us -> 10.9 us  [shifted(): lax.ppermute(value, axis, [(i, (i + step) % count) for i in range(count)])]
  transfers between devices with their start and end apart: 28 -> 29, of which waited for: 11 -> 11; matrix products, arithmetic and copies ran while one was open for 9% -> 3% of each run, Pallas kernels for 20% -> 22%
where the time goes in v1:
time: 207 us; the launch traced here: 206 us
  waiting for transfers between devices  96.9 us (47%)
  Pallas kernels  51.8 us (25%)
  starting transfers between devices  39.8 us (19%)
  local copies, waits for them, and re-layouts  12.9 us (6%)
  other arithmetic  2.8 us (1%)
    ppermute x8, waiting for transfers between devices, shifted_chips(): return lax.ppermute(value, 'tensor', pairs)  39.2 us
    ppermute x10, waiting for transfers between devices, shifted(): lax.ppermute(value, axis, [(i, (i + step) % count) for i in range(count)])  28.1 us
    ppermute x1, waiting for transfers between devices, on_device(): far_kv = lax.ppermute(own_kv, 'pipe', pairs)  28 us
    ppermute x8, starting transfers between devices, shifted_chips(): return lax.ppermute(value, 'tensor', pairs)  17.7 us
    unnamed x47, local copies, waits for them, and re-layouts  11.2 us
    ppermute x10, starting transfers between devices, shifted(): lax.ppermute(value, axis, [(i, (i + step) % count) for i in range(count)])  10.9 us
    pallas_call x2, Pallas kernels, weight_grad(): pl.pallas_call(functools.partial(weight_grad_kernel, count, sums is None)...  7.66 us
    pallas_call x1, Pallas kernels, attention(): pl.pallas_call(attention_kernel, grid=(heads,), in_specs=[column, pl.Bloc...  7.46 us
  transfers between devices with their start and end apart: 29, of which 11 were waited for; matrix products, arithmetic and copies ran while one was open for 3% of the time, Pallas kernels for 22%

profile of v1, /device:TPU:24, one launch (start us, length us, event | category | flops | bytes accessed | tf_op | source)
XLA Modules:
  0.0 205.9 jit_solution(14909111510511949412)
XLA Ops:
  0.6 4.4 %collective-permute-start = (bf16[64,4096]{1,0:T(8,128)(2,1)}, bf16[64,4096]{1,0:T(8,128)(2,1)}, u32[]{:S(2)}, u32[]{:S(2)}) collective-permute-start(bf16[64,4096]{1,0:T(8,128)(2,1)} %bitcast.30), channel_id=1, source_target_pairs={{0,32},{32,64},{64,96},{96,128},{128,160},{160,192},{192,224},{1,3... | collective-permute-start | bytes 1572872 | tf_op jit(solution)/shard_map/ppermute | solution.py:601
  7.8 3.5 %shard_map.102.rest_0_.refs_6_.refs_1_ = bf16[1024,768]{1,0:T(8,128)(2,1)S(1)} custom-call(bf16[1024,512]{1,0:T(8,128)(2,1)S(1)} %bitcast.26, bf16[1024,256]{1,0:T(8,128)(2,1)S(1)} %bitcast.29), custom_call_target="tpu_custom_call" | custom-call | flops 1 | bytes 1 | tf_op jit(solution)/shard_map/pallas_call | solution.py:50
  21.7 2.8 %shard_map.104.refs_0_ = bf16[64,4096]{1,0:T(8,128)(2,1)S(1)} custom-call(s32[2]{0:T(128)S(1)} %pad_add_fusion.1.place_ref, bf16[64,4096]{1,0:T(8,128)(2,1)S(1)} %bitcast.32, bf16[64,4096]{1,0:T(8,128)(2,1)} %collective-permute-done.below_ref, bf16[64,4096]{1,0:T(8,128)(2,1)} %collective-permute-done.1.above_ref, ...), custom_call_target="tpu_custom_call" | custom-call | flops 1 | bytes 1 | tf_op jit(solution)/shard_map/pallas_call | solution.py:164
  24.7 6.4 %collective-permute-start.2 = (bf16[64,4096]{1,0:T(8,128)(2,1)S(1)}, bf16[64,4096]{1,0:T(8,128)(2,1)S(1)}, u32[]{:S(2)}, u32[]{:S(2)}) collective-permute-start(bf16[64,4096]{1,0:T(8,128)(2,1)S(1)} %shard_map.104.refs_0_), channel_id=1, source_target_pairs={{0,24},{4,28},{8,0},{12,4},{16,8},{20,12},{24,16},{28,20},{1,25},{... | collective-permute-start | bytes 1572872 | tf_op jit(solution)/shard_map/ppermute | solution.py:571
  31.1 16.2 %collective-permute-done.4.refs_0_.refs_10_.refs_5_ = bf16[1024,768]{1,0:T(8,128)(2,1)S(1)} collective-permute-done((bf16[1024,768]{1,0:T(8,128)(2,1)S(1)}, bf16[1024,768]{1,0:T(8,128)(2,1)S(1)}, u32[]{:S(2)}, u32[]{:S(2)}) %collective-permute-start.4) | collective-permute-done | bytes 1572896 | tf_op jit(solution)/shard_map/ppermute | solution.py:564
  50.5 2.8 %collective-permute-start.9 = (bf16[512,768]{1,0:T(8,128)(2,1)S(1)}, bf16[512,768]{1,0:T(8,128)(2,1)S(1)}, u32[]{:S(2)}, u32[]{:S(2)}) collective-permute-start(bf16[512,768]{1,0:T(8,128)(2,1)S(1)} %get-tuple-element.28.refs_2_), channel_id=1, source_target_pairs={{0,1},{1,2},{2,3},{3,0},{4,5},{5,6},{6,7},{7,4},{8,9},{9,10},{10,1... | collective-permute-start | bytes 2359304 | tf_op jit(solution)/shard_map/ppermute | solution.py:564
  54.1 4.3 %collective-permute-done.3.refs_1_ = bf16[64,4096]{1,0:T(8,128)(2,1)S(1)} collective-permute-done((bf16[64,4096]{1,0:T(8,128)(2,1)S(1)}, bf16[64,4096]{1,0:T(8,128)(2,1)S(1)}, u32[]{:S(2)}, u32[]{:S(2)}) %collective-permute-start.3) | collective-permute-done | bytes 524320 | tf_op jit(solution)/shard_map/ppermute | solution.py:571
  62.6 12.3 %collective-permute-done.7.refs_2_ = bf16[32,4096]{1,0:T(8,128)(2,1)S(1)} collective-permute-done((bf16[32,4096]{1,0:T(8,128)(2,1)S(1)}, bf16[32,4096]{1,0:T(8,128)(2,1)S(1)}, u32[]{:S(2)}, u32[]{:S(2)}) %collective-permute-start.7) | collective-permute-done | bytes 262176 | tf_op jit(solution)/shard_map/ppermute | solution.py:571
  77.0 3.0 %shard_map.107 = (bf16[256,1024]{1,0:T(8,128)(2,1)}, bf16[256,1024]{1,0:T(8,128)(2,1)}, bf16[256,1024]{1,0:T(8,128)(2,1)}, bf16[64,4096]{1,0:T(8,128)(2,1)}) custom-call(bf16[64,4096]{1,0:T(8,128)(2,1)S(1)} %shard_map.104.refs_0_, bf16[128,4096]{1,0:T(8,128)(2,1)} %get-tuple-element.29.refs_1_, bf16[32,4096]{1,0:T(8,128)(2,1)S(1)} %collective-permute-done.7.refs_2_, ...), custom_call_target="tpu_custom_call" | custom-call | flops 1 | bytes 1 | tf_op jit(solution)/shard_map/pallas_call | solution.py:89
  88.2 6.5 %shard_map.108 = (bf16[512,768]{1,0:T(8,128)(2,1)S(1)}, bf16[512,1024]{1,0:T(8,128)(2,1)S(1)}) custom-call(bf16[64,4096]{1,0:T(8,128)(2,1)S(1)} %copy-done.5, bf16[128,4096]{1,0:T(8,128)(2,1)} %get-tuple-element.29.refs_1_, bf16[64,4096]{1,0:T(8,128)(2,1)} %get-tuple-element.33.refs_2_, bf16[64,4096]{1,0:T(8,128)(2,1)S(1)} %copy-done.12, ...), custom_call_target="tpu_custom_call" | custom-call | flops 1 | bytes 1 | tf_op jit(solution)/shard_map/pallas_call | solution.py:317
  94.7 7.5 %shard_map.109 = (bf16[512,512]{1,0:T(8,128)(2,1)S(1)}, bf16[512,768]{1,0:T(8,128)(2,1)S(1)}) custom-call(bf16[512,768]{1,0:T(8,128)(2,1)S(1)} %get-tuple-element.34.q_ref.kv_ref, bf16[512,768]{1,0:T(8,128)(2,1)S(1)} %get-tuple-element.34.q_ref.kv_ref, f32[512,128]{1,0:T(8,128)S(1)} %get-tuple-element.69.rest_1_.cos_ref, f32[512,128]{1,0:T(8,128)S(1)} %copy-done.10, ...), custom_call_target="tpu_custom_call" | custom-call | flops 1 | bytes 1 | tf_op jit(solution)/shard_map/pallas_call | solution.py:388
  102.2 6.2 %collective-permute-done.15.refs_8_.refs_3_ = bf16[256,1024]{1,0:T(8,128)(2,1)} collective-permute-done((bf16[256,1024]{1,0:T(8,128)(2,1)}, bf16[256,1024]{1,0:T(8,128)(2,1)}, u32[]{:S(2)}, u32[]{:S(2)}) %collective-permute-start.15) | collective-permute-done | bytes 524320 | tf_op jit(solution)/shard_map/ppermute | solution.py:564
  108.5 3.6 %shard_map.111 = bf16[256,4096]{1,0:T(8,128)(2,1)S(1)} custom-call(bf16[512,768]{1,0:T(8,128)(2,1)S(1)} %get-tuple-element.36.refs_0_.refs_5_, bf16[1024,768]{1,0:T(8,128)(2,1)S(1)} %shard_map.102.rest_0_.refs_6_.refs_1_, bf16[1024,768]{1,0:T(8,128)(2,1)} %collective-permute-done.5.refs_1_.refs_7_.refs_2_, bf16[512,768]{1,0:T(8,128)(2,1)S(1)} %copy-done.3, ...), custom_call_target="tpu_custom_call" | custom-call | flops 1 | bytes 1 | tf_op jit(solution)/shard_map/pallas_call | solution.py:437
  112.2 3.6 %shard_map.110.a_ref = bf16[256,4096]{1,0:T(8,128)(2,1)S(1)} custom-call(bf16[512,768]{1,0:T(8,128)(2,1)S(1)} %get-tuple-element.36.refs_0_.refs_5_, bf16[1024,768]{1,0:T(8,128)(2,1)S(1)} %shard_map.102.rest_0_.refs_6_.refs_1_, bf16[1024,768]{1,0:T(8,128)(2,1)} %collective-permute-done.5.refs_1_.refs_7_.refs_2_, bf16[512,768]{1,0:T(8,128)(2,1)S(1)} %copy-done.3, ...), custom_call_target="tpu_custom_call" | custom-call | flops 1 | bytes 1 | tf_op jit(solution)/shard_map/pallas_call | solution.py:437
  117.4 4.1 %collective-permute-start.18 = (bf16[64,4096]{1,0:T(8,128)(2,1)S(1)}, bf16[64,4096]{1,0:T(8,128)(2,1)S(1)}, u32[]{:S(2)}, u32[]{:S(2)}) collective-permute-start(bf16[64,4096]{1,0:T(8,128)(2,1)S(1)} %get-tuple-element.42), channel_id=1, source_target_pairs={{0,24},{4,28},{8,0},{12,4},{16,8},{20,12},{24,16},{28,20},{1,25},{... | collective-permute-start | bytes 1572872 | tf_op jit(solution)/shard_map/ppermute | solution.py:571
  124.9 19.7 %collective-permute-done.17.up_ref = bf16[64,4096]{1,0:T(8,128)(2,1)S(1)} collective-permute-done((bf16[64,4096]{1,0:T(8,128)(2,1)S(1)}, bf16[64,4096]{1,0:T(8,128)(2,1)S(1)}, u32[]{:S(2)}, u32[]{:S(2)}) %collective-permute-start.17) | collective-permute-done | bytes 524320 | tf_op jit(solution)/shard_map/ppermute | solution.py:571
  146.8 4.1 %collective-permute-start.20 = (bf16[32,4096]{1,0:T(8,128)(2,1)S(1)}, bf16[32,4096]{1,0:T(8,128)(2,1)S(1)}, u32[]{:S(2)}, u32[]{:S(2)}) collective-permute-start(bf16[32,4096]{1,0:T(8,128)(2,1)S(1)} %get-tuple-element.46), channel_id=1, source_target_pairs={{0,24},{4,28},{8,0},{12,4},{16,8},{20,12},{24,16},{28,20},{1,25},{... | collective-permute-start | bytes 786440 | tf_op jit(solution)/shard_map/ppermute | solution.py:571
  150.9 4.1 %shard_map.113 = bf16[512,4,128]{2,1,0:T(4,128)(2,1)} custom-call(s32[8]{0:T(128)S(1)} %get-tuple-element.63.place_ref, bf16[512,512]{1,0:T(8,128)(2,1)S(1)} %get-tuple-element.35.in_ref, bf16[64,4096]{1,0:T(8,128)(2,1)S(1)} %get-tuple-element.40.after_ref.kept_ref.refs_10_), custom_call_target="tpu_custom_call" | custom-call | flops 1 | bytes 1 | tf_op jit(solution)/shard_map/pallas_call | solution.py:213
  155.0 4.2 %collective-permute-done.26.refs_8_.refs_9_ = bf16[512,768]{1,0:T(8,128)(2,1)S(1)} collective-permute-done((bf16[512,768]{1,0:T(8,128)(2,1)S(1)}, bf16[512,768]{1,0:T(8,128)(2,1)S(1)}, u32[]{:S(2)}, u32[]{:S(2)}) %collective-permute-start.26) | collective-permute-done | bytes 786464 | tf_op jit(solution)/shard_map/ppermute | solution.py:564
  160.3 4.6 %shard_map.116.refs_4_ = f32[1024,768]{1,0:T(8,128)S(1)} custom-call(bf16[512,1024]{1,0:T(8,128)(2,1)S(1)} %get-tuple-element.47.refs_0_, bf16[256,1024]{1,0:T(8,128)(2,1)} %collective-permute-done.13.refs_6_.refs_1_, bf16[256,1024]{1,0:T(8,128)(2,1)S(1)} %collective-permute-done.23.refs_2_, bf16[256,1024]{1,0:T(8,128)(2,1)} %collective-permute-done.15.refs_8_.refs_3_, ...), custom_call_target="tpu_custom_call" | custom-call | flops 1 | bytes 1 | tf_op jit(solution)/shard_map/pallas_call | solution.py:519
  164.9 3.1 %shard_map.117 = (bf16[1024,512]{1,0:T(8,128)(2,1)S(1)}, bf16[1024,256]{1,0:T(8,128)(2,1)S(1)}) custom-call(bf16[256,1024]{1,0:T(8,128)(2,1)} %collective-permute-done.14.refs_7_.refs_0_, bf16[256,1024]{1,0:T(8,128)(2,1)S(1)} %collective-permute-done.21.refs_1_, bf16[512,768]{1,0:T(8,128)(2,1)S(1)} %collective-permute-done.22.refs_2_.refs_3_, ...), custom_call_target="tpu_custom_call" | custom-call | flops 1 | bytes 1 | tf_op jit(solution)/shard_map/pallas_call | solution.py:519
  168.0 3.6 %collective-permute-start.27 = (bf16[1024,512]{1,0:T(8,128)(2,1)S(1)}, bf16[1024,512]{1,0:T(8,128)(2,1)S(1)}, u32[]{:S(2)}, u32[]{:S(2)}) collective-permute-start(bf16[1024,512]{1,0:T(8,128)(2,1)S(1)} %get-tuple-element.48.q_ref), channel_id=1, source_target_pairs={{0,224},{32,192},{64,160},{96,128},{128,96},{160,64},{192,32},{224... | collective-permute-start | bytes 3145736 | tf_op jit(solution)/shard_map/ppermute | solution.py:691
  173.8 28.0 %collective-permute-done.28.kv_far_ref = bf16[1024,256]{1,0:T(8,128)(2,1)S(1)} collective-permute-done((bf16[1024,256]{1,0:T(8,128)(2,1)S(1)}, bf16[1024,256]{1,0:T(8,128)(2,1)S(1)}, u32[]{:S(2)}, u32[]{:S(2)}) %collective-permute-start.28) | collective-permute-done | bytes 524320 | tf_op jit(solution)/shard_map/ppermute | solution.py:692
  202.9 3.0 %shard_map.118 = (f32[1024,4,128]{2,1,0:T(4,128)}, f32[1024,2,128]{2,1,0:T(2,128)}) custom-call(bf16[1024,512]{1,0:T(8,128)(2,1)S(1)} %get-tuple-element.48.q_ref, bf16[1024,512]{1,0:T(8,128)(2,1)S(1)} %collective-permute-done.27.q_far_ref, bf16[1024,256]{1,0:T(8,128)(2,1)S(1)} %get-tuple-element.49.kv_ref, ...), custom_call_target="tpu_custom_call" | custom-call | flops 1 | bytes 1 | tf_op jit(solution)/shard_map/pallas_call | solution.py:547
  (116 shorter events, 42.5 us)
Async XLA Ops:
  0.6 21.0 %collective-permute-start = (bf16[64,4096]{1,0:T(8,128)(2,1)}, bf16[64,4096]{1,0:T(8,128)(2,1)}, u32[]{:S(2)}, u32[]{:S(2)}) collective-permute-start(bf16[64,4096]{1,0:T(8,128)(2,1)} %bitcast.30), channel_id=1, source_target_pairs={{0,32},{32,64},{64,96},{96,128},{128,160},{160,192},{192,224},{1,3... | collective-permute-start | bytes 1572872 | tf_op jit(solution)/shard_map/ppermute | solution.py:601
  5.0 16.7 %collective-permute-start.1 = (bf16[64,4096]{1,0:T(8,128)(2,1)}, bf16[64,4096]{1,0:T(8,128)(2,1)}, u32[]{:S(2)}, u32[]{:S(2)}) collective-permute-start(bf16[64,4096]{1,0:T(8,128)(2,1)} %bitcast.31), channel_id=1, source_target_pairs={{32,0},{64,32},{96,64},{128,96},{160,128},{192,160},{224,192},{33,... | collective-permute-start | bytes 1572872 | tf_op jit(solution)/shard_map/ppermute | solution.py:602
  11.4 35.9 %collective-permute-start.4 = (bf16[1024,768]{1,0:T(8,128)(2,1)S(1)}, bf16[1024,768]{1,0:T(8,128)(2,1)S(1)}, u32[]{:S(2)}, u32[]{:S(2)}) collective-permute-start(bf16[1024,768]{1,0:T(8,128)(2,1)S(1)} %shard_map.102.rest_0_.refs_6_.refs_1_), channel_id=1, source_target_pairs={{0,1},{1,2},{2,3},{3,0},{4,5},{5,6},{6,7},{7,4},{8,9},{9,10},{10,1... | collective-permute-start | bytes 4718600 | tf_op jit(solution)/shard_map/ppermute | solution.py:564
  11.7 37.0 %collective-permute-start.5 = (bf16[1024,768]{1,0:T(8,128)(2,1)S(1)}, bf16[1024,768]{1,0:T(8,128)(2,1)}, u32[]{:S(2)}, u32[]{:S(2)}) collective-permute-start(bf16[1024,768]{1,0:T(8,128)(2,1)S(1)} %shard_map.102.rest_0_.refs_6_.refs_1_), channel_id=1, source_target_pairs={{0,3},{1,0},{2,1},{3,2},{4,7},{5,4},{6,5},{7,6},{8,11},{9,8},{10,9... | collective-permute-start | bytes 4718600 | tf_op jit(solution)/shard_map/ppermute | solution.py:564
  24.7 29.4 %collective-permute-start.2 = (bf16[64,4096]{1,0:T(8,128)(2,1)S(1)}, bf16[64,4096]{1,0:T(8,128)(2,1)S(1)}, u32[]{:S(2)}, u32[]{:S(2)}) collective-permute-start(bf16[64,4096]{1,0:T(8,128)(2,1)S(1)} %shard_map.104.refs_0_), channel_id=1, source_target_pairs={{0,24},{4,28},{8,0},{12,4},{16,8},{20,12},{24,16},{28,20},{1,25},{... | collective-permute-start | bytes 1572872 | tf_op jit(solution)/shard_map/ppermute | solution.py:571
  31.1 27.4 %collective-permute-start.3 = (bf16[64,4096]{1,0:T(8,128)(2,1)S(1)}, bf16[64,4096]{1,0:T(8,128)(2,1)S(1)}, u32[]{:S(2)}, u32[]{:S(2)}) collective-permute-start(bf16[64,4096]{1,0:T(8,128)(2,1)S(1)} %shard_map.104.refs_0_), channel_id=1, source_target_pairs={{0,8},{4,12},{8,16},{12,20},{16,24},{20,28},{24,0},{28,4},{1,9},{5... | collective-permute-start | bytes 1572872 | tf_op jit(solution)/shard_map/ppermute | solution.py:571
  50.0 27.0 %collective-permute-start.10 = (bf16[512,768]{1,0:T(8,128)(2,1)S(1)}, bf16[512,768]{1,0:T(8,128)(2,1)S(1)}, u32[]{:S(2)}, u32[]{:S(2)}) collective-permute-start(bf16[512,768]{1,0:T(8,128)(2,1)S(1)} %get-tuple-element.32), channel_id=1, source_target_pairs={{0,3},{1,0},{2,1},{3,2},{4,7},{5,4},{6,5},{7,6},{8,11},{9,8},{10,9... | collective-permute-start | bytes 2359304 | tf_op jit(solution)/shard_map/ppermute | solution.py:564
  50.5 26.5 %collective-permute-start.9 = (bf16[512,768]{1,0:T(8,128)(2,1)S(1)}, bf16[512,768]{1,0:T(8,128)(2,1)S(1)}, u32[]{:S(2)}, u32[]{:S(2)}) collective-permute-start(bf16[512,768]{1,0:T(8,128)(2,1)S(1)} %get-tuple-element.28.refs_2_), channel_id=1, source_target_pairs={{0,1},{1,2},{2,3},{3,0},{4,5},{5,6},{6,7},{7,4},{8,9},{9,10},{10,1... | collective-permute-start | bytes 2359304 | tf_op jit(solution)/shard_map/ppermute | solution.py:564
  59.5 24.4 %collective-permute-start.11 = (bf16[128,4096]{1,0:T(8,128)(2,1)}, bf16[128,4096]{1,0:T(8,128)(2,1)}, u32[]{:S(2)}, u32[]{:S(2)}) collective-permute-start(bf16[128,4096]{1,0:T(8,128)(2,1)} %get-tuple-element.29.refs_1_), channel_id=1, source_target_pairs={{0,4},{4,0},{8,12},{12,8},{16,20},{20,16},{24,28},{28,24},{1,5},{5... | collective-permute-start | bytes 3145736 | tf_op jit(solution)/shard_map/ppermute | solution.py:575
  59.6 15.3 %collective-permute-start.7 = (bf16[32,4096]{1,0:T(8,128)(2,1)S(1)}, bf16[32,4096]{1,0:T(8,128)(2,1)S(1)}, u32[]{:S(2)}, u32[]{:S(2)}) collective-permute-start(bf16[32,4096]{1,0:T(8,128)(2,1)S(1)} %get-tuple-element.30), channel_id=1, source_target_pairs={{0,24},{4,28},{8,0},{12,4},{16,8},{20,12},{24,16},{28,20},{1,25},{... | collective-permute-start | bytes 786440 | tf_op jit(solution)/shard_map/ppermute | solution.py:571
  60.8 16.1 %collective-permute-start.8 = (bf16[32,4096]{1,0:T(8,128)(2,1)S(1)}, bf16[32,4096]{1,0:T(8,128)(2,1)S(1)}, u32[]{:S(2)}, u32[]{:S(2)}) collective-permute-start(bf16[32,4096]{1,0:T(8,128)(2,1)S(1)} %get-tuple-element.31), channel_id=1, source_target_pairs={{0,8},{4,12},{8,16},{12,20},{16,24},{20,28},{24,0},{28,4},{1,9},{5... | collective-permute-start | bytes 786440 | tf_op jit(solution)/shard_map/ppermute | solution.py:571
  80.8 21.4 %collective-permute-start.13 = (bf16[256,1024]{1,0:T(8,128)(2,1)}, bf16[256,1024]{1,0:T(8,128)(2,1)}, u32[]{:S(2)}, u32[]{:S(2)}) collective-permute-start(bf16[256,1024]{1,0:T(8,128)(2,1)} %get-tuple-element.37), channel_id=1, source_target_pairs={{0,1},{1,2},{2,3},{3,0},{4,5},{5,6},{6,7},{7,4},{8,9},{9,10},{10,1... | collective-permute-start | bytes 1572872 | tf_op jit(solution)/shard_map/ppermute | solution.py:564
  81.4 20.9 %collective-permute-start.14 = (bf16[256,1024]{1,0:T(8,128)(2,1)}, bf16[256,1024]{1,0:T(8,128)(2,1)}, u32[]{:S(2)}, u32[]{:S(2)}) collective-permute-start(bf16[256,1024]{1,0:T(8,128)(2,1)} %get-tuple-element.38), channel_id=1, source_target_pairs={{0,2},{1,3},{2,0},{3,1},{4,6},{5,7},{6,4},{7,5},{8,10},{9,11},{10,... | collective-permute-start | bytes 1572872 | tf_op jit(solution)/shard_map/ppermute | solution.py:564
  82.7 25.7 %collective-permute-start.15 = (bf16[256,1024]{1,0:T(8,128)(2,1)}, bf16[256,1024]{1,0:T(8,128)(2,1)}, u32[]{:S(2)}, u32[]{:S(2)}) collective-permute-start(bf16[256,1024]{1,0:T(8,128)(2,1)} %get-tuple-element.39), channel_id=1, source_target_pairs={{0,3},{1,0},{2,1},{3,2},{4,7},{5,4},{6,5},{7,6},{8,11},{9,8},{10,9... | collective-permute-start | bytes 1572872 | tf_op jit(solution)/shard_map/ppermute | solution.py:564
  117.3 27.4 %collective-permute-start.17 = (bf16[64,4096]{1,0:T(8,128)(2,1)S(1)}, bf16[64,4096]{1,0:T(8,128)(2,1)S(1)}, u32[]{:S(2)}, u32[]{:S(2)}) collective-permute-start(bf16[64,4096]{1,0:T(8,128)(2,1)S(1)} %get-tuple-element.41), channel_id=1, source_target_pairs={{0,8},{4,12},{8,16},{12,20},{16,24},{20,28},{24,0},{28,4},{1,9},{5... | collective-permute-start | bytes 1572872 | tf_op jit(solution)/shard_map/ppermute | solution.py:571
  117.4 27.3 %collective-permute-start.18 = (bf16[64,4096]{1,0:T(8,128)(2,1)S(1)}, bf16[64,4096]{1,0:T(8,128)(2,1)S(1)}, u32[]{:S(2)}, u32[]{:S(2)}) collective-permute-start(bf16[64,4096]{1,0:T(8,128)(2,1)S(1)} %get-tuple-element.42), channel_id=1, source_target_pairs={{0,24},{4,28},{8,0},{12,4},{16,8},{20,12},{24,16},{28,20},{1,25},{... | collective-permute-start | bytes 1572872 | tf_op jit(solution)/shard_map/ppermute | solution.py:571
  121.5 25.3 %collective-permute-start.25 = (bf16[512,768]{1,0:T(8,128)(2,1)S(1)}, bf16[512,768]{1,0:T(8,128)(2,1)S(1)}, u32[]{:S(2)}, u32[]{:S(2)}) collective-permute-start(bf16[512,768]{1,0:T(8,128)(2,1)S(1)} %get-tuple-element.36.refs_0_.refs_5_), channel_id=1, source_target_pairs={{0,1},{1,2},{2,3},{3,0},{4,5},{5,6},{6,7},{7,4},{8,9},{9,10},{10,1... | collective-permute-start | bytes 2359304 | tf_op jit(solution)/shard_map/ppermute | solution.py:564
  122.5 36.8 %collective-permute-start.26 = (bf16[512,768]{1,0:T(8,128)(2,1)S(1)}, bf16[512,768]{1,0:T(8,128)(2,1)S(1)}, u32[]{:S(2)}, u32[]{:S(2)}) collective-permute-start(bf16[512,768]{1,0:T(8,128)(2,1)S(1)} %get-tuple-element.36.refs_0_.refs_5_), channel_id=1, source_target_pairs={{0,3},{1,0},{2,1},{3,2},{4,7},{5,4},{6,5},{7,6},{8,11},{9,8},{10,9... | collective-permute-start | bytes 2359304 | tf_op jit(solution)/shard_map/ppermute | solution.py:564
  123.6 41.3 %collective-permute-start.22 = (bf16[512,768]{1,0:T(8,128)(2,1)S(1)}, bf16[512,768]{1,0:T(8,128)(2,1)S(1)}, u32[]{:S(2)}, u32[]{:S(2)}) collective-permute-start(bf16[512,768]{1,0:T(8,128)(2,1)S(1)} %get-tuple-element.36.refs_0_.refs_5_), channel_id=1, source_target_pairs={{0,2},{1,3},{2,0},{3,1},{4,6},{5,7},{6,4},{7,5},{8,10},{9,11},{10,... | collective-permute-start | bytes 2359304 | tf_op jit(solution)/shard_map/ppermute | solution.py:564
  144.7 20.2 %collective-permute-start.21 = (bf16[256,1024]{1,0:T(8,128)(2,1)}, bf16[256,1024]{1,0:T(8,128)(2,1)S(1)}, u32[]{:S(2)}, u32[]{:S(2)}) collective-permute-start(bf16[256,1024]{1,0:T(8,128)(2,1)} %collective-permute-done.14.refs_7_.refs_0_), channel_id=1, source_target_pairs={{0,4},{4,0},{8,12},{12,8},{16,20},{20,16},{24,28},{28,24},{1,5},{5... | collective-permute-start | bytes 1572872 | tf_op jit(solution)/shard_map/ppermute | solution.py:575
  146.8 25.4 %collective-permute-start.19 = (bf16[32,4096]{1,0:T(8,128)(2,1)S(1)}, bf16[32,4096]{1,0:T(8,128)(2,1)S(1)}, u32[]{:S(2)}, u32[]{:S(2)}) collective-permute-start(bf16[32,4096]{1,0:T(8,128)(2,1)S(1)} %get-tuple-element.45.refs_5_), channel_id=1, source_target_pairs={{0,8},{4,12},{8,16},{12,20},{16,24},{20,28},{24,0},{28,4},{1,9},{5... | collective-permute-start | bytes 786440 | tf_op jit(solution)/shard_map/ppermute | solution.py:571
  146.8 25.4 %collective-permute-start.20 = (bf16[32,4096]{1,0:T(8,128)(2,1)S(1)}, bf16[32,4096]{1,0:T(8,128)(2,1)S(1)}, u32[]{:S(2)}, u32[]{:S(2)}) collective-permute-start(bf16[32,4096]{1,0:T(8,128)(2,1)S(1)} %get-tuple-element.46), channel_id=1, source_target_pairs={{0,24},{4,28},{8,0},{12,4},{16,8},{20,12},{24,16},{28,20},{1,25},{... | collective-permute-start | bytes 786440 | tf_op jit(solution)/shard_map/ppermute | solution.py:571
  168.0 33.9 %collective-permute-start.27 = (bf16[1024,512]{1,0:T(8,128)(2,1)S(1)}, bf16[1024,512]{1,0:T(8,128)(2,1)S(1)}, u32[]{:S(2)}, u32[]{:S(2)}) collective-permute-start(bf16[1024,512]{1,0:T(8,128)(2,1)S(1)} %get-tuple-element.48.q_ref), channel_id=1, source_target_pairs={{0,224},{32,192},{64,160},{96,128},{128,96},{160,64},{192,32},{224... | collective-permute-start | bytes 3145736 | tf_op jit(solution)/shard_map/ppermute | solution.py:691
  171.6 30.2 %collective-permute-start.28 = (bf16[1024,256]{1,0:T(8,128)(2,1)S(1)}, bf16[1024,256]{1,0:T(8,128)(2,1)S(1)}, u32[]{:S(2)}, u32[]{:S(2)}) collective-permute-start(bf16[1024,256]{1,0:T(8,128)(2,1)S(1)} %get-tuple-element.49.kv_ref), channel_id=1, source_target_pairs={{0,224},{32,192},{64,160},{96,128},{128,96},{160,64},{192,32},{224... | collective-permute-start | bytes 1572872 | tf_op jit(solution)/shard_map/ppermute | solution.py:692
  (27 other events, 166.8 us)

commit v2 on v1

--- a/solution.py
+++ b/solution.py
@@ -11,6 +11,7 @@
 BF = jnp.bfloat16
 F32 = jnp.float32
 GROUP = 128
+TOKEN = jax.ShapeDtypeStruct((8, 128), jnp.float32)
 LIGHT = pl.CostEstimate(flops=1, bytes_accessed=1, transcendentals=0)
 VM = pl.BlockSpec(memory_space=pltpu.VMEM)
 
@@ -119,9 +120,8 @@
     return copied([first, second], specs, after, moves, shapes)
 
 
-def pack(tokens, cols, joined, after):
+def pack_near(tokens, cols, rows):
     count = tokens[0].shape[1] // cols - 1
-    rows = sum(t.shape[0] for t in tokens)
     moves = []
     for block in range(count):
         row = 0
@@ -130,14 +130,51 @@
             take = (slice(0, size), slice((block + 1) * cols, (block + 2) * cols))
             moves.append((n, take, block, (slice(row, row + size), slice(0, cols))))
             row += size
-    row, model = 0, tokens[0].shape[1]
-    for n in range(len(tokens) - joined, len(tokens)):
-        size = tokens[n].shape[0]
+    specs = [whole(t.shape) for t in tokens]
+    return copied(tokens, specs, [], moves, [(rows, cols)] * count)
+
+
+def pack_kernel(moves, parts, blocks, *refs):
+    tokens, outs, sems = refs[:parts], refs[-2 - blocks : -1], refs[-1]
+    copies = []
+    for n, (source, take, target, put) in enumerate(moves):
+        copies.append(
+            pltpu.make_async_copy(tokens[source].at[take], outs[target].at[put], sems.at[n])
+        )
+    for copy in copies:
+        copy.start()
+    for copy in copies:
+        copy.wait()
+
+
+def pack_rest(tokens, blocks, after):
+    rows, cols = blocks[0].shape
+    count = len(blocks)
+    model = tokens[0].shape[1]
+    total = sum(t.shape[0] for t in tokens)
+    moves, row = [], 0
+    for n, part in enumerate(tokens):
+        size = part.shape[0]
+        for block in range(count):
+            take = (slice(0, size), slice((block + 1) * cols, (block + 2) * cols))
+            put = (slice(rows - total + row, rows - total + row + size), slice(0, cols))
+            moves.append((n, take, block, put))
         every = (slice(0, size), slice(0, model))
         moves.append((n, every, count, (slice(row, row + size), slice(0, model))))
         row += size
-    specs = [whole(t.shape) for t in tokens]
-    return copied(tokens, specs, after, moves, [(rows, cols)] * count + [(row, model)])
+    anywhere = pl.BlockSpec(memory_space=pl.ANY)
+    return pl.pallas_call(
+        functools.partial(pack_kernel, moves, len(tokens), count),
+        grid=(1,),
+        in_specs=[whole(t.shape) for t in tokens] + [anywhere] * (count + len(after)),
+        out_specs=[anywhere] * (count + 1),
+        out_shape=[jax.ShapeDtypeStruct((rows, cols), BF)] * count
+        + [jax.ShapeDtypeStruct((total, model), BF)],
+        input_output_aliases={len(tokens) + i: i for i in range(count)},
+        scratch_shapes=[pltpu.SemaphoreType.DMA((len(moves),))],
+        compiler_params=pltpu.CompilerParams(vmem_limit_bytes=8 * 2**20),
+        cost_estimate=LIGHT,
+    )(*tokens, *blocks, *after)
 
 
 def relay_kernel(place_ref, fresh_ref, below_ref, above_ref, *rest):
@@ -175,7 +212,8 @@
     )(place, fresh, below, above, *after)
 
 
-def gather_kernel(place_ref, in_ref, out_ref):
+def gather_kernel(place_ref, in_ref, out_ref, token_ref):
+    token_ref[...] = jnp.zeros_like(token_ref)
     width = in_ref.shape[2]
     for i in range(in_ref.shape[1]):
         out_ref[:, i * width : (i + 1) * width] = in_ref[:, i, :]
@@ -191,15 +229,19 @@
             num_scalar_prefetch=1,
             grid=(count,),
             in_specs=[pl.BlockSpec((tile, heads, width), lambda i, s: (s[i], 0, 0))],
-            out_specs=pl.BlockSpec((tile, heads * width), lambda i, s: (i, 0)),
+            out_specs=[
+                pl.BlockSpec((tile, heads * width), lambda i, s: (i, 0)),
+                whole(TOKEN.shape),
+            ],
         ),
-        out_shape=jax.ShapeDtypeStruct((rows, heads * width), value.dtype),
+        out_shape=[jax.ShapeDtypeStruct((rows, heads * width), value.dtype), TOKEN],
         compiler_params=pltpu.CompilerParams(vmem_limit_bytes=4 * 2**20),
         cost_estimate=LIGHT,
     )(place, value)
 
 
-def scatter_kernel(place_ref, in_ref, after_ref, out_ref):
+def scatter_kernel(place_ref, in_ref, after_ref, out_ref, token_ref):
+    token_ref[...] = jnp.zeros_like(token_ref)
     width = out_ref.shape[2]
     for i in range(out_ref.shape[1]):
         out_ref[:, i, :] = in_ref[:, i * width : (i + 1) * width]
@@ -219,9 +261,12 @@
                 pl.BlockSpec((tile, cols), lambda i, s: (i, 0)),
                 pl.BlockSpec(memory_space=pl.ANY),
             ],
-            out_specs=pl.BlockSpec((tile, heads, width), lambda i, s: (s[i], 0, 0)),
+            out_specs=[
+                pl.BlockSpec((tile, heads, width), lambda i, s: (s[i], 0, 0)),
+                whole(TOKEN.shape),
+            ],
         ),
-        out_shape=jax.ShapeDtypeStruct((rows, heads, width), value.dtype),
+        out_shape=[jax.ShapeDtypeStruct((rows, heads, width), value.dtype), TOKEN],
         compiler_params=pltpu.CompilerParams(vmem_limit_bytes=4 * 2**20),
         cost_estimate=LIGHT,
     )(place, value, after)
@@ -235,26 +280,34 @@
     return jax.ShapeDtypeStruct((value.shape[0] // 2, value.shape[1]), value.dtype)
 
 
-def second_step_kernel(up_ref, down_ref, next_ref, prev_ref, up_out, down_out):
+def second_step_kernel(up_ref, down_ref, next_ref, prev_ref, *rest):
+    up_out, down_out, token_ref = rest[-3:]
+    token_ref[...] = jnp.zeros_like(token_ref)
     up_out[...] = (up_ref[...].astype(F32) + next_ref[...].astype(F32)).astype(BF)
     down_out[...] = (down_ref[...].astype(F32) + prev_ref[...].astype(F32)).astype(BF)
 
 
-def second_step(up, down, next_top, prev_bot):
-    outs = [half_of(up), half_of(down)]
+def second_step(up, down, next_top, prev_bot, after):
+    outs = [half_of(up), half_of(down), TOKEN]
     return pl.pallas_call(
         second_step_kernel,
         grid=(1,),
         in_specs=[first_half(up), first_half(down)]
-        + [whole(next_top.shape), whole(prev_bot.shape)],
+        + [whole(next_top.shape), whole(prev_bot.shape)]
+        + [pl.BlockSpec(memory_space=pl.ANY)] * len(after),
         out_specs=[whole(o.shape) for o in outs],
         out_shape=outs,
         compiler_params=pltpu.CompilerParams(vmem_limit_bytes=4 * 2**20),
-        cost_estimate=LIGHT,
-    )(up, down, next_top, prev_bot)
-
-
-def input_grad_kernel(shift_ref, kept_ref, up_ref, down_ref, up2_ref, down2_ref, out_ref):
+        cost_estimate=pl.CostEstimate(
+            flops=8 * 10**9, bytes_accessed=1, transcendentals=0
+        ),
+    )(up, down, next_top, prev_bot, *after)
+
+
+def input_grad_kernel(
+    shift_ref, kept_ref, up_ref, down_ref, up2_ref, down2_ref, out_ref, token_ref
+):
+    token_ref[...] = jnp.zeros_like(token_ref)
     half = up2_ref.shape[0]
     total = kept_ref[...].astype(F32)
     bottom = total[half:] + up_ref[...].astype(F32) + down2_ref[...].astype(F32)
@@ -279,9 +332,12 @@
                 part(rows // 2, 0),
                 part(rows // 2, 0),
             ],
-            out_specs=pl.BlockSpec((rows, tile), lambda j, s: (0, (j + s[0]) % replicas)),
+            out_specs=[
+                pl.BlockSpec((rows, tile), lambda j, s: (0, (j + s[0]) % replicas)),
+                whole(TOKEN.shape),
+            ],
         ),
-        out_shape=jax.ShapeDtypeStruct((rows, model), BF),
+        out_shape=[jax.ShapeDtypeStruct((rows, model), BF), TOKEN],
         compiler_params=pltpu.CompilerParams(vmem_limit_bytes=4 * 2**20),
         cost_estimate=pl.CostEstimate(
             flops=40 * 10**9, bytes_accessed=160 * 2**20, transcendentals=0
@@ -448,7 +504,9 @@
     )(grads, *weights, *after)
 
 
-def chip_sum_kernel(cuts, a_ref, b_ref, *outs):
+def chip_sum_kernel(cuts, a_ref, b_ref, *rest):
+    outs = rest[-1 - len(cuts) : -1]
+    rest[-1][...] = jnp.zeros_like(rest[-1])
     for out, ranges in zip(outs, cuts):
         row = 0
         for low, high in ranges:
@@ -457,7 +515,7 @@
             row += high - low
 
 
-def chip_sum(a, b, cuts):
+def chip_sum(a, b, cuts, after):
     rows, model = a.shape
     tile = model // 4
     sizes = [sum(high - low for low, high in ranges) for ranges in cuts]
@@ -465,23 +523,24 @@
     return pl.pallas_call(
         functools.partial(chip_sum_kernel, cuts),
         grid=(model // tile,),
-        in_specs=[block(rows)] * 2,
-        out_specs=[block(size) for size in sizes],
-        out_shape=[jax.ShapeDtypeStruct((size, model), BF) for size in sizes],
+        in_specs=[block(rows)] * 2 + [pl.BlockSpec(memory_space=pl.ANY)] * len(after),
+        out_specs=[block(size) for size in sizes] + [whole(TOKEN.shape)],
+        out_shape=[jax.ShapeDtypeStruct((size, model), BF) for size in sizes] + [TOKEN],
         compiler_params=pltpu.CompilerParams(vmem_limit_bytes=6 * 2**20),
         cost_estimate=LIGHT,
-    )(a, b)
+    )(a, b, *after)
 
 
 def weight_grad_kernel(count, first, *refs):
     tokens, grads, rest = refs[:count], refs[count : 2 * count], refs[2 * count :]
-    rest = rest[-1:] if first else rest[:1] + rest[-2:]
+    rest = rest[-2:] if first else rest[:1] + rest[-2:]
     total = None if first else rest[0][...]
     for x, d in zip(tokens, grads):
         term = dot(x[...], d[...], ((0,), (0,)))
         total = term if total is None else total + term
     if first:
         rest[0][...] = total
+        rest[1][...] = jnp.zeros_like(rest[1])
     else:
         q_ref, kv_ref = rest[1:]
         q_cols = q_ref.shape[1]
@@ -505,8 +564,8 @@
     if sums is None:
         operands = tuple(after)
         in_specs += [pl.BlockSpec(memory_space=pl.ANY)] * len(after)
-        out_specs = block(cols)
-        out_shape = jax.ShapeDtypeStruct((d_rows, cols), F32)
+        out_specs = [block(cols), whole(TOKEN.shape)]
+        out_shape = [jax.ShapeDtypeStruct((d_rows, cols), F32), TOKEN]
     else:
         operands = (sums,) + tuple(after)
         in_specs.append(block(cols))
@@ -613,7 +672,7 @@
     order = (chip + order) % chips
     place = jnp.concatenate([order * 2 + core, order * 2 + 1 - core])
     pos = jnp.take(positions[0, 0].reshape(-1, piece), place, axis=0).reshape(-1)
-    cotangent = gather_rows(place, out_grad[0, 0])
+    cotangent, rows_set = gather_rows(place, out_grad[0, 0])
     angle_half = width // 2
     inv_freq = 1000000.0 ** (-jnp.arange(angle_half, dtype=F32) / angle_half)
     angles = pos.astype(F32)[:, None] * inv_freq[None, :]
@@ -626,7 +685,7 @@
         fresh,
         from_below,
         from_above,
-        [w_own, cos_t, sin_t, cotangent],
+        [w_own, cos_t, sin_t, rows_set],
     )
     prev = shifted_chips(own, 1)
     after = shifted_chips(own, -1)
@@ -639,9 +698,8 @@
     across_top = shifted_chips(next_top, -1)
     across_bot = shifted_chips(prev_bot, 1)
 
-    *blocks, across = pack(
-        [own, beside, across_top, across_bot], d_rows, 2, [far_top, far_bot]
-    )
+    blocks = pack_near([own, beside], d_rows, near)
+    *blocks, across = pack_rest([across_top, across_bot], blocks, [far_top, far_bot])
     sent = [shifted(blocks[k - 1], "dp", k) for k in range(1, replicas)]
     token_parts = [own, beside, across]
     other_parts = [other_own, other_core(beside), other_core(across)]
@@ -656,7 +714,7 @@
     low = [i * piece for i in range(chips)]
     mid = [i * piece + half for i in range(chips)]
     high = [(i + 1) * piece for i in range(chips)]
-    kept, up, next_top, down, prev_bot = chip_sum(
+    kept, up, next_top, down, prev_bot, chip_set = chip_sum(
         own_part,
         other_part,
         [
@@ -666,32 +724,41 @@
             [(mid[3], high[3]), (low[2], mid[2])],
             [(mid[2], high[2])],
         ],
+        [],
     )
     up = shifted_chips(up, 1)
     down = shifted_chips(down, -1)
 
-    up2_part, down2_part = second_step(up, down, next_top, prev_bot)
+    d_before = shifted(d_own, "dp", 1)
+    d_after = shifted(d_own, "dp", -1)
+    before_top, after_bot = halves(
+        d_before, d_after, [chip_set] + sent_other, False
+    )
+    d_far_top = shifted(before_top, "dp", 1)
+    d_far_bot = shifted(after_bot, "dp", -1)
+    attn_out, out_set = scatter_rows(place, attended, width, chip_set)
+    attn_out = attn_out[None, None]
+    sums, sums_set = weight_grad(
+        [x_own, sent[0], sent_other[0], sent[2], sent_other[2]],
+        [(d_own, None), (d_before, 0), (d_before, 1), (d_after, 0), (d_after, 1)],
+        None,
+        q_cols,
+        [chip_set, out_set],
+    )
+    up2_part, down2_part, step_set = second_step(
+        up, down, next_top, prev_bot, [sums_set, out_set]
+    )
     up2 = shifted_chips(up2_part, 1)
     down2 = shifted_chips(down2_part, -1)
-    grad_input = input_grad(replica, replicas, kept, up, down, up2, down2)
-
-    d_sent = [shifted(d_own, "dp", k) for k in range(1, replicas)]
-    attn_out = scatter_rows(place, attended, width, kept)[None, None]
-    sums = weight_grad(
-        [x_own, sent[0], sent_other[0], sent[2], sent_other[2]],
-        [(d_own, None), (d_sent[0], 0), (d_sent[0], 1), (d_sent[2], 0), (d_sent[2], 1)],
-        None,
-        q_cols,
-        [kept, attn_out],
-    )
+    grad_input, input_set = input_grad(replica, replicas, kept, up, down, up2, down2)
     own_q, own_kv = weight_grad(
-        [sent[1], sent_other[1]], [(d_sent[1], 0), (d_sent[1], 1)], sums, q_cols, [up2_part]
+        [sent[1], sent_other[1]], [(d_far_top, None), (d_far_bot, None)], sums, q_cols, [step_set]
     )
     pairs = [(i, ends - i) for i in range(sections)]
     far_q = lax.ppermute(own_q, "pipe", pairs)
     far_kv = lax.ppermute(own_kv, "pipe", pairs)
     grad_query, grad_keyval = mirror_sum(
-        own_q, far_q, own_kv, far_kv, [grad_input], width
+        own_q, far_q, own_kv, far_kv, [input_set], width
     )
     return attn_out, grad_input[None, None], grad_query[None], grad_keyval[None, :, None]
 

time: 207 us -> 203 us (0.981)
  waiting for transfers between devices: 96.9 us -> 94.5 us
    ppermute x8, waiting for transfers between devices: 39.2 us -> 25.7 us  [shifted_chips(): return lax.ppermute(value, 'tensor', pairs)]
    ppermute x1, waiting for transfers between devices: 28 us -> 34.1 us  [on_device(): far_kv = lax.ppermute(own_kv, 'pipe', pairs)]
    ppermute x10 -> x11, waiting for transfers between devices: 28.1 us -> 31.6 us  [shifted(): lax.ppermute(value, axis, [(i, (i + step) % count) for i in range(count)])]
    unnamed x47 -> x41, local copies, waits for them, and re-layouts: 11.2 us -> 9.27 us
    ppermute x10 -> x11, starting transfers between devices: 10.9 us -> 11.6 us  [shifted(): lax.ppermute(value, axis, [(i, (i + step) % count) for i in range(count)])]
    pallas_call x3 -> x4, Pallas kernels: 5.27 us -> 4.97 us  [copied(): pl.pallas_call(functools.partial(copy_kernel, moves, count), grid=(1,), i...]
  transfers between devices with their start and end apart: 29 -> 30, of which waited for: 11 -> 13; matrix products, arithmetic and copies ran while one was open for 3% -> 3% of each run, Pallas kernels for 22% -> 23%
where the time goes in v2:
time: 203 us
  waiting for transfers between devices  94.5 us (47%)
  Pallas kernels  52.5 us (26%)
  starting transfers between devices  40.2 us (20%)
  local copies, waits for them, and re-layouts  10.9 us (5%)
  other arithmetic  2.8 us (1%)
    ppermute x1, waiting for transfers between devices, on_device(): far_kv = lax.ppermute(own_kv, 'pipe', pairs)  34.1 us
    ppermute x11, waiting for transfers between devices, shifted(): lax.ppermute(value, axis, [(i, (i + step) % count) for i in range(count)])  31.6 us
    ppermute x8, waiting for transfers between devices, shifted_chips(): return lax.ppermute(value, 'tensor', pairs)  25.7 us
    ppermute x8, starting transfers between devices, shifted_chips(): return lax.ppermute(value, 'tensor', pairs)  17.8 us
    ppermute x11, starting transfers between devices, shifted(): lax.ppermute(value, axis, [(i, (i + step) % count) for i in range(count)])  11.6 us
    unnamed x41, local copies, waits for them, and re-layouts  9.27 us
    pallas_call x2, Pallas kernels, weight_grad(): pl.pallas_call(functools.partial(weight_grad_kernel, count, sums is None)...  7.67 us
    pallas_call x1, Pallas kernels, attention(): pl.pallas_call(attention_kernel, grid=(heads,), in_specs=[column, pl.Bloc...  7.46 us
  transfers between devices with their start and end apart: 30, of which 13 were waited for; matrix products, arithmetic and copies ran while one was open for 3% of the time, Pallas kernels for 23%

profile of v2, /device:TPU:24, one launch (start us, length us, event | category | flops | bytes accessed | tf_op | source)
XLA Modules:
  0.0 202.8 jit_solution(7802483412633799353)
XLA Ops:
  0.6 4.3 %collective-permute-start = (bf16[64,4096]{1,0:T(8,128)(2,1)}, bf16[64,4096]{1,0:T(8,128)(2,1)}, u32[]{:S(2)}, u32[]{:S(2)}) collective-permute-start(bf16[64,4096]{1,0:T(8,128)(2,1)} %bitcast.28), channel_id=1, source_target_pairs={{0,32},{32,64},{64,96},{96,128},{128,160},{160,192},{192,224},{1,3... | collective-permute-start | bytes 1572872 | tf_op jit(solution)/shard_map/ppermute | solution.py:660
  7.8 3.5 %shard_map.102.rest_0_.refs_6_.refs_1_ = bf16[1024,768]{1,0:T(8,128)(2,1)S(1)} custom-call(bf16[1024,512]{1,0:T(8,128)(2,1)S(1)} %bitcast.26, bf16[1024,256]{1,0:T(8,128)(2,1)S(1)} %bitcast.27), custom_call_target="tpu_custom_call" | custom-call | flops 1 | bytes 1 | tf_op jit(solution)/shard_map/pallas_call | solution.py:51
  21.7 2.8 %shard_map.104.refs_0_ = bf16[64,4096]{1,0:T(8,128)(2,1)S(1)} custom-call(s32[2]{0:T(128)S(1)} %pad_add_fusion.1.place_ref, bf16[64,4096]{1,0:T(8,128)(2,1)S(1)} %bitcast.30, bf16[64,4096]{1,0:T(8,128)(2,1)} %collective-permute-done.below_ref, bf16[64,4096]{1,0:T(8,128)(2,1)} %collective-permute-done.1.above_ref, ...), custom_call_target="tpu_custom_call" | custom-call | flops 1 | bytes 1 | tf_op jit(solution)/shard_map/pallas_call | solution.py:201
  24.6 6.4 %collective-permute-start.2 = (bf16[64,4096]{1,0:T(8,128)(2,1)S(1)}, bf16[64,4096]{1,0:T(8,128)(2,1)S(1)}, u32[]{:S(2)}, u32[]{:S(2)}) collective-permute-start(bf16[64,4096]{1,0:T(8,128)(2,1)S(1)} %shard_map.104.refs_0_), channel_id=1, source_target_pairs={{0,24},{4,28},{8,0},{12,4},{16,8},{20,12},{24,16},{28,20},{1,25},{... | collective-permute-start | bytes 1572872 | tf_op jit(solution)/shard_map/ppermute | solution.py:630
  31.0 16.2 %collective-permute-done.4.refs_0_.refs_10_.refs_5_ = bf16[1024,768]{1,0:T(8,128)(2,1)S(1)} collective-permute-done((bf16[1024,768]{1,0:T(8,128)(2,1)S(1)}, bf16[1024,768]{1,0:T(8,128)(2,1)S(1)}, u32[]{:S(2)}, u32[]{:S(2)}) %collective-permute-start.4) | collective-permute-done | bytes 1572896 | tf_op jit(solution)/shard_map/ppermute | solution.py:623
  54.0 4.3 %collective-permute-done.3.refs_1_ = bf16[64,4096]{1,0:T(8,128)(2,1)S(1)} collective-permute-done((bf16[64,4096]{1,0:T(8,128)(2,1)S(1)}, bf16[64,4096]{1,0:T(8,128)(2,1)S(1)}, u32[]{:S(2)}, u32[]{:S(2)}) %collective-permute-start.3) | collective-permute-done | bytes 524320 | tf_op jit(solution)/shard_map/ppermute | solution.py:630
  64.8 10.0 %collective-permute-done.7.refs_0_ = bf16[32,4096]{1,0:T(8,128)(2,1)S(1)} collective-permute-done((bf16[32,4096]{1,0:T(8,128)(2,1)S(1)}, bf16[32,4096]{1,0:T(8,128)(2,1)S(1)}, u32[]{:S(2)}, u32[]{:S(2)}) %collective-permute-start.7) | collective-permute-done | bytes 262176 | tf_op jit(solution)/shard_map/ppermute | solution.py:630
  86.4 6.5 %shard_map.109 = (bf16[512,768]{1,0:T(8,128)(2,1)S(1)}, bf16[512,1024]{1,0:T(8,128)(2,1)S(1)}) custom-call(bf16[64,4096]{1,0:T(8,128)(2,1)S(1)} %copy-done.5, bf16[128,4096]{1,0:T(8,128)(2,1)} %get-tuple-element.45.refs_1_, bf16[64,4096]{1,0:T(8,128)(2,1)} %get-tuple-element.52.refs_2_, bf16[64,4096]{1,0:T(8,128)(2,1)S(1)} %copy-done.9, ...), custom_call_target="tpu_custom_call" | custom-call | flops 1 | bytes 1 | tf_op jit(solution)/shard_map/pallas_call | solution.py:373
  92.9 7.5 %shard_map.110 = (bf16[512,512]{1,0:T(8,128)(2,1)S(1)}, bf16[512,768]{1,0:T(8,128)(2,1)S(1)}) custom-call(bf16[512,768]{1,0:T(8,128)(2,1)S(1)} %get-tuple-element.53.q_ref.kv_ref, bf16[512,768]{1,0:T(8,128)(2,1)S(1)} %get-tuple-element.53.q_ref.kv_ref, f32[512,128]{1,0:T(8,128)S(1)} %get-tuple-element.99.rest_1_.cos_ref, f32[512,128]{1,0:T(8,128)S(1)} %copy-done.7, ...), custom_call_target="tpu_custom_call" | custom-call | flops 1 | bytes 1 | tf_op jit(solution)/shard_map/pallas_call | solution.py:444
  100.4 6.2 %collective-permute-done.15.refs_8_.refs_3_ = bf16[256,1024]{1,0:T(8,128)(2,1)} collective-permute-done((bf16[256,1024]{1,0:T(8,128)(2,1)}, bf16[256,1024]{1,0:T(8,128)(2,1)}, u32[]{:S(2)}, u32[]{:S(2)}) %collective-permute-start.15) | collective-permute-done | bytes 524320 | tf_op jit(solution)/shard_map/ppermute | solution.py:623
  106.6 3.6 %shard_map.112 = bf16[256,4096]{1,0:T(8,128)(2,1)S(1)} custom-call(bf16[512,768]{1,0:T(8,128)(2,1)S(1)} %get-tuple-element.56.refs_0_.refs_5_, bf16[1024,768]{1,0:T(8,128)(2,1)S(1)} %shard_map.102.rest_0_.refs_6_.refs_1_, bf16[1024,768]{1,0:T(8,128)(2,1)} %collective-permute-done.5.refs_1_.refs_7_.refs_2_, bf16[512,768]{1,0:T(8,128)(2,1)S(1)} %copy-done.3, ...), custom_call_target="tpu_custom_call" | custom-call | flops 1 | bytes 1 | tf_op jit(solution)/shard_map/pallas_call | solution.py:493
  112.9 3.0 %collective-permute-done.16.b_ref = bf16[256,4096]{1,0:T(8,128)(2,1)S(1)} collective-permute-done((bf16[256,4096]{1,0:T(8,128)(2,1)S(1)}, bf16[256,4096]{1,0:T(8,128)(2,1)S(1)}, u32[]{:S(2)}, u32[]{:S(2)}) %collective-permute-start.16) | collective-permute-done | bytes 2097184 | tf_op jit(solution)/shard_map/ppermute | solution.py:634
  116.1 3.6 %shard_map.111.a_ref = bf16[256,4096]{1,0:T(8,128)(2,1)S(1)} custom-call(bf16[512,768]{1,0:T(8,128)(2,1)S(1)} %get-tuple-element.56.refs_0_.refs_5_, bf16[1024,768]{1,0:T(8,128)(2,1)S(1)} %shard_map.102.rest_0_.refs_6_.refs_1_, bf16[1024,768]{1,0:T(8,128)(2,1)} %collective-permute-done.5.refs_1_.refs_7_.refs_2_, bf16[512,768]{1,0:T(8,128)(2,1)S(1)} %copy-done.3, ...), custom_call_target="tpu_custom_call" | custom-call | flops 1 | bytes 1 | tf_op jit(solution)/shard_map/pallas_call | solution.py:493
  120.8 4.1 %collective-permute-start.18 = (bf16[64,4096]{1,0:T(8,128)(2,1)S(1)}, bf16[64,4096]{1,0:T(8,128)(2,1)S(1)}, u32[]{:S(2)}, u32[]{:S(2)}) collective-permute-start(bf16[64,4096]{1,0:T(8,128)(2,1)S(1)} %get-tuple-element.64), channel_id=1, source_target_pairs={{0,24},{4,28},{8,0},{12,4},{16,8},{20,12},{24,16},{28,20},{1,25},{... | collective-permute-start | bytes 1572872 | tf_op jit(solution)/shard_map/ppermute | solution.py:630
  124.9 5.9 %collective-permute-done.21.refs_6_.refs_7_.refs_0_ = bf16[512,768]{1,0:T(8,128)(2,1)S(1)} collective-permute-done((bf16[512,768]{1,0:T(8,128)(2,1)S(1)}, bf16[512,768]{1,0:T(8,128)(2,1)S(1)}, u32[]{:S(2)}, u32[]{:S(2)}) %collective-permute-start.21) | collective-permute-done | bytes 786464 | tf_op jit(solution)/shard_map/ppermute | solution.py:623
  135.1 4.1 %shard_map.114 = (bf16[512,4,128]{2,1,0:T(4,128)(2,1)}, f32[8,128]{1,0:T(8,128)S(1)}) custom-call(s32[8]{0:T(128)S(1)} %get-tuple-element.93.place_ref, bf16[512,512]{1,0:T(8,128)(2,1)S(1)} %get-tuple-element.55.in_ref, f32[8,128]{1,0:T(8,128)S(1)} %get-tuple-element.60.after_ref.refs_10_.refs_2_), custom_call_target="tpu_custom_call" | custom-call | flops 1 | bytes 1 | tf_op jit(solution)/shard_map/pallas_call | solution.py:255
  139.2 4.6 %shard_map.115 = (f32[1024,768]{1,0:T(8,128)S(1)}, f32[8,128]{1,0:T(8,128)S(1)}) custom-call(bf16[512,1024]{1,0:T(8,128)(2,1)S(1)} %get-tuple-element.67.refs_0_, bf16[256,1024]{1,0:T(8,128)(2,1)} %collective-permute-done.13.refs_6_.refs_1_, bf16[256,1024]{1,0:T(8,128)(2,1)S(1)} %collective-permute-done.19.refs_2_.refs_3_, ...), custom_call_target="tpu_custom_call" | custom-call | flops 1 | bytes 1 | tf_op jit(solution)/shard_map/pallas_call | solution.py:578
  143.9 4.4 %collective-permute-done.17.up_ref = bf16[64,4096]{1,0:T(8,128)(2,1)S(1)} collective-permute-done((bf16[64,4096]{1,0:T(8,128)(2,1)S(1)}, bf16[64,4096]{1,0:T(8,128)(2,1)S(1)}, u32[]{:S(2)}, u32[]{:S(2)}) %collective-permute-start.17) | collective-permute-done | bytes 524320 | tf_op jit(solution)/shard_map/ppermute | solution.py:630
  148.5 4.1 %collective-permute-start.24 = (bf16[32,4096]{1,0:T(8,128)(2,1)S(1)}, bf16[32,4096]{1,0:T(8,128)(2,1)S(1)}, u32[]{:S(2)}, u32[]{:S(2)}) collective-permute-start(bf16[32,4096]{1,0:T(8,128)(2,1)S(1)} %get-tuple-element.71), channel_id=1, source_target_pairs={{0,24},{4,28},{8,0},{12,4},{16,8},{20,12},{24,16},{28,20},{1,25},{... | collective-permute-start | bytes 786440 | tf_op jit(solution)/shard_map/ppermute | solution.py:630
  152.7 3.1 %shard_map.119 = (bf16[1024,512]{1,0:T(8,128)(2,1)S(1)}, bf16[1024,256]{1,0:T(8,128)(2,1)S(1)}) custom-call(bf16[256,1024]{1,0:T(8,128)(2,1)} %collective-permute-done.14.refs_7_.refs_0_, bf16[256,1024]{1,0:T(8,128)(2,1)S(1)} %collective-permute-done.25.refs_4_.refs_1_, bf16[256,768]{1,0:T(8,128)(2,1)S(1)} %collective-permute-done.26.refs_2_, ...), custom_call_target="tpu_custom_call" | custom-call | flops 1 | bytes 1 | tf_op jit(solution)/shard_map/pallas_call | solution.py:578
  155.7 3.8 %collective-permute-start.28 = (bf16[1024,512]{1,0:T(8,128)(2,1)S(1)}, bf16[1024,512]{1,0:T(8,128)(2,1)S(1)}, u32[]{:S(2)}, u32[]{:S(2)}) collective-permute-start(bf16[1024,512]{1,0:T(8,128)(2,1)S(1)} %get-tuple-element.77.q_ref), channel_id=1, source_target_pairs={{0,224},{32,192},{64,160},{96,128},{128,96},{160,64},{192,32},{224... | collective-permute-start | bytes 3145736 | tf_op jit(solution)/shard_map/ppermute | solution.py:758
  159.9 4.1 %collective-permute-done.23.up2_ref = bf16[32,4096]{1,0:T(8,128)(2,1)S(1)} collective-permute-done((bf16[32,4096]{1,0:T(8,128)(2,1)S(1)}, bf16[32,4096]{1,0:T(8,128)(2,1)S(1)}, u32[]{:S(2)}, u32[]{:S(2)}) %collective-permute-start.23) | collective-permute-done | bytes 262176 | tf_op jit(solution)/shard_map/ppermute | solution.py:630
  165.6 34.1 %collective-permute-done.29.kv_far_ref = bf16[1024,256]{1,0:T(8,128)(2,1)S(1)} collective-permute-done((bf16[1024,256]{1,0:T(8,128)(2,1)S(1)}, bf16[1024,256]{1,0:T(8,128)(2,1)S(1)}, u32[]{:S(2)}, u32[]{:S(2)}) %collective-permute-start.29) | collective-permute-done | bytes 524320 | tf_op jit(solution)/shard_map/ppermute | solution.py:759
  199.8 3.0 %shard_map.120 = (f32[1024,4,128]{2,1,0:T(4,128)}, f32[1024,2,128]{2,1,0:T(2,128)}) custom-call(bf16[1024,512]{1,0:T(8,128)(2,1)S(1)} %get-tuple-element.77.q_ref, bf16[1024,512]{1,0:T(8,128)(2,1)S(1)} %collective-permute-done.28.q_far_ref, bf16[1024,256]{1,0:T(8,128)(2,1)S(1)} %get-tuple-element.78.kv_ref, ...), custom_call_target="tpu_custom_call" | custom-call | flops 1 | bytes 1 | tf_op jit(solution)/shard_map/pallas_call | solution.py:606
  (114 shorter events, 47.7 us)
Async XLA Ops:
  0.6 21.0 %collective-permute-start = (bf16[64,4096]{1,0:T(8,128)(2,1)}, bf16[64,4096]{1,0:T(8,128)(2,1)}, u32[]{:S(2)}, u32[]{:S(2)}) collective-permute-start(bf16[64,4096]{1,0:T(8,128)(2,1)} %bitcast.28), channel_id=1, source_target_pairs={{0,32},{32,64},{64,96},{96,128},{128,160},{160,192},{192,224},{1,3... | collective-permute-start | bytes 1572872 | tf_op jit(solution)/shard_map/ppermute | solution.py:660
  5.0 16.7 %collective-permute-start.1 = (bf16[64,4096]{1,0:T(8,128)(2,1)}, bf16[64,4096]{1,0:T(8,128)(2,1)}, u32[]{:S(2)}, u32[]{:S(2)}) collective-permute-start(bf16[64,4096]{1,0:T(8,128)(2,1)} %bitcast.29), channel_id=1, source_target_pairs={{32,0},{64,32},{96,64},{128,96},{160,128},{192,160},{224,192},{33,... | collective-permute-start | bytes 1572872 | tf_op jit(solution)/shard_map/ppermute | solution.py:661
  11.3 35.9 %collective-permute-start.4 = (bf16[1024,768]{1,0:T(8,128)(2,1)S(1)}, bf16[1024,768]{1,0:T(8,128)(2,1)S(1)}, u32[]{:S(2)}, u32[]{:S(2)}) collective-permute-start(bf16[1024,768]{1,0:T(8,128)(2,1)S(1)} %shard_map.102.rest_0_.refs_6_.refs_1_), channel_id=1, source_target_pairs={{0,1},{1,2},{2,3},{3,0},{4,5},{5,6},{6,7},{7,4},{8,9},{9,10},{10,1... | collective-permute-start | bytes 4718600 | tf_op jit(solution)/shard_map/ppermute | solution.py:623
  11.6 37.0 %collective-permute-start.5 = (bf16[1024,768]{1,0:T(8,128)(2,1)S(1)}, bf16[1024,768]{1,0:T(8,128)(2,1)}, u32[]{:S(2)}, u32[]{:S(2)}) collective-permute-start(bf16[1024,768]{1,0:T(8,128)(2,1)S(1)} %shard_map.102.rest_0_.refs_6_.refs_1_), channel_id=1, source_target_pairs={{0,3},{1,0},{2,1},{3,2},{4,7},{5,4},{6,5},{7,6},{8,11},{9,8},{10,9... | collective-permute-start | bytes 4718600 | tf_op jit(solution)/shard_map/ppermute | solution.py:623
  24.6 29.4 %collective-permute-start.2 = (bf16[64,4096]{1,0:T(8,128)(2,1)S(1)}, bf16[64,4096]{1,0:T(8,128)(2,1)S(1)}, u32[]{:S(2)}, u32[]{:S(2)}) collective-permute-start(bf16[64,4096]{1,0:T(8,128)(2,1)S(1)} %shard_map.104.refs_0_), channel_id=1, source_target_pairs={{0,24},{4,28},{8,0},{12,4},{16,8},{20,12},{24,16},{28,20},{1,25},{... | collective-permute-start | bytes 1572872 | tf_op jit(solution)/shard_map/ppermute | solution.py:630
  31.0 27.4 %collective-permute-start.3 = (bf16[64,4096]{1,0:T(8,128)(2,1)S(1)}, bf16[64,4096]{1,0:T(8,128)(2,1)S(1)}, u32[]{:S(2)}, u32[]{:S(2)}) collective-permute-start(bf16[64,4096]{1,0:T(8,128)(2,1)S(1)} %shard_map.104.refs_0_), channel_id=1, source_target_pairs={{0,8},{4,12},{8,16},{12,20},{16,24},{20,28},{24,0},{28,4},{1,9},{5... | collective-permute-start | bytes 1572872 | tf_op jit(solution)/shard_map/ppermute | solution.py:630
  50.0 27.0 %collective-permute-start.10 = (bf16[512,768]{1,0:T(8,128)(2,1)S(1)}, bf16[512,768]{1,0:T(8,128)(2,1)S(1)}, u32[]{:S(2)}, u32[]{:S(2)}) collective-permute-start(bf16[512,768]{1,0:T(8,128)(2,1)S(1)} %get-tuple-element.51), channel_id=1, source_target_pairs={{0,3},{1,0},{2,1},{3,2},{4,7},{5,4},{6,5},{7,6},{8,11},{9,8},{10,9... | collective-permute-start | bytes 2359304 | tf_op jit(solution)/shard_map/ppermute | solution.py:623
  50.5 26.4 %collective-permute-start.9 = (bf16[512,768]{1,0:T(8,128)(2,1)S(1)}, bf16[512,768]{1,0:T(8,128)(2,1)S(1)}, u32[]{:S(2)}, u32[]{:S(2)}) collective-permute-start(bf16[512,768]{1,0:T(8,128)(2,1)S(1)} %get-tuple-element.44.refs_2_), channel_id=1, source_target_pairs={{0,1},{1,2},{2,3},{3,0},{4,5},{5,6},{6,7},{7,4},{8,9},{9,10},{10,1... | collective-permute-start | bytes 2359304 | tf_op jit(solution)/shard_map/ppermute | solution.py:623
  59.4 22.6 %collective-permute-start.11 = (bf16[128,4096]{1,0:T(8,128)(2,1)}, bf16[128,4096]{1,0:T(8,128)(2,1)}, u32[]{:S(2)}, u32[]{:S(2)}) collective-permute-start(bf16[128,4096]{1,0:T(8,128)(2,1)} %get-tuple-element.45.refs_1_), channel_id=1, source_target_pairs={{0,4},{4,0},{8,12},{12,8},{16,20},{20,16},{24,28},{28,24},{1,5},{5... | collective-permute-start | bytes 3145736 | tf_op jit(solution)/shard_map/ppermute | solution.py:634
  59.5 15.3 %collective-permute-start.7 = (bf16[32,4096]{1,0:T(8,128)(2,1)S(1)}, bf16[32,4096]{1,0:T(8,128)(2,1)S(1)}, u32[]{:S(2)}, u32[]{:S(2)}) collective-permute-start(bf16[32,4096]{1,0:T(8,128)(2,1)S(1)} %get-tuple-element.46), channel_id=1, source_target_pairs={{0,24},{4,28},{8,0},{12,4},{16,8},{20,12},{24,16},{28,20},{1,25},{... | collective-permute-start | bytes 786440 | tf_op jit(solution)/shard_map/ppermute | solution.py:630
  60.8 16.1 %collective-permute-start.8 = (bf16[32,4096]{1,0:T(8,128)(2,1)S(1)}, bf16[32,4096]{1,0:T(8,128)(2,1)S(1)}, u32[]{:S(2)}, u32[]{:S(2)}) collective-permute-start(bf16[32,4096]{1,0:T(8,128)(2,1)S(1)} %get-tuple-element.47), channel_id=1, source_target_pairs={{0,8},{4,12},{8,16},{12,20},{16,24},{20,28},{24,0},{28,4},{1,9},{5... | collective-permute-start | bytes 786440 | tf_op jit(solution)/shard_map/ppermute | solution.py:630
  79.0 21.4 %collective-permute-start.13 = (bf16[256,1024]{1,0:T(8,128)(2,1)}, bf16[256,1024]{1,0:T(8,128)(2,1)}, u32[]{:S(2)}, u32[]{:S(2)}) collective-permute-start(bf16[256,1024]{1,0:T(8,128)(2,1)} %get-tuple-element.57), channel_id=1, source_target_pairs={{0,1},{1,2},{2,3},{3,0},{4,5},{5,6},{6,7},{7,4},{8,9},{9,10},{10,1... | collective-permute-start | bytes 1572872 | tf_op jit(solution)/shard_map/ppermute | solution.py:623
  79.5 20.9 %collective-permute-start.14 = (bf16[256,1024]{1,0:T(8,128)(2,1)}, bf16[256,1024]{1,0:T(8,128)(2,1)}, u32[]{:S(2)}, u32[]{:S(2)}) collective-permute-start(bf16[256,1024]{1,0:T(8,128)(2,1)} %get-tuple-element.58), channel_id=1, source_target_pairs={{0,2},{1,3},{2,0},{3,1},{4,6},{5,7},{6,4},{7,5},{8,10},{9,11},{10,... | collective-permute-start | bytes 1572872 | tf_op jit(solution)/shard_map/ppermute | solution.py:623
  80.9 25.7 %collective-permute-start.15 = (bf16[256,1024]{1,0:T(8,128)(2,1)}, bf16[256,1024]{1,0:T(8,128)(2,1)}, u32[]{:S(2)}, u32[]{:S(2)}) collective-permute-start(bf16[256,1024]{1,0:T(8,128)(2,1)} %get-tuple-element.59), channel_id=1, source_target_pairs={{0,3},{1,0},{2,1},{3,2},{4,7},{5,4},{6,5},{7,6},{8,11},{9,8},{10,9... | collective-permute-start | bytes 1572872 | tf_op jit(solution)/shard_map/ppermute | solution.py:623
  110.9 19.9 %collective-permute-start.21 = (bf16[512,768]{1,0:T(8,128)(2,1)S(1)}, bf16[512,768]{1,0:T(8,128)(2,1)S(1)}, u32[]{:S(2)}, u32[]{:S(2)}) collective-permute-start(bf16[512,768]{1,0:T(8,128)(2,1)S(1)} %get-tuple-element.56.refs_0_.refs_5_), channel_id=1, source_target_pairs={{0,1},{1,2},{2,3},{3,0},{4,5},{5,6},{6,7},{7,4},{8,9},{9,10},{10,1... | collective-permute-start | bytes 2359304 | tf_op jit(solution)/shard_map/ppermute | solution.py:623
  111.8 20.8 %collective-permute-start.22 = (bf16[512,768]{1,0:T(8,128)(2,1)S(1)}, bf16[512,768]{1,0:T(8,128)(2,1)S(1)}, u32[]{:S(2)}, u32[]{:S(2)}) collective-permute-start(bf16[512,768]{1,0:T(8,128)(2,1)S(1)} %get-tuple-element.56.refs_0_.refs_5_), channel_id=1, source_target_pairs={{0,3},{1,0},{2,1},{3,2},{4,7},{5,4},{6,5},{7,6},{8,11},{9,8},{10,9... | collective-permute-start | bytes 2359304 | tf_op jit(solution)/shard_map/ppermute | solution.py:623
  120.7 27.6 %collective-permute-start.17 = (bf16[64,4096]{1,0:T(8,128)(2,1)S(1)}, bf16[64,4096]{1,0:T(8,128)(2,1)S(1)}, u32[]{:S(2)}, u32[]{:S(2)}) collective-permute-start(bf16[64,4096]{1,0:T(8,128)(2,1)S(1)} %get-tuple-element.63), channel_id=1, source_target_pairs={{0,8},{4,12},{8,16},{12,20},{16,24},{20,28},{24,0},{28,4},{1,9},{5... | collective-permute-start | bytes 1572872 | tf_op jit(solution)/shard_map/ppermute | solution.py:630
  120.8 27.5 %collective-permute-start.18 = (bf16[64,4096]{1,0:T(8,128)(2,1)S(1)}, bf16[64,4096]{1,0:T(8,128)(2,1)S(1)}, u32[]{:S(2)}, u32[]{:S(2)}) collective-permute-start(bf16[64,4096]{1,0:T(8,128)(2,1)S(1)} %get-tuple-element.64), channel_id=1, source_target_pairs={{0,24},{4,28},{8,0},{12,4},{16,8},{20,12},{24,16},{28,20},{1,25},{... | collective-permute-start | bytes 1572872 | tf_op jit(solution)/shard_map/ppermute | solution.py:630
  133.0 19.6 %collective-permute-start.26 = (bf16[256,768]{1,0:T(8,128)(2,1)S(1)}, bf16[256,768]{1,0:T(8,128)(2,1)S(1)}, u32[]{:S(2)}, u32[]{:S(2)}) collective-permute-start(bf16[256,768]{1,0:T(8,128)(2,1)S(1)} %get-tuple-element.73), channel_id=1, source_target_pairs={{0,1},{1,2},{2,3},{3,0},{4,5},{5,6},{6,7},{7,4},{8,9},{9,10},{10,1... | collective-permute-start | bytes 1179656 | tf_op jit(solution)/shard_map/ppermute | solution.py:623
  133.4 19.3 %collective-permute-start.27 = (bf16[256,768]{1,0:T(8,128)(2,1)S(1)}, bf16[256,768]{1,0:T(8,128)(2,1)S(1)}, u32[]{:S(2)}, u32[]{:S(2)}) collective-permute-start(bf16[256,768]{1,0:T(8,128)(2,1)S(1)} %get-tuple-element.74), channel_id=1, source_target_pairs={{0,3},{1,0},{2,1},{3,2},{4,7},{5,4},{6,5},{7,6},{8,11},{9,8},{10,9... | collective-permute-start | bytes 1179656 | tf_op jit(solution)/shard_map/ppermute | solution.py:623
  148.4 15.6 %collective-permute-start.23 = (bf16[32,4096]{1,0:T(8,128)(2,1)S(1)}, bf16[32,4096]{1,0:T(8,128)(2,1)S(1)}, u32[]{:S(2)}, u32[]{:S(2)}) collective-permute-start(bf16[32,4096]{1,0:T(8,128)(2,1)S(1)} %get-tuple-element.70), channel_id=1, source_target_pairs={{0,8},{4,12},{8,16},{12,20},{16,24},{20,28},{24,0},{28,4},{1,9},{5... | collective-permute-start | bytes 786440 | tf_op jit(solution)/shard_map/ppermute | solution.py:630
  148.5 15.5 %collective-permute-start.24 = (bf16[32,4096]{1,0:T(8,128)(2,1)S(1)}, bf16[32,4096]{1,0:T(8,128)(2,1)S(1)}, u32[]{:S(2)}, u32[]{:S(2)}) collective-permute-start(bf16[32,4096]{1,0:T(8,128)(2,1)S(1)} %get-tuple-element.71), channel_id=1, source_target_pairs={{0,24},{4,28},{8,0},{12,4},{16,8},{20,12},{24,16},{28,20},{1,25},{... | collective-permute-start | bytes 786440 | tf_op jit(solution)/shard_map/ppermute | solution.py:630
  155.7 44.1 %collective-permute-start.28 = (bf16[1024,512]{1,0:T(8,128)(2,1)S(1)}, bf16[1024,512]{1,0:T(8,128)(2,1)S(1)}, u32[]{:S(2)}, u32[]{:S(2)}) collective-permute-start(bf16[1024,512]{1,0:T(8,128)(2,1)S(1)} %get-tuple-element.77.q_ref), channel_id=1, source_target_pairs={{0,224},{32,192},{64,160},{96,128},{128,96},{160,64},{192,32},{224... | collective-permute-start | bytes 3145736 | tf_op jit(solution)/shard_map/ppermute | solution.py:758
  159.5 40.3 %collective-permute-start.29 = (bf16[1024,256]{1,0:T(8,128)(2,1)S(1)}, bf16[1024,256]{1,0:T(8,128)(2,1)S(1)}, u32[]{:S(2)}, u32[]{:S(2)}) collective-permute-start(bf16[1024,256]{1,0:T(8,128)(2,1)S(1)} %get-tuple-element.78.kv_ref), channel_id=1, source_target_pairs={{0,224},{32,192},{64,160},{96,128},{128,96},{160,64},{192,32},{224... | collective-permute-start | bytes 1572872 | tf_op jit(solution)/shard_map/ppermute | solution.py:759
  (25 other events, 164.5 us)

commit v3 on v2

--- a/solution.py
+++ b/solution.py
@@ -468,8 +468,8 @@
     )(projected, projected, cos_t, sin_t, positions[None, :], positions[:, None], out_grad)
 
 
-def partial_kernel(parts, rows, *refs):
-    weights, (out_ref, held, sems) = refs[1 : 1 + parts], refs[-3:]
+def partial_kernel(parts, *refs):
+    weights, (own_ref, other_ref, held, sems) = refs[1 : 1 + parts], refs[-4:]
     copies, at = [], 0
     for n, ref in enumerate(weights):
         size = ref.shape[0]
@@ -477,29 +477,32 @@
         at += size
     for copy in copies:
         copy.start()
-    grads = refs[0][rows[0] : rows[1], :]
+    grads = refs[0][...]
+    near = own_ref.shape[0]
     at = 0
     for copy, ref in zip(copies, weights):
         columns = slice(at, at + ref.shape[0])
         copy.wait()
-        out_ref[:, columns] = dot(grads, held[columns, :], ((1,), (1,))).astype(BF)
+        total = dot(grads, held[columns, :], ((1,), (1,))).astype(BF)
+        own_ref[:, columns] = total[:near]
+        other_ref[:, columns] = total[near:]
         at += ref.shape[0]
 
 
-def partial(grads, weights, rows, after):
-    cols = grads.shape[1]
+def partial(grads, weights, after):
+    rows, cols = grads.shape
     model = sum(w.shape[0] for w in weights)
     anywhere = pl.BlockSpec(memory_space=pl.ANY)
     return pl.pallas_call(
-        functools.partial(partial_kernel, len(weights), rows),
+        functools.partial(partial_kernel, len(weights)),
         in_specs=[VM] + [anywhere] * (len(weights) + len(after)),
-        out_specs=VM,
-        out_shape=jax.ShapeDtypeStruct((rows[1] - rows[0], model), BF),
+        out_specs=[VM, VM],
+        out_shape=[jax.ShapeDtypeStruct((rows // 2, model), BF)] * 2,
         scratch_shapes=[
             pltpu.VMEM((model, cols), BF),
             pltpu.SemaphoreType.DMA((len(weights),)),
         ],
-        compiler_params=pltpu.CompilerParams(vmem_limit_bytes=12 * 2**20),
+        compiler_params=pltpu.CompilerParams(vmem_limit_bytes=16 * 2**20),
         cost_estimate=LIGHT,
     )(grads, *weights, *after)
 
@@ -708,9 +711,9 @@
     projected, x_own = project(token_parts + other_parts, weights, d_rows)
     attended, d_own = attention(projected, heads, width, cos_t, sin_t, pos, cotangent)
 
-    other_part = other_core(partial(d_own, weights, (near, seq_len), sent))
+    own_part, other_part = partial(d_own, weights, sent)
+    other_part = other_core(other_part)
     sent_other = [other_core(x) for x in sent]
-    own_part = partial(d_own, weights, (0, near), ())
     low = [i * piece for i in range(chips)]
     mid = [i * piece + half for i in range(chips)]
     high = [(i + 1) * piece for i in range(chips)]

time: 203 us -> 201 us (level)
  Pallas kernels: 52.5 us -> 50.2 us
    ppermute x8, waiting for transfers between devices: 25.7 us -> 22.1 us  [shifted_chips(): return lax.ppermute(value, 'tensor', pairs)]
    ppermute x11, waiting for transfers between devices: 31.6 us -> 35.3 us  [shifted(): lax.ppermute(value, axis, [(i, (i + step) % count) for i in range(count)])]
    pallas_call x2 -> x1, Pallas kernels: 7.15 us -> 4.79 us  [partial(): pl.pallas_call(functools.partial(partial_kernel, len(weights)), in_specs=...]
  transfers between devices with their start and end apart: 30 -> 30, of which waited for: 13 -> 13; matrix products, arithmetic and copies ran while one was open for 3% -> 3% of each run, Pallas kernels for 23% -> 21%
where the time goes in v3:
time: 201 us; the launch traced here: 200 us
  waiting for transfers between devices  94.5 us (47%)
  Pallas kernels  50.2 us (25%)
  starting transfers between devices  40.2 us (20%)
  local copies, waits for them, and re-layouts  10.9 us (5%)
  other arithmetic  2.8 us (1%)
    ppermute x11, waiting for transfers between devices, shifted(): lax.ppermute(value, axis, [(i, (i + step) % count) for i in range(count)])  35.3 us
    ppermute x1, waiting for transfers between devices, on_device(): far_kv = lax.ppermute(own_kv, 'pipe', pairs)  34.1 us
    ppermute x8, waiting for transfers between devices, shifted_chips(): return lax.ppermute(value, 'tensor', pairs)  22.1 us
    ppermute x8, starting transfers between devices, shifted_chips(): return lax.ppermute(value, 'tensor', pairs)  17.8 us
    ppermute x11, starting transfers between devices, shifted(): lax.ppermute(value, axis, [(i, (i + step) % count) for i in range(count)])  11.6 us
    unnamed x41, local copies, waits for them, and re-layouts  9.23 us
    pallas_call x2, Pallas kernels, weight_grad(): pl.pallas_call(functools.partial(weight_grad_kernel, count, sums is None)...  7.68 us
    pallas_call x1, Pallas kernels, attention(): pl.pallas_call(attention_kernel, grid=(heads,), in_specs=[column, pl.Bloc...  7.46 us
  transfers between devices with their start and end apart: 30, of which 13 were waited for; matrix products, arithmetic and copies ran while one was open for 3% of the time, Pallas kernels for 21%

profile of v3, /device:TPU:24, one launch (start us, length us, event | category | flops | bytes accessed | tf_op | source)
XLA Modules:
  0.0 200.4 jit_solution(13048510402196568386)
XLA Ops:
  0.6 4.3 %collective-permute-start = (bf16[64,4096]{1,0:T(8,128)(2,1)}, bf16[64,4096]{1,0:T(8,128)(2,1)}, u32[]{:S(2)}, u32[]{:S(2)}) collective-permute-start(bf16[64,4096]{1,0:T(8,128)(2,1)} %bitcast.28), channel_id=1, source_target_pairs={{0,32},{32,64},{64,96},{96,128},{128,160},{160,192},{192,224},{1,3... | collective-permute-start | bytes 1572872 | tf_op jit(solution)/shard_map/ppermute | solution.py:663
  7.8 3.5 %shard_map.102.rest_0_.refs_6_.refs_1_ = bf16[1024,768]{1,0:T(8,128)(2,1)S(1)} custom-call(bf16[1024,512]{1,0:T(8,128)(2,1)S(1)} %bitcast.26, bf16[1024,256]{1,0:T(8,128)(2,1)S(1)} %bitcast.27), custom_call_target="tpu_custom_call" | custom-call | flops 1 | bytes 1 | tf_op jit(solution)/shard_map/pallas_call | solution.py:51
  21.7 2.8 %shard_map.104.refs_0_ = bf16[64,4096]{1,0:T(8,128)(2,1)S(1)} custom-call(s32[2]{0:T(128)S(1)} %pad_add_fusion.1.place_ref, bf16[64,4096]{1,0:T(8,128)(2,1)S(1)} %bitcast.30, bf16[64,4096]{1,0:T(8,128)(2,1)} %collective-permute-done.below_ref, bf16[64,4096]{1,0:T(8,128)(2,1)} %collective-permute-done.1.above_ref, ...), custom_call_target="tpu_custom_call" | custom-call | flops 1 | bytes 1 | tf_op jit(solution)/shard_map/pallas_call | solution.py:201
  24.6 6.4 %collective-permute-start.2 = (bf16[64,4096]{1,0:T(8,128)(2,1)S(1)}, bf16[64,4096]{1,0:T(8,128)(2,1)S(1)}, u32[]{:S(2)}, u32[]{:S(2)}) collective-permute-start(bf16[64,4096]{1,0:T(8,128)(2,1)S(1)} %shard_map.104.refs_0_), channel_id=1, source_target_pairs={{0,24},{4,28},{8,0},{12,4},{16,8},{20,12},{24,16},{28,20},{1,25},{... | collective-permute-start | bytes 1572872 | tf_op jit(solution)/shard_map/ppermute | solution.py:633
  31.0 16.3 %collective-permute-done.4.refs_0_.refs_10_.refs_5_ = bf16[1024,768]{1,0:T(8,128)(2,1)S(1)} collective-permute-done((bf16[1024,768]{1,0:T(8,128)(2,1)S(1)}, bf16[1024,768]{1,0:T(8,128)(2,1)S(1)}, u32[]{:S(2)}, u32[]{:S(2)}) %collective-permute-start.4) | collective-permute-done | bytes 1572896 | tf_op jit(solution)/shard_map/ppermute | solution.py:626
  50.5 2.8 %collective-permute-start.9 = (bf16[512,768]{1,0:T(8,128)(2,1)S(1)}, bf16[512,768]{1,0:T(8,128)(2,1)S(1)}, u32[]{:S(2)}, u32[]{:S(2)}) collective-permute-start(bf16[512,768]{1,0:T(8,128)(2,1)S(1)} %get-tuple-element.46.refs_2_), channel_id=1, source_target_pairs={{0,1},{1,2},{2,3},{3,0},{4,5},{5,6},{6,7},{7,4},{8,9},{9,10},{10,1... | collective-permute-start | bytes 2359304 | tf_op jit(solution)/shard_map/ppermute | solution.py:626
  54.0 4.3 %collective-permute-done.3.refs_1_ = bf16[64,4096]{1,0:T(8,128)(2,1)S(1)} collective-permute-done((bf16[64,4096]{1,0:T(8,128)(2,1)S(1)}, bf16[64,4096]{1,0:T(8,128)(2,1)S(1)}, u32[]{:S(2)}, u32[]{:S(2)}) %collective-permute-start.3) | collective-permute-done | bytes 524320 | tf_op jit(solution)/shard_map/ppermute | solution.py:633
  62.5 2.3 %shard_map.107 = (bf16[256,1024]{1,0:T(8,128)(2,1)}, bf16[256,1024]{1,0:T(8,128)(2,1)}, bf16[256,1024]{1,0:T(8,128)(2,1)}) custom-call(bf16[64,4096]{1,0:T(8,128)(2,1)S(1)} %shard_map.104.refs_0_, bf16[128,4096]{1,0:T(8,128)(2,1)} %get-tuple-element.47.refs_1_), custom_call_target="tpu_custom_call" | custom-call | flops 1 | bytes 1 | tf_op jit(solution)/shard_map/pallas_call | solution.py:90
  64.8 10.0 %collective-permute-done.7.refs_0_ = bf16[32,4096]{1,0:T(8,128)(2,1)S(1)} collective-permute-done((bf16[32,4096]{1,0:T(8,128)(2,1)S(1)}, bf16[32,4096]{1,0:T(8,128)(2,1)S(1)}, u32[]{:S(2)}, u32[]{:S(2)}) %collective-permute-start.7) | collective-permute-done | bytes 262176 | tf_op jit(solution)/shard_map/ppermute | solution.py:633
  86.4 6.5 %shard_map.109 = (bf16[512,768]{1,0:T(8,128)(2,1)S(1)}, bf16[512,1024]{1,0:T(8,128)(2,1)S(1)}) custom-call(bf16[64,4096]{1,0:T(8,128)(2,1)S(1)} %copy-done.5, bf16[128,4096]{1,0:T(8,128)(2,1)} %get-tuple-element.47.refs_1_, bf16[64,4096]{1,0:T(8,128)(2,1)} %get-tuple-element.54.refs_2_, bf16[64,4096]{1,0:T(8,128)(2,1)S(1)} %copy-done.9, ...), custom_call_target="tpu_custom_call" | custom-call | flops 1 | bytes 1 | tf_op jit(solution)/shard_map/pallas_call | solution.py:373
  92.9 7.5 %shard_map.110 = (bf16[512,512]{1,0:T(8,128)(2,1)S(1)}, bf16[512,768]{1,0:T(8,128)(2,1)S(1)}) custom-call(bf16[512,768]{1,0:T(8,128)(2,1)S(1)} %get-tuple-element.55.q_ref.kv_ref, bf16[512,768]{1,0:T(8,128)(2,1)S(1)} %get-tuple-element.55.q_ref.kv_ref, f32[512,128]{1,0:T(8,128)S(1)} %get-tuple-element.103.rest_1_.cos_ref, f32[512,128]{1,0:T(8,128)S(1)} %copy-done.7, ...), custom_call_target="tpu_custom_call" | custom-call | flops 1 | bytes 1 | tf_op jit(solution)/shard_map/pallas_call | solution.py:444
  100.4 6.2 %collective-permute-done.15.refs_8_.refs_3_ = bf16[256,1024]{1,0:T(8,128)(2,1)} collective-permute-done((bf16[256,1024]{1,0:T(8,128)(2,1)}, bf16[256,1024]{1,0:T(8,128)(2,1)}, u32[]{:S(2)}, u32[]{:S(2)}) %collective-permute-start.15) | collective-permute-done | bytes 524320 | tf_op jit(solution)/shard_map/ppermute | solution.py:626
  106.6 4.8 %shard_map.111 = (bf16[256,4096]{1,0:T(8,128)(2,1)S(1)}, bf16[256,4096]{1,0:T(8,128)(2,1)S(1)}) custom-call(bf16[512,768]{1,0:T(8,128)(2,1)S(1)} %get-tuple-element.58.refs_0_.refs_5_, bf16[1024,768]{1,0:T(8,128)(2,1)S(1)} %shard_map.102.rest_0_.refs_6_.refs_1_, bf16[1024,768]{1,0:T(8,128)(2,1)} %collective-permute-done.5.refs_1_.refs_7_.refs_2_, ...), custom_call_target="tpu_custom_call" | custom-call | flops 1 | bytes 1 | tf_op jit(solution)/shard_map/pallas_call | solution.py:496
  114.1 3.0 %collective-permute-done.16.b_ref = bf16[256,4096]{1,0:T(8,128)(2,1)S(1)} collective-permute-done((bf16[256,4096]{1,0:T(8,128)(2,1)S(1)}, bf16[256,4096]{1,0:T(8,128)(2,1)S(1)}, u32[]{:S(2)}, u32[]{:S(2)}) %collective-permute-start.16) | collective-permute-done | bytes 2097184 | tf_op jit(solution)/shard_map/ppermute | solution.py:637
  118.4 4.1 %collective-permute-start.18 = (bf16[64,4096]{1,0:T(8,128)(2,1)S(1)}, bf16[64,4096]{1,0:T(8,128)(2,1)S(1)}, u32[]{:S(2)}, u32[]{:S(2)}) collective-permute-start(bf16[64,4096]{1,0:T(8,128)(2,1)S(1)} %get-tuple-element.68), channel_id=1, source_target_pairs={{0,24},{4,28},{8,0},{12,4},{16,8},{20,12},{24,16},{28,20},{1,25},{... | collective-permute-start | bytes 1572872 | tf_op jit(solution)/shard_map/ppermute | solution.py:633
  122.5 9.5 %collective-permute-done.21.refs_6_.refs_7_.refs_0_ = bf16[512,768]{1,0:T(8,128)(2,1)S(1)} collective-permute-done((bf16[512,768]{1,0:T(8,128)(2,1)S(1)}, bf16[512,768]{1,0:T(8,128)(2,1)S(1)}, u32[]{:S(2)}, u32[]{:S(2)}) %collective-permute-start.21) | collective-permute-done | bytes 786464 | tf_op jit(solution)/shard_map/ppermute | solution.py:626
  136.4 4.1 %shard_map.113 = (bf16[512,4,128]{2,1,0:T(4,128)(2,1)}, f32[8,128]{1,0:T(8,128)S(1)}) custom-call(s32[8]{0:T(128)S(1)} %get-tuple-element.97.place_ref, bf16[512,512]{1,0:T(8,128)(2,1)S(1)} %get-tuple-element.57.in_ref, f32[8,128]{1,0:T(8,128)S(1)} %get-tuple-element.64.after_ref.refs_10_.refs_2_), custom_call_target="tpu_custom_call" | custom-call | flops 1 | bytes 1 | tf_op jit(solution)/shard_map/pallas_call | solution.py:255
  140.5 4.6 %shard_map.114 = (f32[1024,768]{1,0:T(8,128)S(1)}, f32[8,128]{1,0:T(8,128)S(1)}) custom-call(bf16[512,1024]{1,0:T(8,128)(2,1)S(1)} %get-tuple-element.71.refs_0_, bf16[256,1024]{1,0:T(8,128)(2,1)} %collective-permute-done.13.refs_6_.refs_1_, bf16[256,1024]{1,0:T(8,128)(2,1)S(1)} %collective-permute-done.19.refs_2_.refs_3_, ...), custom_call_target="tpu_custom_call" | custom-call | flops 1 | bytes 1 | tf_op jit(solution)/shard_map/pallas_call | solution.py:581
  146.1 4.1 %collective-permute-start.24 = (bf16[32,4096]{1,0:T(8,128)(2,1)S(1)}, bf16[32,4096]{1,0:T(8,128)(2,1)S(1)}, u32[]{:S(2)}, u32[]{:S(2)}) collective-permute-start(bf16[32,4096]{1,0:T(8,128)(2,1)S(1)} %get-tuple-element.75), channel_id=1, source_target_pairs={{0,24},{4,28},{8,0},{12,4},{16,8},{20,12},{24,16},{28,20},{1,25},{... | collective-permute-start | bytes 786440 | tf_op jit(solution)/shard_map/ppermute | solution.py:633
  150.3 3.1 %shard_map.118 = (bf16[1024,512]{1,0:T(8,128)(2,1)S(1)}, bf16[1024,256]{1,0:T(8,128)(2,1)S(1)}) custom-call(bf16[256,1024]{1,0:T(8,128)(2,1)} %collective-permute-done.14.refs_7_.refs_0_, bf16[256,1024]{1,0:T(8,128)(2,1)S(1)} %collective-permute-done.25.refs_4_.refs_1_, bf16[256,768]{1,0:T(8,128)(2,1)S(1)} %collective-permute-done.26.refs_2_, ...), custom_call_target="tpu_custom_call" | custom-call | flops 1 | bytes 1 | tf_op jit(solution)/shard_map/pallas_call | solution.py:581
  153.3 3.8 %collective-permute-start.28 = (bf16[1024,512]{1,0:T(8,128)(2,1)S(1)}, bf16[1024,512]{1,0:T(8,128)(2,1)S(1)}, u32[]{:S(2)}, u32[]{:S(2)}) collective-permute-start(bf16[1024,512]{1,0:T(8,128)(2,1)S(1)} %get-tuple-element.81.q_ref), channel_id=1, source_target_pairs={{0,224},{32,192},{64,160},{96,128},{128,96},{160,64},{192,32},{224... | collective-permute-start | bytes 3145736 | tf_op jit(solution)/shard_map/ppermute | solution.py:761
  157.6 4.1 %collective-permute-done.23.up2_ref = bf16[32,4096]{1,0:T(8,128)(2,1)S(1)} collective-permute-done((bf16[32,4096]{1,0:T(8,128)(2,1)S(1)}, bf16[32,4096]{1,0:T(8,128)(2,1)S(1)}, u32[]{:S(2)}, u32[]{:S(2)}) %collective-permute-start.23) | collective-permute-done | bytes 262176 | tf_op jit(solution)/shard_map/ppermute | solution.py:633
  163.3 34.1 %collective-permute-done.29.kv_far_ref = bf16[1024,256]{1,0:T(8,128)(2,1)S(1)} collective-permute-done((bf16[1024,256]{1,0:T(8,128)(2,1)S(1)}, bf16[1024,256]{1,0:T(8,128)(2,1)S(1)}, u32[]{:S(2)}, u32[]{:S(2)}) %collective-permute-start.29) | collective-permute-done | bytes 524320 | tf_op jit(solution)/shard_map/ppermute | solution.py:762
  197.4 3.0 %shard_map.119 = (f32[1024,4,128]{2,1,0:T(4,128)}, f32[1024,2,128]{2,1,0:T(2,128)}) custom-call(bf16[1024,512]{1,0:T(8,128)(2,1)S(1)} %get-tuple-element.81.q_ref, bf16[1024,512]{1,0:T(8,128)(2,1)S(1)} %collective-permute-done.28.q_far_ref, bf16[1024,256]{1,0:T(8,128)(2,1)S(1)} %get-tuple-element.82.kv_ref, ...), custom_call_target="tpu_custom_call" | custom-call | flops 1 | bytes 1 | tf_op jit(solution)/shard_map/pallas_call | solution.py:609
  (113 shorter events, 43.5 us)
Async XLA Ops:
  0.6 21.0 %collective-permute-start = (bf16[64,4096]{1,0:T(8,128)(2,1)}, bf16[64,4096]{1,0:T(8,128)(2,1)}, u32[]{:S(2)}, u32[]{:S(2)}) collective-permute-start(bf16[64,4096]{1,0:T(8,128)(2,1)} %bitcast.28), channel_id=1, source_target_pairs={{0,32},{32,64},{64,96},{96,128},{128,160},{160,192},{192,224},{1,3... | collective-permute-start | bytes 1572872 | tf_op jit(solution)/shard_map/ppermute | solution.py:663
  5.0 16.7 %collective-permute-start.1 = (bf16[64,4096]{1,0:T(8,128)(2,1)}, bf16[64,4096]{1,0:T(8,128)(2,1)}, u32[]{:S(2)}, u32[]{:S(2)}) collective-permute-start(bf16[64,4096]{1,0:T(8,128)(2,1)} %bitcast.29), channel_id=1, source_target_pairs={{32,0},{64,32},{96,64},{128,96},{160,128},{192,160},{224,192},{33,... | collective-permute-start | bytes 1572872 | tf_op jit(solution)/shard_map/ppermute | solution.py:664
  11.4 35.9 %collective-permute-start.4 = (bf16[1024,768]{1,0:T(8,128)(2,1)S(1)}, bf16[1024,768]{1,0:T(8,128)(2,1)S(1)}, u32[]{:S(2)}, u32[]{:S(2)}) collective-permute-start(bf16[1024,768]{1,0:T(8,128)(2,1)S(1)} %shard_map.102.rest_0_.refs_6_.refs_1_), channel_id=1, source_target_pairs={{0,1},{1,2},{2,3},{3,0},{4,5},{5,6},{6,7},{7,4},{8,9},{9,10},{10,1... | collective-permute-start | bytes 4718600 | tf_op jit(solution)/shard_map/ppermute | solution.py:626
  11.7 37.0 %collective-permute-start.5 = (bf16[1024,768]{1,0:T(8,128)(2,1)S(1)}, bf16[1024,768]{1,0:T(8,128)(2,1)}, u32[]{:S(2)}, u32[]{:S(2)}) collective-permute-start(bf16[1024,768]{1,0:T(8,128)(2,1)S(1)} %shard_map.102.rest_0_.refs_6_.refs_1_), channel_id=1, source_target_pairs={{0,3},{1,0},{2,1},{3,2},{4,7},{5,4},{6,5},{7,6},{8,11},{9,8},{10,9... | collective-permute-start | bytes 4718600 | tf_op jit(solution)/shard_map/ppermute | solution.py:626
  24.6 29.4 %collective-permute-start.2 = (bf16[64,4096]{1,0:T(8,128)(2,1)S(1)}, bf16[64,4096]{1,0:T(8,128)(2,1)S(1)}, u32[]{:S(2)}, u32[]{:S(2)}) collective-permute-start(bf16[64,4096]{1,0:T(8,128)(2,1)S(1)} %shard_map.104.refs_0_), channel_id=1, source_target_pairs={{0,24},{4,28},{8,0},{12,4},{16,8},{20,12},{24,16},{28,20},{1,25},{... | collective-permute-start | bytes 1572872 | tf_op jit(solution)/shard_map/ppermute | solution.py:633
  31.0 27.4 %collective-permute-start.3 = (bf16[64,4096]{1,0:T(8,128)(2,1)S(1)}, bf16[64,4096]{1,0:T(8,128)(2,1)S(1)}, u32[]{:S(2)}, u32[]{:S(2)}) collective-permute-start(bf16[64,4096]{1,0:T(8,128)(2,1)S(1)} %shard_map.104.refs_0_), channel_id=1, source_target_pairs={{0,8},{4,12},{8,16},{12,20},{16,24},{20,28},{24,0},{28,4},{1,9},{5... | collective-permute-start | bytes 1572872 | tf_op jit(solution)/shard_map/ppermute | solution.py:633
  50.0 27.0 %collective-permute-start.10 = (bf16[512,768]{1,0:T(8,128)(2,1)S(1)}, bf16[512,768]{1,0:T(8,128)(2,1)S(1)}, u32[]{:S(2)}, u32[]{:S(2)}) collective-permute-start(bf16[512,768]{1,0:T(8,128)(2,1)S(1)} %get-tuple-element.53), channel_id=1, source_target_pairs={{0,3},{1,0},{2,1},{3,2},{4,7},{5,4},{6,5},{7,6},{8,11},{9,8},{10,9... | collective-permute-start | bytes 2359304 | tf_op jit(solution)/shard_map/ppermute | solution.py:626
  50.5 26.4 %collective-permute-start.9 = (bf16[512,768]{1,0:T(8,128)(2,1)S(1)}, bf16[512,768]{1,0:T(8,128)(2,1)S(1)}, u32[]{:S(2)}, u32[]{:S(2)}) collective-permute-start(bf16[512,768]{1,0:T(8,128)(2,1)S(1)} %get-tuple-element.46.refs_2_), channel_id=1, source_target_pairs={{0,1},{1,2},{2,3},{3,0},{4,5},{5,6},{6,7},{7,4},{8,9},{9,10},{10,1... | collective-permute-start | bytes 2359304 | tf_op jit(solution)/shard_map/ppermute | solution.py:626
  59.4 22.6 %collective-permute-start.11 = (bf16[128,4096]{1,0:T(8,128)(2,1)}, bf16[128,4096]{1,0:T(8,128)(2,1)}, u32[]{:S(2)}, u32[]{:S(2)}) collective-permute-start(bf16[128,4096]{1,0:T(8,128)(2,1)} %get-tuple-element.47.refs_1_), channel_id=1, source_target_pairs={{0,4},{4,0},{8,12},{12,8},{16,20},{20,16},{24,28},{28,24},{1,5},{5... | collective-permute-start | bytes 3145736 | tf_op jit(solution)/shard_map/ppermute | solution.py:637
  59.5 15.3 %collective-permute-start.7 = (bf16[32,4096]{1,0:T(8,128)(2,1)S(1)}, bf16[32,4096]{1,0:T(8,128)(2,1)S(1)}, u32[]{:S(2)}, u32[]{:S(2)}) collective-permute-start(bf16[32,4096]{1,0:T(8,128)(2,1)S(1)} %get-tuple-element.48), channel_id=1, source_target_pairs={{0,24},{4,28},{8,0},{12,4},{16,8},{20,12},{24,16},{28,20},{1,25},{... | collective-permute-start | bytes 786440 | tf_op jit(solution)/shard_map/ppermute | solution.py:633
  60.8 16.1 %collective-permute-start.8 = (bf16[32,4096]{1,0:T(8,128)(2,1)S(1)}, bf16[32,4096]{1,0:T(8,128)(2,1)S(1)}, u32[]{:S(2)}, u32[]{:S(2)}) collective-permute-start(bf16[32,4096]{1,0:T(8,128)(2,1)S(1)} %get-tuple-element.49), channel_id=1, source_target_pairs={{0,8},{4,12},{8,16},{12,20},{16,24},{20,28},{24,0},{28,4},{1,9},{5... | collective-permute-start | bytes 786440 | tf_op jit(solution)/shard_map/ppermute | solution.py:633
  79.0 21.3 %collective-permute-start.13 = (bf16[256,1024]{1,0:T(8,128)(2,1)}, bf16[256,1024]{1,0:T(8,128)(2,1)}, u32[]{:S(2)}, u32[]{:S(2)}) collective-permute-start(bf16[256,1024]{1,0:T(8,128)(2,1)} %get-tuple-element.59), channel_id=1, source_target_pairs={{0,1},{1,2},{2,3},{3,0},{4,5},{5,6},{6,7},{7,4},{8,9},{9,10},{10,1... | collective-permute-start | bytes 1572872 | tf_op jit(solution)/shard_map/ppermute | solution.py:626
  79.5 20.9 %collective-permute-start.14 = (bf16[256,1024]{1,0:T(8,128)(2,1)}, bf16[256,1024]{1,0:T(8,128)(2,1)}, u32[]{:S(2)}, u32[]{:S(2)}) collective-permute-start(bf16[256,1024]{1,0:T(8,128)(2,1)} %get-tuple-element.60), channel_id=1, source_target_pairs={{0,2},{1,3},{2,0},{3,1},{4,6},{5,7},{6,4},{7,5},{8,10},{9,11},{10,... | collective-permute-start | bytes 1572872 | tf_op jit(solution)/shard_map/ppermute | solution.py:626
  80.9 25.7 %collective-permute-start.15 = (bf16[256,1024]{1,0:T(8,128)(2,1)}, bf16[256,1024]{1,0:T(8,128)(2,1)}, u32[]{:S(2)}, u32[]{:S(2)}) collective-permute-start(bf16[256,1024]{1,0:T(8,128)(2,1)} %get-tuple-element.61), channel_id=1, source_target_pairs={{0,3},{1,0},{2,1},{3,2},{4,7},{5,4},{6,5},{7,6},{8,11},{9,8},{10,9... | collective-permute-start | bytes 1572872 | tf_op jit(solution)/shard_map/ppermute | solution.py:626
  112.1 19.9 %collective-permute-start.21 = (bf16[512,768]{1,0:T(8,128)(2,1)S(1)}, bf16[512,768]{1,0:T(8,128)(2,1)S(1)}, u32[]{:S(2)}, u32[]{:S(2)}) collective-permute-start(bf16[512,768]{1,0:T(8,128)(2,1)S(1)} %get-tuple-element.58.refs_0_.refs_5_), channel_id=1, source_target_pairs={{0,1},{1,2},{2,3},{3,0},{4,5},{5,6},{6,7},{7,4},{8,9},{9,10},{10,1... | collective-permute-start | bytes 2359304 | tf_op jit(solution)/shard_map/ppermute | solution.py:626
  113.1 20.8 %collective-permute-start.22 = (bf16[512,768]{1,0:T(8,128)(2,1)S(1)}, bf16[512,768]{1,0:T(8,128)(2,1)S(1)}, u32[]{:S(2)}, u32[]{:S(2)}) collective-permute-start(bf16[512,768]{1,0:T(8,128)(2,1)S(1)} %get-tuple-element.58.refs_0_.refs_5_), channel_id=1, source_target_pairs={{0,3},{1,0},{2,1},{3,2},{4,7},{5,4},{6,5},{7,6},{8,11},{9,8},{10,9... | collective-permute-start | bytes 2359304 | tf_op jit(solution)/shard_map/ppermute | solution.py:626
  118.3 27.6 %collective-permute-start.17 = (bf16[64,4096]{1,0:T(8,128)(2,1)S(1)}, bf16[64,4096]{1,0:T(8,128)(2,1)S(1)}, u32[]{:S(2)}, u32[]{:S(2)}) collective-permute-start(bf16[64,4096]{1,0:T(8,128)(2,1)S(1)} %get-tuple-element.67), channel_id=1, source_target_pairs={{0,8},{4,12},{8,16},{12,20},{16,24},{20,28},{24,0},{28,4},{1,9},{5... | collective-permute-start | bytes 1572872 | tf_op jit(solution)/shard_map/ppermute | solution.py:633
  118.4 27.5 %collective-permute-start.18 = (bf16[64,4096]{1,0:T(8,128)(2,1)S(1)}, bf16[64,4096]{1,0:T(8,128)(2,1)S(1)}, u32[]{:S(2)}, u32[]{:S(2)}) collective-permute-start(bf16[64,4096]{1,0:T(8,128)(2,1)S(1)} %get-tuple-element.68), channel_id=1, source_target_pairs={{0,24},{4,28},{8,0},{12,4},{16,8},{20,12},{24,16},{28,20},{1,25},{... | collective-permute-start | bytes 1572872 | tf_op jit(solution)/shard_map/ppermute | solution.py:633
  134.3 16.0 %collective-permute-start.26 = (bf16[256,768]{1,0:T(8,128)(2,1)S(1)}, bf16[256,768]{1,0:T(8,128)(2,1)S(1)}, u32[]{:S(2)}, u32[]{:S(2)}) collective-permute-start(bf16[256,768]{1,0:T(8,128)(2,1)S(1)} %get-tuple-element.77), channel_id=1, source_target_pairs={{0,1},{1,2},{2,3},{3,0},{4,5},{5,6},{6,7},{7,4},{8,9},{9,10},{10,1... | collective-permute-start | bytes 1179656 | tf_op jit(solution)/shard_map/ppermute | solution.py:626
  134.6 15.6 %collective-permute-start.27 = (bf16[256,768]{1,0:T(8,128)(2,1)S(1)}, bf16[256,768]{1,0:T(8,128)(2,1)S(1)}, u32[]{:S(2)}, u32[]{:S(2)}) collective-permute-start(bf16[256,768]{1,0:T(8,128)(2,1)S(1)} %get-tuple-element.78), channel_id=1, source_target_pairs={{0,3},{1,0},{2,1},{3,2},{4,7},{5,4},{6,5},{7,6},{8,11},{9,8},{10,9... | collective-permute-start | bytes 1179656 | tf_op jit(solution)/shard_map/ppermute | solution.py:626
  146.1 15.6 %collective-permute-start.23 = (bf16[32,4096]{1,0:T(8,128)(2,1)S(1)}, bf16[32,4096]{1,0:T(8,128)(2,1)S(1)}, u32[]{:S(2)}, u32[]{:S(2)}) collective-permute-start(bf16[32,4096]{1,0:T(8,128)(2,1)S(1)} %get-tuple-element.74), channel_id=1, source_target_pairs={{0,8},{4,12},{8,16},{12,20},{16,24},{20,28},{24,0},{28,4},{1,9},{5... | collective-permute-start | bytes 786440 | tf_op jit(solution)/shard_map/ppermute | solution.py:633
  146.1 15.5 %collective-permute-start.24 = (bf16[32,4096]{1,0:T(8,128)(2,1)S(1)}, bf16[32,4096]{1,0:T(8,128)(2,1)S(1)}, u32[]{:S(2)}, u32[]{:S(2)}) collective-permute-start(bf16[32,4096]{1,0:T(8,128)(2,1)S(1)} %get-tuple-element.75), channel_id=1, source_target_pairs={{0,24},{4,28},{8,0},{12,4},{16,8},{20,12},{24,16},{28,20},{1,25},{... | collective-permute-start | bytes 786440 | tf_op jit(solution)/shard_map/ppermute | solution.py:633
  153.3 44.1 %collective-permute-start.28 = (bf16[1024,512]{1,0:T(8,128)(2,1)S(1)}, bf16[1024,512]{1,0:T(8,128)(2,1)S(1)}, u32[]{:S(2)}, u32[]{:S(2)}) collective-permute-start(bf16[1024,512]{1,0:T(8,128)(2,1)S(1)} %get-tuple-element.81.q_ref), channel_id=1, source_target_pairs={{0,224},{32,192},{64,160},{96,128},{128,96},{160,64},{192,32},{224... | collective-permute-start | bytes 3145736 | tf_op jit(solution)/shard_map/ppermute | solution.py:761
  157.1 40.2 %collective-permute-start.29 = (bf16[1024,256]{1,0:T(8,128)(2,1)S(1)}, bf16[1024,256]{1,0:T(8,128)(2,1)S(1)}, u32[]{:S(2)}, u32[]{:S(2)}) collective-permute-start(bf16[1024,256]{1,0:T(8,128)(2,1)S(1)} %get-tuple-element.82.kv_ref), channel_id=1, source_target_pairs={{0,224},{32,192},{64,160},{96,128},{128,96},{160,64},{192,32},{224... | collective-permute-start | bytes 1572872 | tf_op jit(solution)/shard_map/ppermute | solution.py:762
  (25 other events, 153.7 us)
